TPU v7x, 32 devices: a whole 2x2x4 slice. The times are simulated.
32 devices in a mesh: tiles: 2 (over x), disp: 8 (over z, y), rows: 2 (over core).
Axes of the slice: x: 2, y: 2, z: 4, core: 2. Of those that a mesh axis runs over, the one named last changes fastest.
Arguments:
- volume: bfloat16 [32, 192, 64, 512], P(None, 'disp', ('tiles', 'rows')), parts along dimension 2, may hold values from -1000 to 1000, as said below
- conv_weight: bfloat16 [27, 32, 32], replicated, may hold values from -0.21875 to 0.21875
- conv_bias: float32 [32], replicated, may hold values from -3 to 3
- reg_weight: bfloat16 [27, 32], replicated, may hold values from -0.875 to 0.875
Outputs:
- disparity: float32 [64, 512], P(('tiles', 'rows')), parts along dimension 0
There are 2 independent parts, one for each index of `tiles`. A program takes and returns all parts, laid end to end along the dimension named above; an argument that names none is the same for every part. Nothing has to cross between parts.
Inputs may be any that keep to these rules, and one draw needn't show every extreme that they name: `volume`: Real-valued matching features.
All inputs are finite; a program needn't handle non-finite values.
Results may differ from a plain program's by a relative error of at most 0.008.
Values may be sent and summed in bfloat16 or wider, within the bound.
No kernel may reach another device: no remote copies, remote signals or barrier semaphores. Data moves between devices by JAX's collectives and lax.ppermute only.
A program may use at most 384 MiB of HBM per device.

v0:
```python
import jax
import jax.numpy as jnp
from jax import lax
from jax.sharding import PartitionSpec as P


def padded(x, sides, width):
    for axis, dim in sides:
        count, length = (lax.axis_size(axis), x.shape[dim])
        up = [(i, (i + 1) % count) for i in range(count - 1)]
        down = [(j, i) for i, j in up]
        last = lax.slice_in_dim(x, length - width, length, axis=dim)
        initial = lax.slice_in_dim(x, 0, width, axis=dim)
        before = lax.ppermute(last, axis, up)
        after = lax.ppermute(initial, axis, down)
        x = jnp.concatenate([before, x, after], axis=dim)
    return x


def joined(value, axis, join):
    pieces = jax.tree.map(lambda part: lax.all_gather(part, axis), value)
    head = jax.tree.map(lambda part: part[0], pieces)
    tail = jax.tree.map(lambda part: part[1:], pieces)
    running, _ = lax.scan(lambda running, slab: (join(running, slab), None), head, tail)
    return running


def aggregate(extended, conv_weight):
    out_depth = extended.shape[1] - 2
    out_rows = extended.shape[2] - 2
    out_cols = extended.shape[3] - 2
    stacked = jnp.stack(
        [extended[:, :, :, col_tap : col_tap + out_cols] for col_tap in range(3)], 0
    )
    summed = None
    for depth_tap in range(3):
        for row_tap in range(3):
            start = 9 * depth_tap + 3 * row_tap
            kernel = conv_weight[start : start + 3]
            window = stacked[
                :, :, depth_tap : depth_tap + out_depth, row_tap : row_tap + out_rows, :
            ]
            term = jnp.einsum("koc,kcdhw->odhw", kernel, window, preferred_element_type=jnp.float32)
            summed = term if summed is None else summed + term
    return summed


def regress(extended, reg_weight):
    depth = extended.shape[1] - 2
    height = extended.shape[2] - 2
    width = extended.shape[3] - 2
    tapped = jnp.einsum("tc,cdhw->tdhw", reg_weight, extended, preferred_element_type=jnp.float32)
    cost = None
    for depth_tap in range(3):
        for row_tap in range(3):
            for col_tap in range(3):
                piece = tapped[
                    9 * depth_tap + 3 * row_tap + col_tap,
                    depth_tap : depth_tap + depth,
                    row_tap : row_tap + height,
                    col_tap : col_tap + width,
                ]
                cost = piece if cost is None else cost + piece
    return cost


def pad_columns(array):
    return jnp.pad(array, ((0, 0), (0, 0), (0, 0), (1, 1)))


def combine(first, second):
    peak = jnp.maximum(first[0], second[0])
    left = jnp.exp(first[0] - peak)
    right = jnp.exp(second[0] - peak)
    return (peak, first[1] * left + second[1] * right, first[2] * left + second[2] * right)


def body(volume, conv_weight, conv_bias, reg_weight):
    planes_dev = volume.shape[1]
    bias = conv_bias[:, None, None, None]
    extended = padded(volume, (("disp", 1), ("rows", 2)), 1)
    summed = aggregate(pad_columns(extended), conv_weight)
    hidden = jnp.maximum(summed + bias, 0.0).astype(jnp.bfloat16)
    hidden_ext = padded(hidden, (("disp", 1), ("rows", 2)), 1)
    cost = regress(pad_columns(hidden_ext), reg_weight)
    score = -cost
    local_peak = jnp.max(score, axis=0)
    expo = jnp.exp(score - local_peak[None])
    planes = (lax.axis_index("disp") * planes_dev + jnp.arange(planes_dev, dtype=jnp.int32)).astype(
        jnp.float32
    )
    total = jnp.sum(expo, axis=0)
    moment = jnp.sum(planes[:, None, None] * expo, axis=0)
    peak, total, moment = joined((local_peak, total, moment), "disp", combine)
    return moment / total


def solution(mesh):
    in_specs = (P(None, "disp", ("tiles", "rows"), None), P(), P(), P())
    out_specs = P(("tiles", "rows"), None)
    return jax.shard_map(body, mesh=mesh, in_specs=in_specs, out_specs=out_specs, check_vma=False)
```

profile of v0, /device:TPU:0, one launch (start us, length us, event | category | flops | bytes accessed | tf_op | source)
XLA Modules:
  0.0 613.6 jit_solution(1206597589906461967)
XLA Ops:
  1.6 4.9 collective-permute-start
  8.1 20.8 %collective-permute-done = bf16[32,1,16,512]{3,0,2,1:T(8,128)(2,1)S(1)} collective-permute-done((bf16[32,1,16,512]{3,0,2,1:T(8,128)(2,1)S(1)}, bf16[32,1,16,512]{3,0,2,1:T(8,128)(2,1)S(1)}, u32[]{:S(2)}, u32[]{:S(2)}) %collective-permute-start) | collective-permute-done | bytes 524320 | tf_op jit(solution)/shard_map/ppermute | solution.py:14
  28.9 12.9 %constant_dynamic-update-slice_fusion.1 = bf16[32,26,16,512]{3,0,2,1:T(8,128)(2,1)S(1)} fusion(bf16[32,26,16,512]{3,0,2,1:T(8,128)(2,1)S(1)} %constant_dynamic-update-slice_fusion.2, bf16[32,24,16,512]{3,2,1,0:T(8,128)(2,1)} %param.6), kind=kLoop, calls=%fused_computation.124 | loop fusion | bytes 25165824
  47.6 7.0 %fusion.83 = (bf16[1,32,26,18,512]{4,1,0,3,2:T(8,128)(2,1)}, bf16[32,26,18,512]{3,0,2,1:T(8,128)(2,1)S(1)}) fusion(bf16[32,26,1,512]{3,0,2,1:T(8,128)(2,1)S(1)} %collective-permute-done.3, bf16[32,26,16,512]{3,0,2,1:T(8,128)(2,1)S(1)} %constant_dynamic-update-slice_fusion, bf16[32,26,1,512]{3,0,2,1:T(8,128)(2,1)S(1)} %collective-permute-done.2), kind=kLoop, calls=%fused_computation.132 | loop fusion | flops 15335424 | bytes 46006272 | tf_op jit(solution)/shard_map/stack | solution.py:32
  54.6 18.4 %fusion.41 = (bf16[1,32,26,18,512]{4,1,0,3,2:T(8,128)(2,1)}, bf16[1,32,26,18,512]{4,1,0,3,2:T(8,128)(2,1)}) fusion(bf16[32,26,18,512]{3,0,2,1:T(8,128)(2,1)S(1)} %get-tuple-element.95), kind=kLoop, calls=%fused_computation.57 | loop fusion | bytes 46006272 | tf_op jit(solution)/shard_map/stack | solution.py:32
  73.0 30.5 %pad_maximum_fusion = bf16[3,32,26,18,512]{4,1,0,3,2:T(8,128)(2,1)} fusion(bf16[1,32,26,18,512]{4,1,0,3,2:T(8,128)(2,1)} %get-tuple-element.93, bf16[1,32,26,18,512]{4,1,0,3,2:T(8,128)(2,1)} %get-tuple-element.94, bf16[1,32,26,18,512]{4,1,0,3,2:T(8,128)(2,1)} %get-tuple-element.92), kind=kLoop, calls=%fused_computation.10 | loop fusion | flops 46006272 | bytes 92012544 | tf_op jit(solution)/shard_map/stack | solution.py:32
  103.5 23.2 %fusion.10 = f32[24,16,512,32,1]{2,3,4,1,0:T(8,128)} fusion(bf16[3,32,26,18,512]{4,1,0,3,2:T(8,128)(2,1)} %pad_maximum_fusion, bf16[27,32,32]{2,1,0:T(8,128)(2,1)S(1)} %copy-done.1), kind=kOutput, calls=%fused_computation.18 | convolution fusion | flops 1207959552 | bytes 62939136 | tf_op jit(solution)/shard_map/koc,kcdhw->odhw/dot_general | solution.py:43
  126.7 23.2 %fusion.12 = f32[24,16,512,32,1]{2,3,4,1,0:T(8,128)} fusion(bf16[3,32,26,18,512]{4,1,0,3,2:T(8,128)(2,1)} %pad_maximum_fusion, bf16[27,32,32]{2,1,0:T(8,128)(2,1)S(1)} %copy-done.1), kind=kOutput, calls=%fused_computation.20 | convolution fusion | flops 1207959552 | bytes 62939136 | tf_op jit(solution)/shard_map/koc,kcdhw->odhw/dot_general | solution.py:43
  149.9 23.3 %fusion.14 = f32[24,16,512,32,1]{2,3,4,1,0:T(8,128)} fusion(bf16[3,32,26,18,512]{4,1,0,3,2:T(8,128)(2,1)} %pad_maximum_fusion, bf16[27,32,32]{2,1,0:T(8,128)(2,1)S(1)} %copy-done.1), kind=kOutput, calls=%fused_computation.22 | convolution fusion | flops 1207959552 | bytes 62939136 | tf_op jit(solution)/shard_map/koc,kcdhw->odhw/dot_general | solution.py:43
  173.2 23.2 %fusion.16 = f32[24,16,512,32,1]{2,3,4,1,0:T(8,128)} fusion(bf16[3,32,26,18,512]{4,1,0,3,2:T(8,128)(2,1)} %pad_maximum_fusion, bf16[27,32,32]{2,1,0:T(8,128)(2,1)S(1)} %copy-done.1), kind=kOutput, calls=%fused_computation.24 | convolution fusion | flops 1207959552 | bytes 62939136 | tf_op jit(solution)/shard_map/koc,kcdhw->odhw/dot_general | solution.py:43
  196.4 23.2 %fusion.18 = f32[24,16,512,32,1]{2,3,4,1,0:T(8,128)} fusion(bf16[3,32,26,18,512]{4,1,0,3,2:T(8,128)(2,1)} %pad_maximum_fusion, bf16[27,32,32]{2,1,0:T(8,128)(2,1)S(1)} %copy-done.1), kind=kOutput, calls=%fused_computation.26 | convolution fusion | flops 1207959552 | bytes 62939136 | tf_op jit(solution)/shard_map/koc,kcdhw->odhw/dot_general | solution.py:43
  219.6 23.4 %fusion.20 = f32[24,16,512,32,1]{2,3,4,1,0:T(8,128)} fusion(bf16[3,32,26,18,512]{4,1,0,3,2:T(8,128)(2,1)} %pad_maximum_fusion, bf16[27,32,32]{2,1,0:T(8,128)(2,1)S(1)} %copy-done.1), kind=kOutput, calls=%fused_computation.28 | convolution fusion | flops 1207959552 | bytes 62939136 | tf_op jit(solution)/shard_map/koc,kcdhw->odhw/dot_general | solution.py:43
  243.0 23.2 %fusion.6 = f32[24,16,512,32,1]{2,3,4,1,0:T(8,128)} fusion(bf16[3,32,26,18,512]{4,1,0,3,2:T(8,128)(2,1)} %pad_maximum_fusion, bf16[27,32,32]{2,1,0:T(8,128)(2,1)S(1)} %copy-done.1), kind=kOutput, calls=%fused_computation.14 | convolution fusion | flops 1207959552 | bytes 62939136 | tf_op jit(solution)/shard_map/koc,kcdhw->odhw/dot_general | solution.py:43
  266.2 23.2 %fusion.8 = f32[24,16,512,32,1]{2,3,4,1,0:T(8,128)} fusion(bf16[3,32,26,18,512]{4,1,0,3,2:T(8,128)(2,1)} %pad_maximum_fusion, bf16[27,32,32]{2,1,0:T(8,128)(2,1)S(1)} %copy-done.1), kind=kOutput, calls=%fused_computation.16 | convolution fusion | flops 1207959552 | bytes 62939136 | tf_op jit(solution)/shard_map/koc,kcdhw->odhw/dot_general | solution.py:43
  289.3 77.6 %fusion.43 = bf16[32,24,16,512]{3,0,2,1:T(8,128)(2,1)} fusion(f32[32]{0:T(128)S(1)} %copy-done.2, f32[24,16,512,32,1]{2,3,4,1,0:T(8,128)} %fusion.6, f32[24,16,512,32,1]{2,3,4,1,0:T(8,128)} %fusion.8, f32[24,16,512,32,1]{2,3,4,1,0:T(8,128)} %fusion.10, f32[24,16,512,32,1]{2,3,4,1,0:T(8,128)} %fusion.12, f32[24,16,512,32,1]{2,3,4,1,0:T(8,128)} %fusion.14, ...), kind=kOutput, calls=%fused_computation.60 | convolution fusion | flops 1277165568 | bytes 251683328 | tf_op jit(solution)/shard_map/koc,kcdhw->odhw/dot_general | solution.py:43
  368.2 4.4 collective-permute-start.4
  373.9 21.4 %collective-permute-done.4 = bf16[32,1,16,512]{3,0,2,1:T(8,128)(2,1)S(1)} collective-permute-done((bf16[32,1,16,512]{3,0,2,1:T(8,128)(2,1)S(1)}, bf16[32,1,16,512]{3,0,2,1:T(8,128)(2,1)S(1)}, u32[]{:S(2)}, u32[]{:S(2)}) %collective-permute-start.4) | collective-permute-done | bytes 524320 | tf_op jit(solution)/shard_map/ppermute | solution.py:14
  403.5 27.8 %fusion.40 = f32[27,26,18,514]{3,0,2,1:T(8,128)} fusion(bf16[32,26,1,512]{3,0,2,1:T(8,128)(2,1)} %collective-permute-done.7, bf16[32,26,1,512]{3,0,2,1:T(8,128)(2,1)} %collective-permute-done.6, bf16[32,1,16,512]{3,0,2,1:T(8,128)(2,1)S(1)} %collective-permute-done.5, bf16[32,24,16,512]{3,0,2,1:T(8,128)(2,1)} %fusion.43, ...), kind=kOutput, calls=%fused_computation.56 | convolution fusion | flops 554231808 | bytes 41316768 | tf_op jit(solution)/shard_map/tc,cdhw->tdhw/dot_general | solution.py:52
  431.3 24.7 %fusion.87 = (f32[1,24,16,512]{3,0,2,1:T(1,128)S(1)}, f32[1,24,16,512]{3,0,2,1:T(1,128)S(1)}, f32[1,24,16,512]{3,0,2,1:T(1,128)}, f32[1,24,16,512]{3,0,2,1:T(1,1...) fusion(f32[27,26,18,514]{3,0,2,1:T(8,128)} %fusion.40), kind=kLoop, calls=%fused_computation.135 | loop fusion | bytes 12582912 | tf_op jit(solution)/shard_map/slice | solution.py:57
  456.0 53.0 %fusion.86 = (f32[1,24,16,512]{3,0,2,1:T(1,128)}, f32[1,24,16,512]{3,0,2,1:T(1,128)}, f32[1,24,16,512]{3,0,2,1:T(1,128)}, f32[1,24,16,512]{3,0,2,1:T(1,128)}, f3...) fusion(f32[27,26,18,514]{3,0,2,1:T(8,128)} %fusion.40), kind=kLoop, calls=%fused_computation.134 | loop fusion | bytes 29884416 | tf_op jit(solution)/shard_map/slice | solution.py:57
  509.3 9.9 %fusion.84 = (f32[16,512]{1,0:T(8,128)S(1)}, f32[24,16,512]{2,1,0:T(8,128)S(1)}) fusion(f32[1,24,16,512]{3,2,0,1:T(8,128)S(1)} %copy.55, f32[1,24,16,512]{3,0,2,1:T(1,128)} %get-tuple-element.91, f32[1,24,16,512]{3,0,2,1:T(1,128)} %get-tuple-element.66, f32[1,24,16,512]{3,0,2,1:T(1,128)} %get-tuple-element.67, f32[1,24,16,512]{3,0,2,1:T(1,128)} %get-tuple-element.68, ...), kind=kLoop, calls=%fused_computation.133 | loop fusion | flops 5300224 | bytes 21266432 | tf_op jit(solution)/shard_map/reduce_max | solution.py:87
  519.3 31.0 %all-gather.1 = f32[128,512]{1,0:T(8,128)S(1)} all-gather(f32[16,512]{1,0:T(8,128)S(1)} %get-tuple-element.46), channel_id=3, replica_groups=mesh['tiles'=2,'disp'=8,'rows'=2] {'disp'}, dimensions={0}, use_global_device_ids=true | all-gather | bytes 294912 | tf_op jit(solution)/shard_map/all_gather | solution.py:21
  550.3 30.8 %all-gather.2 = f32[128,512]{1,0:T(8,128)S(1)} all-gather(f32[16,512]{1,0:T(8,128)S(1)} %get-tuple-element.45), channel_id=4, replica_groups=mesh['tiles'=2,'disp'=8,'rows'=2] {'disp'}, dimensions={0}, use_global_device_ids=true | all-gather | bytes 294912 | tf_op jit(solution)/shard_map/all_gather | solution.py:21
  581.2 30.8 %all-gather = f32[128,512]{1,0:T(8,128)S(1)} all-gather(f32[16,512]{1,0:T(8,128)S(1)} %get-tuple-element.63), channel_id=2, replica_groups=mesh['tiles'=2,'disp'=8,'rows'=2] {'disp'}, dimensions={0}, use_global_device_ids=true | all-gather | bytes 294912 | tf_op jit(solution)/shard_map/all_gather | solution.py:21
  (59 shorter events, 22.0 us)
Async XLA Ops:
  0.0 403.5 %copy-start = (bf16[27,32]{1,0:T(8,128)(2,1)S(1)}, bf16[27,32]{1,0:T(8,128)(2,1)}, u32[]{:S(2)}) copy-start(bf16[27,32]{1,0:T(8,128)(2,1)} %param.9) | copy-start | bytes 5188
  1.6 27.3 %collective-permute-start = (bf16[32,1,16,512]{3,0,2,1:T(8,128)(2,1)S(1)}, bf16[32,1,16,512]{3,0,2,1:T(8,128)(2,1)S(1)}, u32[]{:S(2)}, u32[]{:S(2)}) collective-permute-start(bf16[32,1,16,512]{3,0,2,1:T(8,128)(2,1)S(1)} %copy.179), channel_id=1, source_target_pairs={{0,2},{2,4},{4,6},{6,8},{8,10},{10,12},{12,14},{1,3},{3,5},{5,7},{... | collective-permute-start | bytes 1572872 | tf_op jit(solution)/shard_map/ppermute | solution.py:14
  6.8 35.0 %collective-permute-start.1 = (bf16[32,1,16,512]{3,0,2,1:T(8,128)(2,1)S(1)}, bf16[32,1,16,512]{3,0,2,1:T(8,128)(2,1)S(1)}, u32[]{:S(2)}, u32[]{:S(2)}) collective-permute-start(bf16[32,1,16,512]{3,0,2,1:T(8,128)(2,1)S(1)} %copy.180), channel_id=1, source_target_pairs={{2,0},{4,2},{6,4},{8,6},{10,8},{12,10},{14,12},{3,1},{5,3},{7,5},{... | collective-permute-start | bytes 1572872 | tf_op jit(solution)/shard_map/ppermute | solution.py:15
  42.0 3.3 collective-permute-start.2
  43.3 4.3 collective-permute-start.3
  73.0 30.5 %copy-start.1 = (bf16[27,32,32]{2,1,0:T(8,128)(2,1)S(1)}, bf16[27,32,32]{2,1,0:T(8,128)(2,1)}, u32[]{:S(2)}) copy-start(bf16[27,32,32]{2,1,0:T(8,128)(2,1)} %param.7) | copy-start | bytes 165892
  266.2 23.2 %copy-start.2 = (f32[32]{0:T(128)S(1)}, f32[32]{0:T(128)}, u32[]{:S(2)}) copy-start(f32[32]{0:T(128)} %param.8) | copy-start | bytes 388
  368.2 27.1 %collective-permute-start.4 = (bf16[32,1,16,512]{3,0,2,1:T(8,128)(2,1)S(1)}, bf16[32,1,16,512]{3,0,2,1:T(8,128)(2,1)S(1)}, u32[]{:S(2)}, u32[]{:S(2)}) collective-permute-start(bf16[32,1,16,512]{3,0,2,1:T(8,128)(2,1)S(1)} %get-tuple-element.100), channel_id=1, source_target_pairs={{0,2},{2,4},{4,6},{6,8},{8,10},{10,12},{12,14},{1,3},{3,5},{5,7},{... | collective-permute-start | bytes 1572872 | tf_op jit(solution)/shard_map/ppermute | solution.py:14
  372.6 22.7 %collective-permute-start.5 = (bf16[32,1,16,512]{3,0,2,1:T(8,128)(2,1)S(1)}, bf16[32,1,16,512]{3,0,2,1:T(8,128)(2,1)S(1)}, u32[]{:S(2)}, u32[]{:S(2)}) collective-permute-start(bf16[32,1,16,512]{3,0,2,1:T(8,128)(2,1)S(1)} %get-tuple-element.101), channel_id=1, source_target_pairs={{2,0},{4,2},{6,4},{8,6},{10,8},{12,10},{14,12},{3,1},{5,3},{7,5},{... | collective-permute-start | bytes 1572872 | tf_op jit(solution)/shard_map/ppermute | solution.py:15
  396.9 3.5 collective-permute-start.6
  399.1 4.4 collective-permute-start.7
where the time goes:
time: 617 us; the launch traced here: 614 us
  matrix products  291 us (47%)
  local copies, waits for them, and re-layouts  113 us (18%)
  blocking collectives  92.6 us (15%)
  other arithmetic  50.4 us (8%)
  waiting for transfers between devices  47.7 us (8%)
  starting transfers between devices  18.6 us (3%)
    dot_general x9, matrix products, aggregate(): jnp.einsum('koc,kcdhw->odhw', kernel, window, preferred_element_type=jnp....  263 us
    all_gather x3, blocking collectives, joined(): pieces = jax.tree.map(lambda part: lax.all_gather(part, axis), value)  92.6 us
    slice x2, local copies, waits for them, and re-layouts, regress(): tapped[9 * depth_tap + 3 * row_tap + col_tap, depth_tap:depth_tap + depth...  77.7 us
    ppermute x4, waiting for transfers between devices, padded(): before = lax.ppermute(last, axis, up)  42.2 us
    another operation x2, other arithmetic, aggregate(): jnp.stack([extended[:, :, :, col_tap:col_tap + out_cols] for col_tap in r...  37.5 us
    dot_general x1, matrix products, regress(): jnp.einsum('tc,cdhw->tdhw', reg_weight, extended, preferred_element_type=...  27.8 us
    another operation x1, local copies, waits for them, and re-layouts, aggregate(): jnp.stack([extended[:, :, :, col_tap:col_tap + out_cols] for col_tap in r...  18.4 us
    unnamed x11, local copies, waits for them, and re-layouts  13.6 us
  transfers between devices with their start and end apart: 8, of which 5 were waited for; matrix products, arithmetic and copies ran while one was open for 2% of the time, Pallas kernels for 0%

commit v1 on v0

v1 whole, which is shorter than its diff:
```python
import functools

import jax
import jax.numpy as jnp
import numpy as np
from jax import lax
from jax.experimental import pallas as pl
from jax.experimental.pallas import tpu as pltpu
from jax.sharding import PartitionSpec as P

BF16 = jnp.bfloat16
F32 = jnp.float32
LANES = 256

PAIR = (
    (((0, 1, 0, 3), (0, 2, 0, 3), (0, 0, 0, 2)), ((0, 0), (0, 1))),
    (((3, 1, 0, 3), (3, 2, 0, 3), (3, 3, 0, 2)), ((1, 0), (1, 1))),
    (((1, 0, 0, 3), (2, 0, 0, 3), (3, 0, 0, 2)), ((0, 0), (1, 0))),
    (((1, 3, 0, 3), (2, 3, 0, 3), (0, 3, 0, 2)), ((0, 1), (1, 1))),
    (((1, 1, 0, 3), (1, 2, 0, 3), (0, 0, 2, 3), (0, 3, 2, 3)), ((0, 0), (0, 1), (1, 0), (1, 1))),
    (((2, 1, 0, 3), (2, 2, 0, 3), (3, 3, 2, 3), (3, 0, 2, 3)), ((0, 0), (0, 1), (1, 0), (1, 1))),
)
SINGLE = (
    (((0, 0, 0, 3), (1, 0, 0, 3), (2, 0, 0, 2)), ((0, 0),)),
    (((0, 3, 0, 3), (1, 3, 0, 3), (2, 3, 0, 2)), ((0, 1),)),
    (((0, 1, 0, 3), (0, 2, 0, 3), (1, 1, 0, 2)), ((0, 0), (0, 1))),
    (((1, 1, 2, 3), (1, 2, 0, 3), (2, 1, 0, 3), (2, 2, 0, 1)), ((0, 0), (0, 1))),
    (((2, 2, 1, 3), (2, 0, 2, 3), (2, 3, 2, 3)), ((0, 0), (0, 1))),
)


def tap_table(spec):
    rows = []
    for blocks, outs in spec:
        for do, ho in outs:
            row = []
            for dd, hh, c0, c1 in blocks:
                for c in range(c0, c1):
                    a, b = dd - do, hh - ho
                    row.append(9 * a + 3 * b + c if 0 <= a < 3 and 0 <= b < 3 else 27)
            rows.append(row + [27] * (8 - len(row)))
    return np.array(rows)


def packed_weights(conv_weight, spec):
    table = tap_table(spec)
    pick = jnp.asarray(table[:, :, None] == np.arange(27), BF16)
    ch = conv_weight.shape[1]
    out = jnp.einsum("mkt,toi->moki", pick, conv_weight, preferred_element_type=F32)
    return out.astype(BF16).reshape(table.shape[0] * ch, 8 * ch)


def regression_rows(reg_weight, rows, inputs, first):
    ch = reg_weight.shape[1]
    taps = reg_weight.reshape(3, 3, 3, ch)
    total = None
    for b in range(3):
        hit = np.arange(inputs)[None, :] + first == np.arange(rows)[:, None] + b - 1
        hit = jnp.asarray(hit, BF16)
        term = taps[:, b][:, :, None, None, :] * hit[None, None, :, :, None]
        total = term if total is None else total + term
    return total.reshape(9 * rows, inputs * ch)


def edge_rows(reg_weight, rows):
    ch = reg_weight.shape[1]
    taps = reg_weight.reshape(3, 3, 3, ch)
    before = jnp.pad(taps[:, 2], ((0, 0), (0, 0), (0, (rows - 1) * ch)))
    after = jnp.pad(taps[:, 0], ((0, 0), (0, 0), ((rows - 1) * ch, 0)))
    both = jnp.concatenate([before, after, jnp.zeros((3, 2, rows * ch), BF16)], axis=1)
    return both.reshape(24, rows * ch)


def shifted(x, by):
    width = x.shape[-1]
    moved = pltpu.roll(x, by % width, x.ndim - 1)
    lane = lax.broadcasted_iota(jnp.int32, x.shape[:-1] + (128,), x.ndim - 1)
    zero = jnp.zeros(x.shape[:-1] + (128,), x.dtype)
    if by == 1:
        edge = jnp.where(lane == 0, zero, moved[..., :128])
        return jnp.concatenate([edge, moved[..., 128:]], axis=-1)
    edge = jnp.where(lane == 127, zero, moved[..., width - 128 :])
    return jnp.concatenate([moved[..., : width - 128], edge], axis=-1)


def put(taps_ref, slot, row, count, at, x):
    size, width = x.shape[1], x.shape[2]
    ch = taps_ref.shape[2] // 3
    flat = x.reshape(count * size, width)
    for c, y in ((0, shifted(flat, 1)), (1, flat), (2, shifted(flat, -1))):
        where = pl.ds(c * ch + at, size)
        taps_ref[slot, pl.ds(row, count), where, :] = y.reshape(count, size, width)


def stage(taps_ref, slot, first_row, block, half):
    size = block.shape[0]
    put(taps_ref, slot, first_row, block.shape[1], half * size, jnp.swapaxes(block, 0, 1))


def patch(spec, taps_ref, slots, row, lanes, weight_ref):
    ch = taps_ref.shape[2] // 3
    sums = {}
    at = 0
    for blocks, outs in spec:
        pieces = [
            taps_ref[slots[dd], row + hh, c0 * ch : c1 * ch, lanes] for dd, hh, c0, c1 in blocks
        ]
        x = jnp.concatenate(pieces, axis=0)
        w = weight_ref[at : at + len(outs) * ch, : x.shape[0]]
        y = jnp.dot(w, x, preferred_element_type=F32)
        for k, out in enumerate(outs):
            part = y[k * ch : (k + 1) * ch]
            sums[out] = part if out not in sums else sums[out] + part
        at += len(outs) * ch
    return sums


def inner_kernel(
    vol_ref, above_ref, below_ref, weight_ref, bias_ref, reg_ref, cost_ref, edge_ref,
    taps_ref, hidden_ref, acc_ref, acc_edge_ref,
):
    s = pl.program_id(0)
    last = pl.num_programs(0) - 1
    ch, _, rows, width = vol_ref.shape
    planes = cost_ref.shape[0]
    half = ch // 2
    new = (s % 3) * 2

    def stage_part(part):
        p, h = part // 2, part % 2
        if h == 0:
            put(taps_ref, new + p, 0, 1, 0, above_ref[p][None])
            put(taps_ref, new + p, rows + 1, 1, 0, below_ref[p][None])
        block = vol_ref[h * half : (h + 1) * half, p]
        stage(taps_ref, new + p, 1, block, h)

    @pl.when(s < 2)
    def _():
        for part in range(4):
            stage_part(part)

    @pl.when(s == 2)
    def _():
        acc_ref[...] = jnp.zeros_like(acc_ref)
        acc_edge_ref[...] = jnp.zeros_like(acc_edge_ref)

    @pl.when(s >= 2)
    def _():
        old = ((s - 2) % 3) * 2
        mid = ((s - 1) % 3) * 2
        slots = (old, old + 1, mid, mid + 1)
        pairs = rows // 2
        done = 0
        for j in range(pairs):
            for n in range(0, width, LANES):
                lanes = slice(n, n + LANES)
                sums = patch(PAIR, taps_ref, slots, 2 * j, lanes, weight_ref)
                for (do, ho), y in sums.items():
                    y = jnp.maximum(y + bias_ref[...], 0.0).astype(BF16)
                    at = (2 * j + ho) * ch
                    hidden_ref[do, at : at + ch, lanes] = y
            while done * pairs < 4 * (j + 1) and done < 4:
                stage_part(done)
                done += 1
        first = 2 * (s - 2) + 1
        for do in range(2):
            for n in range(0, width, LANES):
                lanes = slice(n, n + LANES)
                y = jnp.dot(reg_ref[...], hidden_ref[do, :, lanes], preferred_element_type=F32)
                for a in range(3):
                    plane = first + do + 1 - a
                    for c in range(3):
                        at = (a * 3 + c) * rows
                        acc_ref[c, plane, :, lanes] += y[at : at + rows]
                    at = 9 * rows + a * 8
                    acc_edge_ref[plane, :, lanes] += y[at : at + 8]

    @pl.when(s == last)
    def _():
        def finish(d, carry):
            cost_ref[d] = shifted(acc_ref[0, d], 1) + acc_ref[1, d] + shifted(acc_ref[2, d], -1)
            e = acc_edge_ref[d]
            right, left = shifted(e, 1), shifted(e, -1)
            edge_ref[0, pl.ds(d, 1)] = right[0:1] + e[1:2] + left[2:3]
            edge_ref[1, pl.ds(d, 1)] = right[3:4] + e[4:5] + left[5:6]
            return carry

        lax.fori_loop(0, planes, finish, 0)


def inner(volume, above, below, weights, bias, reg):
    ch, planes, rows, width = volume.shape
    blocks = planes // 2
    block = lambda s: jnp.minimum(s, blocks - 1)
    whole = lambda x: pl.BlockSpec(x.shape, lambda s: (0,) * x.ndim)
    cost = jax.ShapeDtypeStruct((planes, rows, width), F32)
    edge = jax.ShapeDtypeStruct((2, planes, width), F32)
    work = 2 * 27 * ch * ch * planes * rows * width
    return pl.pallas_call(
        inner_kernel,
        name="inner",
        grid=(blocks + 1,),
        out_shape=(cost, edge),
        in_specs=[
            pl.BlockSpec((ch, 2, rows, width), lambda s: (0, block(s), 0, 0)),
            pl.BlockSpec((2, ch, width), lambda s: (block(s), 0, 0)),
            pl.BlockSpec((2, ch, width), lambda s: (block(s), 0, 0)),
            whole(weights), whole(bias), whole(reg),
        ],
        out_specs=(
            pl.BlockSpec(cost.shape, lambda s: (0, 0, 0)),
            pl.BlockSpec(edge.shape, lambda s: (0, 0, 0)),
        ),
        scratch_shapes=[
            pltpu.VMEM((6, rows + 2, 3 * ch, width), BF16),
            pltpu.VMEM((2, rows * ch, width), BF16),
            pltpu.VMEM((3, planes, rows, width), F32),
            pltpu.VMEM((planes, 8, width), F32),
        ],
        compiler_params=pltpu.CompilerParams(vmem_limit_bytes=40 << 20),
        cost_estimate=pl.CostEstimate(
            flops=2 * work, bytes_accessed=volume.size * 2, transcendentals=0
        ),
    )(volume, above, below, weights, bias, reg)


def outer_kernel(
    keep_ref, vol_ref, lo_ref, hi_ref, above_ref, below_ref, weight_ref, bias_ref, reg_ref, out_ref,
    taps_ref, hidden_ref,
):
    s = pl.program_id(0)
    ch, _, rows, width = vol_ref.shape
    half = ch // 2
    for p in range(3):
        put(taps_ref, p, 0, 2, 0, above_ref[p])
        put(taps_ref, p, rows + 2, 2, 0, below_ref[p])
    for h in range(2):
        part = slice(h * half, (h + 1) * half)
        far = jnp.where(s == 0, lo_ref[part], hi_ref[part])
        stage(taps_ref, 2 * s, 2, far, h)
        for p in range(2):
            stage(taps_ref, 1 + p - s, 2, vol_ref[part, p], h)
    pairs = rows // 2 + 1
    for j in range(pairs):
        for n in range(0, width, LANES):
            lanes = slice(n, n + LANES)
            sums = patch(SINGLE, taps_ref, (0, 1, 2), 2 * j, lanes, weight_ref)
            for (_, ho), y in sums.items():
                y = jnp.maximum(y + bias_ref[...], 0.0)
                r = 2 * j + ho
                if r == 0:
                    y = jnp.where(keep_ref[0] > 0, y, 0.0)
                if r == rows + 1:
                    y = jnp.where(keep_ref[1] > 0, y, 0.0)
                hidden_ref[r * ch : (r + 1) * ch, lanes] = y.astype(BF16)
    y = jnp.dot(reg_ref[...], hidden_ref[...], preferred_element_type=F32)
    for a in range(3):
        r = [y[(a * 3 + c) * rows : (a * 3 + c + 1) * rows] for c in range(3)]
        out_ref[0, 2 - a] = shifted(r[0], 1) + r[1] + shifted(r[2], -1)


def outer(keep, volume, lo, hi, above, below, weights, bias, reg):
    ch, planes, rows, width = volume.shape
    whole = lambda x: pl.BlockSpec(x.shape, lambda s: (0,) * x.ndim)
    out = jax.ShapeDtypeStruct((2, 3, rows, width), F32)
    work = 2 * 27 * ch * ch * 2 * rows * width
    return pl.pallas_call(
        outer_kernel,
        name="outer",
        grid=(2,),
        out_shape=out,
        in_specs=[
            pl.BlockSpec(memory_space=pltpu.SMEM),
            pl.BlockSpec((ch, 2, rows, width), lambda s: (0, s * (planes // 2 - 1), 0, 0)),
            whole(lo), whole(hi),
            pl.BlockSpec((3, 2, ch, width), lambda s: (s, 0, 0, 0)),
            pl.BlockSpec((3, 2, ch, width), lambda s: (s, 0, 0, 0)),
            whole(weights), whole(bias), whole(reg),
        ],
        out_specs=pl.BlockSpec((1, 3, rows, width), lambda s: (s, 0, 0, 0)),
        scratch_shapes=[
            pltpu.VMEM((3, rows + 4, 3 * ch, width), BF16),
            pltpu.VMEM(((rows + 2) * ch, width), BF16),
        ],
        compiler_params=pltpu.CompilerParams(vmem_limit_bytes=40 << 20),
        cost_estimate=pl.CostEstimate(flops=2 * work, bytes_accessed=1 << 22, transcendentals=0),
    )(keep, volume, lo, hi, above, below, weights, bias, reg)


def stats_kernel(
    first_ref, cost_ref, above_ref, below_ref, outer_ref, lo_ref, hi_ref, out_ref, score_ref
):
    planes, rows, width = cost_ref.shape
    row = lax.broadcasted_iota(jnp.int32, (rows, width), 0)
    extra = {0: outer_ref[0, 1] + lo_ref[...], 1: outer_ref[0, 2]}
    for d, x in ((planes - 2, outer_ref[1, 0]), (planes - 1, outer_ref[1, 1] + hi_ref[...])):
        extra[d] = x if d not in extra else extra[d] + x
    peak = None
    for d in range(planes):
        cost = cost_ref[d]
        cost = cost + jnp.where(row == 0, above_ref[d : d + 1], 0.0)
        cost = cost + jnp.where(row == rows - 1, below_ref[d : d + 1], 0.0)
        if d in extra:
            cost = cost + extra[d]
        score = -cost
        score_ref[d] = score
        peak = score if peak is None else jnp.maximum(peak, score)
    total = jnp.zeros((rows, width), F32)
    moment = jnp.zeros((rows, width), F32)
    first = first_ref[0].astype(F32)
    for d in range(planes):
        expo = jnp.exp(score_ref[d] - peak)
        total = total + expo
        moment = moment + (first + float(d)) * expo
    out_ref[0] = peak
    out_ref[1] = total
    out_ref[2] = moment


def stats(first, cost, above, below, outer_out, lo, hi):
    planes, rows, width = cost.shape
    vmem = pl.BlockSpec(memory_space=pltpu.VMEM)
    return pl.pallas_call(
        stats_kernel,
        name="stats",
        out_shape=jax.ShapeDtypeStruct((3, rows, width), F32),
        in_specs=[pl.BlockSpec(memory_space=pltpu.SMEM)] + [vmem] * 6,
        out_specs=vmem,
        scratch_shapes=[pltpu.VMEM((planes, rows, width), F32)],
        compiler_params=pltpu.CompilerParams(vmem_limit_bytes=40 << 20),
    )(first, cost, above, below, outer_out, lo, hi)


def combine(first, second):
    peak = jnp.maximum(first[0], second[0])
    left = jnp.exp(first[0] - peak)
    right = jnp.exp(second[0] - peak)
    return jnp.stack(
        [peak, first[1] * left + second[1] * right, first[2] * left + second[2] * right]
    )


def up(x, axis):
    count = lax.axis_size(axis)
    return lax.ppermute(x, axis, [(i, i + 1) for i in range(count - 1)])


def down(x, axis):
    count = lax.axis_size(axis)
    return lax.ppermute(x, axis, [(i + 1, i) for i in range(count - 1)])


def joined(value, axis):
    count = lax.axis_size(axis)
    if count & (count - 1):
        pieces = lax.all_gather(value, axis)
        return functools.reduce(combine, [pieces[i] for i in range(count)])
    index = lax.axis_index(axis)
    step = 1
    while step < count:
        other = lax.ppermute(value, axis, [(i, i ^ step) for i in range(count)])
        lower = (index & step) == 0
        value = combine(jnp.where(lower, value, other), jnp.where(lower, other, value))
        step *= 2
    return value


def body(volume, conv_weight, conv_bias, reg_weight):
    ch, planes, rows, width = volume.shape
    bias = jnp.broadcast_to(conv_bias[:, None], (ch, LANES))
    pair_weights = packed_weights(conv_weight, PAIR)
    single_weights = packed_weights(conv_weight, SINGLE)
    reg_inner = jnp.concatenate(
        [regression_rows(reg_weight, rows, rows, 0), edge_rows(reg_weight, rows)], axis=0
    )
    reg_outer = regression_rows(reg_weight, rows, rows + 2, -1)

    top = jnp.transpose(volume[:, :, 0, :], (1, 0, 2))
    bottom = jnp.transpose(volume[:, :, rows - 1, :], (1, 0, 2))
    above = up(bottom, "rows")
    below = down(top, "rows")

    lo = up(volume[:, planes - 1], "disp")
    hi = down(volume[:, 0], "disp")
    ends = [lo, volume[:, 0], volume[:, 1], volume[:, planes - 2], volume[:, planes - 1], hi]
    turned = lambda r: jnp.stack([jnp.swapaxes(x[:, r : r + 2], 0, 1) for x in ends])
    above2 = up(turned(rows - 2), "rows")
    below2 = down(turned(0), "rows")

    cost, edge = inner(volume, above, below, pair_weights, bias, reg_inner)
    edge_above = up(edge[1], "rows")
    edge_below = down(edge[0], "rows")

    row_index = lax.axis_index("rows")
    keep = jnp.stack([row_index > 0, row_index < lax.axis_size("rows") - 1]).astype(jnp.int32)
    ends_cost = outer(keep, volume, lo, hi, above2, below2, single_weights, bias, reg_outer)
    from_lo = up(ends_cost[1, 2], "disp")
    from_hi = down(ends_cost[0, 0], "disp")

    first = (lax.axis_index("disp") * planes).astype(jnp.int32).reshape(1)
    value = stats(first, cost, edge_above, edge_below, ends_cost, from_lo, from_hi)
    _, total, moment = joined(value, "disp")
    return moment / total


def solution(mesh):
    in_specs = (P(None, "disp", ("tiles", "rows"), None), P(), P(), P())
    out_specs = P(("tiles", "rows"), None)
    return jax.shard_map(body, mesh=mesh, in_specs=in_specs, out_specs=out_specs, check_vma=False)
```

time: 617 us -> 130 us (0.21)
  matrix products: 291 us -> 2.52 us
  blocking collectives: 92.6 us -> 0 us
  local copies, waits for them, and re-layouts: 113 us -> 28.5 us
  Pallas kernels: 0 us -> 51.4 us
  other arithmetic: 50.4 us -> 1.41 us
  waiting for transfers between devices: 47.7 us -> 13.7 us
  starting transfers between devices: 18.6 us -> 31.5 us
    dot_general x10 -> x2, matrix products: 291 us -> 2.52 us  [packed_weights(): jnp.einsum('mkt,toi->moki', pick, conv_weight, preferred_element_type=F32)]
    all_gather x3 -> x0, blocking collectives: 92.6 us -> none  [joined(): pieces = jax.tree.map(lambda part: lax.all_gather(part, axis), value)]
    slice x11 -> x2, local copies, waits for them, and re-layouts: 80.5 us -> 9.57 us  [the longest x1 6.86 us: body(): top = jnp.transpose(volume[:, :, 0, :], (1, 0, 2))]
    pallas_call x0 -> x3, Pallas kernels: none -> 51.4 us  [the longest x1 42.8 us: inner(): pl.pallas_call(inner_kernel, name='inner', grid=(blocks + 1,), out_shape=...]
    another operation x2, other arithmetic: 37.5 us -> 0.02 us  [combine(): jnp.stack([peak, first[1] * left + second[1] * right, first[2] * left + s...]
    ppermute x8 -> x13, waiting for transfers between devices: 47.7 us -> 13.7 us  [the longest x3 8.93 us: joined(): other = lax.ppermute(value, axis, [(i, i ^ step) for i in range(count)])]
    another operation x1, local copies, waits for them, and re-layouts: 18.4 us -> 0.88 us  [body(): jnp.stack([jnp.swapaxes(x[:, r:r + 2], 0, 1) for x in ends])]
    ppermute x8 -> x13, starting transfers between devices: 18.6 us -> 31.5 us  [the longest x5 17.8 us: up(): return lax.ppermute(x, axis, [(i, i + 1) for i in range(count - 1)])]
  transfers between devices with their start and end apart: 8 -> 13, of which waited for: 5 -> 5; matrix products, arithmetic and copies ran while one was open for 2% -> 21% of each run, Pallas kernels for 0% -> 39%
where the time goes in v1:
time: 130 us; the launch traced here: 129 us
  Pallas kernels  51.4 us (40%)
  starting transfers between devices  31.5 us (24%)
  local copies, waits for them, and re-layouts  28.5 us (22%)
  waiting for transfers between devices  13.7 us (11%)
  matrix products  2.52 us (2%)
  other arithmetic  1.41 us (1%)
    pallas_call x1, Pallas kernels, inner(): pl.pallas_call(inner_kernel, name='inner', grid=(blocks + 1,), out_shape=...  42.8 us
    ppermute x5, starting transfers between devices, up(): return lax.ppermute(x, axis, [(i, i + 1) for i in range(count - 1)])  17.8 us
    ppermute x3, waiting for transfers between devices, joined(): other = lax.ppermute(value, axis, [(i, i ^ step) for i in range(count)])  8.93 us
    unnamed x31, local copies, waits for them, and re-layouts  8.33 us
    pallas_call x1, Pallas kernels, outer(): pl.pallas_call(outer_kernel, name='outer', grid=(2,), out_shape=out, in_s...  8.28 us
    ppermute x3, starting transfers between devices, joined(): other = lax.ppermute(value, axis, [(i, i ^ step) for i in range(count)])  6.9 us
    slice x1, local copies, waits for them, and re-layouts, body(): top = jnp.transpose(volume[:, :, 0, :], (1, 0, 2))  6.86 us
    ppermute x5, starting transfers between devices, down(): return lax.ppermute(x, axis, [(i + 1, i) for i in range(count - 1)])  6.75 us
  transfers between devices with their start and end apart: 13, of which 5 were waited for; matrix products, arithmetic and copies ran while one was open for 21% of the time, Pallas kernels for 39%

profile of v1, /device:TPU:0, one launch (start us, length us, event | category | flops | bytes accessed | tf_op | source)
XLA Modules:
  0.0 129.4 jit_solution(2971109339886906072)
XLA Ops:
  0.0 2.7 %fusion.37 = (bf16[32,1,16,512]{3,2,1,0:T(8,128)(2,1)}, bf16[32,1,16,512]{3,2,1,0:T(8,128)(2,1)S(1)}, bf16[32,1,16,512]{3,2,1,0:T(8,128)(2,1)S(1)}, bf16[32,1,16,512]{3,2,1,0:T(8,128)(2,1)}) fusion(bf16[32,24,16,512]{3,2,1,0:T(8,128)(2,1)} %vol_ref.3), kind=kLoop, calls=%fused_computation.101 | loop fusion | bytes 4194304 | tf_op jit(solution)/shard_map/slice | solution.py:385
  3.8 5.7 %collective-permute-start.4 = (bf16[32,16,512]{2,0,1:T(8,128)(2,1)}, bf16[32,16,512]{2,0,1:T(8,128)(2,1)}, u32[]{:S(2)}, u32[]{:S(2)}) collective-permute-start(bf16[32,16,512]{2,0,1:T(8,128)(2,1)} %bitcast.174), channel_id=1, source_target_pairs={{0,2},{2,4},{4,6},{6,8},{8,10},{10,12},{12,14},{1,3},{3,5},{5,7},{... | collective-permute-start | bytes 1572872 | tf_op jit(solution)/shard_map/ppermute | solution.py:345
  11.8 6.9 %fusion.38 = (bf16[32,24,1,512]{3,2,1,0:T(2,128)(2,1)S(1)}, bf16[32,24,1,512]{3,2,1,0:T(2,128)(2,1)S(1)}) fusion(bf16[32,24,16,512]{3,2,1,0:T(8,128)(2,1)} %vol_ref.3), kind=kLoop, calls=%fused_computation.102 | loop fusion | bytes 3145728 | tf_op jit(solution)/shard_map/slice | solution.py:378
  18.7 1.7 %copy.64 = bf16[32,24,1,512]{3,0,1,2:T(8,128)(2,1)} copy(bf16[32,24,1,512]{3,2,1,0:T(2,128)(2,1)S(1)} %get-tuple-element.18) | data formatting | bytes 1572864
  20.5 1.6 %collective-permute-start = (bf16[24,32,512]{2,1,0:T(8,128)(2,1)}, bf16[24,32,512]{2,1,0:T(8,128)(2,1)S(1)}, u32[]{:S(2)}, u32[]{:S(2)}) collective-permute-start(bf16[24,32,512]{2,1,0:T(8,128)(2,1)} %bitcast.172), channel_id=1, source_target_pairs={{0,1},{2,3},{4,5},{6,7},{8,9},{10,11},{12,13},{14,15},{16,17},{18,... | collective-permute-start | bytes 2359304 | tf_op jit(solution)/shard_map/ppermute | solution.py:345
  22.1 1.7 %copy.63 = bf16[32,24,1,512]{3,0,1,2:T(8,128)(2,1)} copy(bf16[32,24,1,512]{3,2,1,0:T(2,128)(2,1)S(1)} %get-tuple-element.17) | data formatting | bytes 1572864
  23.9 1.4 %collective-permute-start.1 = (bf16[24,32,512]{2,1,0:T(8,128)(2,1)}, bf16[24,32,512]{2,1,0:T(8,128)(2,1)S(1)}, u32[]{:S(2)}, u32[]{:S(2)}) collective-permute-start(bf16[24,32,512]{2,1,0:T(8,128)(2,1)} %bitcast.171), channel_id=1, source_target_pairs={{1,0},{3,2},{5,4},{7,6},{9,8},{11,10},{13,12},{15,14},{17,16},{19,... | collective-permute-start | bytes 2359304 | tf_op jit(solution)/shard_map/ppermute | solution.py:350
  26.4 1.4 %fusion = bf16[16,32,8,32]{3,0,1,2:T(8,128)(2,1)} fusion(bf16[16,8,27,1]{2,0,3,1:T(8,128)(2,1)S(1)} %copy-done.1, bf16[27,32,32]{2,1,0:T(8,128)(2,1)S(1)} %copy-done), kind=kOutput, calls=%fused_computation.1 | convolution fusion | flops 7208960 | bytes 324352 | tf_op jit(solution)/shard_map/mkt,toi->moki/dot_general | solution.py:49
  29.0 1.4 %reshape.55.weight_ref = bf16[256,256]{1,0:T(8,128)(2,1)S(1)} reshape(bf16[8,32,8,32]{3,2,1,0:T(8,128)(2,1)} %fusion.1) | data formatting | bytes 262144 | tf_op jit(solution)/shard_map/reshape | solution.py:50
  31.0 1.9 %copy.29 = bf16[16,32,8,32]{3,2,1,0:T(8,128)(2,1)S(1)} copy(bf16[16,32,8,32]{3,0,1,2:T(8,128)(2,1)} %fusion) | data formatting | bytes 524288 | tf_op jit(solution)/shard_map/convert_element_type | solution.py:50
  33.7 1.8 %copy_bitcast_fusion.2 = (bf16[32,16,512]{2,0,1:T(8,128)(2,1)S(1)}, bf16[32,16,512]{2,0,1:T(8,128)(2,1)S(1)}) fusion(bf16[32,1,16,512]{3,2,1,0:T(8,128)(2,1)} %get-tuple-element.13, bf16[32,1,16,512]{3,2,1,0:T(8,128)(2,1)} %get-tuple-element.16), kind=kLoop, calls=%fused_computation.8 | loop fusion | bytes 2097152 | tf_op jit(solution)/shard_map/squeeze | solution.py:385
  39.1 3.1 %collective-permute-start.6 = (bf16[6,2,32,512]{3,2,1,0:T(8,128)(2,1)S(1)}, bf16[6,2,32,512]{3,2,1,0:T(8,128)(2,1)S(1)}, u32[]{:S(2)}, u32[]{:S(2)}) collective-permute-start(bf16[6,2,32,512]{3,2,1,0:T(8,128)(2,1)S(1)} %get-tuple-element.20), channel_id=1, source_target_pairs={{0,1},{2,3},{4,5},{6,7},{8,9},{10,11},{12,13},{14,15},{16,17},{18,... | collective-permute-start | bytes 1179656 | tf_op jit(solution)/shard_map/ppermute | solution.py:345
  42.2 1.5 %collective-permute-start.7 = (bf16[6,2,32,512]{3,2,1,0:T(8,128)(2,1)S(1)}, bf16[6,2,32,512]{3,2,1,0:T(8,128)(2,1)S(1)}, u32[]{:S(2)}, u32[]{:S(2)}) collective-permute-start(bf16[6,2,32,512]{3,2,1,0:T(8,128)(2,1)S(1)} %get-tuple-element.19), channel_id=1, source_target_pairs={{1,0},{3,2},{5,4},{7,6},{9,8},{11,10},{13,12},{15,14},{17,16},{19,... | collective-permute-start | bytes 1179656 | tf_op jit(solution)/shard_map/ppermute | solution.py:350
  46.5 42.8 %inner.1 = (f32[24,16,512]{2,1,0:T(8,128)S(1)}, f32[2,24,512]{2,1,0:T(8,128)S(1)}) custom-call(bf16[32,24,16,512]{3,2,1,0:T(8,128)(2,1)} %vol_ref.3, bf16[24,32,512]{2,1,0:T(8,128)(2,1)S(1)} %collective-permute-done.above_ref, bf16[24,32,512]{2,1,0:T(8,128)(2,1)S(1)} %collective-permute-done.1.below_ref, bf16[512,256]{1,0:T(8,128)(2,1)S(1)} %reshape.52.weight_ref, ...), custom_call_target="tpu_custom_call" | custom-call | flops 21743271936 | bytes 12582912 | tf_op jit(solution)/shard_map/inner/pallas_call | solution.py:199
  89.3 3.0 %collective-permute-start.2 = (f32[24,512]{1,0:T(8,128)S(1)}, f32[24,512]{1,0:T(8,128)S(1)}, u32[]{:S(2)}, u32[]{:S(2)}) collective-permute-start(f32[24,512]{1,0:T(8,128)S(1)} %get-tuple-element.40), channel_id=1, source_target_pairs={{0,1},{2,3},{4,5},{6,7},{8,9},{10,11},{12,13},{14,15},{16,17},{18,... | collective-permute-start | bytes 147464 | tf_op jit(solution)/shard_map/ppermute | solution.py:345
  93.6 8.3 %outer.1.outer_ref = f32[2,3,16,512]{3,2,1,0:T(8,128)S(1)} custom-call(s32[2]{0:T(128)S(1)} %add_convert_fusion.keep_ref, bf16[32,24,16,512]{3,2,1,0:T(8,128)(2,1)} %vol_ref.3, bf16[32,16,512]{2,1,0:T(8,128)(2,1)S(1)} %copy.37.lo_ref, bf16[32,16,512]{2,1,0:T(8,128)(2,1)S(1)} %copy.38.hi_ref, bf16[6,2,32,512]{3,2,1,0:T(8,128)(2,1)S(1)} %collective-permute-done.6.above_ref, ...), custom_call_target="tpu_custom_call" | custom-call | flops 1811939328 | bytes 4194304 | tf_op jit(solution)/shard_map/outer/pallas_call | solution.py:267
  101.9 4.4 %collective-permute-start.8 = (f32[16,512]{1,0:T(8,128)S(1)}, f32[16,512]{1,0:T(8,128)S(1)}, u32[]{:S(2)}, u32[]{:S(2)}) collective-permute-start(f32[16,512]{1,0:T(8,128)S(1)} %get-tuple-element.38), channel_id=1, source_target_pairs={{0,2},{2,4},{4,6},{6,8},{8,10},{10,12},{12,14},{1,3},{3,5},{5,7},{... | collective-permute-start | bytes 98312 | tf_op jit(solution)/shard_map/ppermute | solution.py:345
  107.9 4.4 %collective-permute-done.9.hi_ref = f32[16,512]{1,0:T(8,128)S(1)} collective-permute-done((f32[16,512]{1,0:T(8,128)S(1)}, f32[16,512]{1,0:T(8,128)S(1)}, u32[]{:S(2)}, u32[]{:S(2)}) %collective-permute-start.9) | collective-permute-done | bytes 32800 | tf_op jit(solution)/shard_map/ppermute | solution.py:350
  112.7 2.6 %collective-permute-start.10 = (f32[3,16,512]{2,1,0:T(8,128)S(1)}, f32[3,16,512]{2,1,0:T(8,128)S(1)}, u32[]{:S(2)}, u32[]{:S(2)}) collective-permute-start(f32[3,16,512]{2,1,0:T(8,128)S(1)} %stats.1), channel_id=1, source_target_pairs={{0,2},{2,0},{4,6},{6,4},{8,10},{10,8},{12,14},{14,12},{1,3},{3,1},... | collective-permute-start | bytes 294920 | tf_op jit(solution)/shard_map/ppermute | solution.py:361
  115.3 2.9 %collective-permute-done.10 = f32[3,16,512]{2,1,0:T(8,128)S(1)} collective-permute-done((f32[3,16,512]{2,1,0:T(8,128)S(1)}, f32[3,16,512]{2,1,0:T(8,128)S(1)}, u32[]{:S(2)}, u32[]{:S(2)}) %collective-permute-start.10) | collective-permute-done | bytes 98336 | tf_op jit(solution)/shard_map/ppermute | solution.py:361
  118.3 1.7 %collective-permute-start.11 = (f32[3,16,512]{2,1,0:T(8,128)S(1)}, f32[3,16,512]{2,1,0:T(8,128)S(1)}, u32[]{:S(2)}, u32[]{:S(2)}) collective-permute-start(f32[3,16,512]{2,1,0:T(8,128)S(1)} %pad_maximum_fusion.1), channel_id=1, source_target_pairs={{0,4},{2,6},{4,0},{6,2},{8,12},{10,14},{12,8},{14,10},{1,5},{3,7},... | collective-permute-start | bytes 294920 | tf_op jit(solution)/shard_map/ppermute | solution.py:361
  120.0 3.0 %collective-permute-done.11 = f32[3,16,512]{2,1,0:T(8,128)S(1)} collective-permute-done((f32[3,16,512]{2,1,0:T(8,128)S(1)}, f32[3,16,512]{2,1,0:T(8,128)S(1)}, u32[]{:S(2)}, u32[]{:S(2)}) %collective-permute-start.11) | collective-permute-done | bytes 98336 | tf_op jit(solution)/shard_map/ppermute | solution.py:361
  123.1 2.6 %collective-permute-start.12 = (f32[3,16,512]{2,1,0:T(8,128)S(1)}, f32[3,16,512]{2,1,0:T(8,128)S(1)}, u32[]{:S(2)}, u32[]{:S(2)}) collective-permute-start(f32[3,16,512]{2,1,0:T(8,128)S(1)} %pad_maximum_fusion.2), channel_id=1, source_target_pairs={{0,8},{2,10},{4,12},{6,14},{8,0},{10,2},{12,4},{14,6},{1,9},{3,11}... | collective-permute-start | bytes 294920 | tf_op jit(solution)/shard_map/ppermute | solution.py:361
  125.8 3.0 %collective-permute-done.12 = f32[3,16,512]{2,1,0:T(8,128)S(1)} collective-permute-done((f32[3,16,512]{2,1,0:T(8,128)S(1)}, f32[3,16,512]{2,1,0:T(8,128)S(1)}, u32[]{:S(2)}, u32[]{:S(2)}) %collective-permute-start.12) | collective-permute-done | bytes 98336 | tf_op jit(solution)/shard_map/ppermute | solution.py:361
  (71 shorter events, 17.4 us)
Async XLA Ops:
  3.8 31.7 %collective-permute-start.4 = (bf16[32,16,512]{2,0,1:T(8,128)(2,1)}, bf16[32,16,512]{2,0,1:T(8,128)(2,1)}, u32[]{:S(2)}, u32[]{:S(2)}) collective-permute-start(bf16[32,16,512]{2,0,1:T(8,128)(2,1)} %bitcast.174), channel_id=1, source_target_pairs={{0,2},{2,4},{4,6},{6,8},{8,10},{10,12},{12,14},{1,3},{3,5},{5,7},{... | collective-permute-start | bytes 1572872 | tf_op jit(solution)/shard_map/ppermute | solution.py:345
  10.5 27.7 %collective-permute-start.5 = (bf16[32,16,512]{2,0,1:T(8,128)(2,1)}, bf16[32,16,512]{2,0,1:T(8,128)(2,1)}, u32[]{:S(2)}, u32[]{:S(2)}) collective-permute-start(bf16[32,16,512]{2,0,1:T(8,128)(2,1)} %bitcast.173), channel_id=1, source_target_pairs={{2,0},{4,2},{6,4},{8,6},{10,8},{12,10},{14,12},{3,1},{5,3},{7,5},{... | collective-permute-start | bytes 1572872 | tf_op jit(solution)/shard_map/ppermute | solution.py:350
  18.7 6.6 %copy-start.3 = (bf16[27,32]{1,0:T(8,128)(2,1)S(1)}, bf16[27,32]{1,0:T(8,128)(2,1)}, u32[]{:S(2)}) copy-start(bf16[27,32]{1,0:T(8,128)(2,1)} %param.15) | copy-start | bytes 5188
  18.7 6.6 %copy-start = (bf16[27,32,32]{2,1,0:T(8,128)(2,1)S(1)}, bf16[27,32,32]{2,1,0:T(8,128)(2,1)}, u32[]{:S(2)}) copy-start(bf16[27,32,32]{2,1,0:T(8,128)(2,1)} %param.13) | copy-start | bytes 165892
  18.7 6.6 %copy-start.2 = (bf16[8,8,27,1]{2,1,3,0:T(8,128)(2,1)S(1)}, bf16[8,8,27,1]{2,1,3,0:T(8,128)(2,1)}, u32[]{:S(2)}) copy-start(bf16[8,8,27,1]{2,1,3,0:T(8,128)(2,1)} %constant.50) | copy-start | bytes 10372
  20.4 6.0 %copy-start.1 = (bf16[16,8,27,1]{2,0,3,1:T(8,128)(2,1)S(1)}, bf16[16,8,27,1]{2,0,3,1:T(8,128)(2,1)}, u32[]{:S(2)}) copy-start(bf16[16,8,27,1]{2,0,3,1:T(8,128)(2,1)} %constant.49) | copy-start | bytes 20740
  20.5 25.9 %collective-permute-start = (bf16[24,32,512]{2,1,0:T(8,128)(2,1)}, bf16[24,32,512]{2,1,0:T(8,128)(2,1)S(1)}, u32[]{:S(2)}, u32[]{:S(2)}) collective-permute-start(bf16[24,32,512]{2,1,0:T(8,128)(2,1)} %bitcast.172), channel_id=1, source_target_pairs={{0,1},{2,3},{4,5},{6,7},{8,9},{10,11},{12,13},{14,15},{16,17},{18,... | collective-permute-start | bytes 2359304 | tf_op jit(solution)/shard_map/ppermute | solution.py:345
  22.1 5.9 %copy-start.7 = (bf16[16,18]{1,0:T(8,128)(2,1)S(1)}, bf16[16,18]{1,0:T(8,128)(2,1)}, u32[]{:S(2)}) copy-start(bf16[16,18]{1,0:T(8,128)(2,1)} %constant.42.clone) | copy-start | bytes 1732
  22.1 5.8 %copy-start.8 = (bf16[16,18]{1,0:T(8,128)(2,1)S(1)}, bf16[16,18]{1,0:T(8,128)(2,1)}, u32[]{:S(2)}) copy-start(bf16[16,18]{1,0:T(8,128)(2,1)} %constant.43.clone) | copy-start | bytes 1732
  22.1 5.8 %copy-start.9 = (bf16[16,18]{1,0:T(8,128)(2,1)S(1)}, bf16[16,18]{1,0:T(8,128)(2,1)}, u32[]{:S(2)}) copy-start(bf16[16,18]{1,0:T(8,128)(2,1)} %constant.44.clone) | copy-start | bytes 1732
  23.8 4.4 %copy-start.4 = (bf16[16,16]{1,0:T(8,128)(2,1)S(1)}, bf16[16,16]{1,0:T(8,128)(2,1)}, u32[]{:S(2)}) copy-start(bf16[16,16]{1,0:T(8,128)(2,1)} %constant.39.clone) | copy-start | bytes 1540
  23.8 4.4 %copy-start.5 = (bf16[16,16]{1,0:T(8,128)(2,1)S(1)}, bf16[16,16]{1,0:T(8,128)(2,1)}, u32[]{:S(2)}) copy-start(bf16[16,16]{1,0:T(8,128)(2,1)} %constant.40.clone) | copy-start | bytes 1540
  23.9 4.4 %copy-start.6 = (bf16[16,16]{1,0:T(8,128)(2,1)S(1)}, bf16[16,16]{1,0:T(8,128)(2,1)}, u32[]{:S(2)}) copy-start(bf16[16,16]{1,0:T(8,128)(2,1)} %constant.41.clone) | copy-start | bytes 1540
  23.9 22.5 %collective-permute-start.1 = (bf16[24,32,512]{2,1,0:T(8,128)(2,1)}, bf16[24,32,512]{2,1,0:T(8,128)(2,1)S(1)}, u32[]{:S(2)}, u32[]{:S(2)}) collective-permute-start(bf16[24,32,512]{2,1,0:T(8,128)(2,1)} %bitcast.171), channel_id=1, source_target_pairs={{1,0},{3,2},{5,4},{7,6},{9,8},{11,10},{13,12},{15,14},{17,16},{19,... | collective-permute-start | bytes 2359304 | tf_op jit(solution)/shard_map/ppermute | solution.py:350
  35.5 10.9 %copy-start.10 = (f32[32]{0:T(128)S(1)}, f32[32]{0:T(128)}, u32[]{:S(2)}) copy-start(f32[32]{0:T(128)} %param.14) | copy-start | bytes 388
  39.1 54.5 %collective-permute-start.6 = (bf16[6,2,32,512]{3,2,1,0:T(8,128)(2,1)S(1)}, bf16[6,2,32,512]{3,2,1,0:T(8,128)(2,1)S(1)}, u32[]{:S(2)}, u32[]{:S(2)}) collective-permute-start(bf16[6,2,32,512]{3,2,1,0:T(8,128)(2,1)S(1)} %get-tuple-element.20), channel_id=1, source_target_pairs={{0,1},{2,3},{4,5},{6,7},{8,9},{10,11},{12,13},{14,15},{16,17},{18,... | collective-permute-start | bytes 1179656 | tf_op jit(solution)/shard_map/ppermute | solution.py:345
  42.2 51.4 %collective-permute-start.7 = (bf16[6,2,32,512]{3,2,1,0:T(8,128)(2,1)S(1)}, bf16[6,2,32,512]{3,2,1,0:T(8,128)(2,1)S(1)}, u32[]{:S(2)}, u32[]{:S(2)}) collective-permute-start(bf16[6,2,32,512]{3,2,1,0:T(8,128)(2,1)S(1)} %get-tuple-element.19), channel_id=1, source_target_pairs={{1,0},{3,2},{5,4},{7,6},{9,8},{11,10},{13,12},{15,14},{17,16},{19,... | collective-permute-start | bytes 1179656 | tf_op jit(solution)/shard_map/ppermute | solution.py:350
  89.3 18.4 %collective-permute-start.2 = (f32[24,512]{1,0:T(8,128)S(1)}, f32[24,512]{1,0:T(8,128)S(1)}, u32[]{:S(2)}, u32[]{:S(2)}) collective-permute-start(f32[24,512]{1,0:T(8,128)S(1)} %get-tuple-element.40), channel_id=1, source_target_pairs={{0,1},{2,3},{4,5},{6,7},{8,9},{10,11},{12,13},{14,15},{16,17},{18,... | collective-permute-start | bytes 147464 | tf_op jit(solution)/shard_map/ppermute | solution.py:345
  92.3 15.3 %collective-permute-start.3 = (f32[24,512]{1,0:T(8,128)S(1)}, f32[24,512]{1,0:T(8,128)S(1)}, u32[]{:S(2)}, u32[]{:S(2)}) collective-permute-start(f32[24,512]{1,0:T(8,128)S(1)} %get-tuple-element.39), channel_id=1, source_target_pairs={{1,0},{3,2},{5,4},{7,6},{9,8},{11,10},{13,12},{15,14},{17,16},{19,... | collective-permute-start | bytes 147464 | tf_op jit(solution)/shard_map/ppermute | solution.py:350
  101.9 6.0 %collective-permute-start.8 = (f32[16,512]{1,0:T(8,128)S(1)}, f32[16,512]{1,0:T(8,128)S(1)}, u32[]{:S(2)}, u32[]{:S(2)}) collective-permute-start(f32[16,512]{1,0:T(8,128)S(1)} %get-tuple-element.38), channel_id=1, source_target_pairs={{0,2},{2,4},{4,6},{6,8},{8,10},{10,12},{12,14},{1,3},{3,5},{5,7},{... | collective-permute-start | bytes 98312 | tf_op jit(solution)/shard_map/ppermute | solution.py:345
  106.3 6.0 %collective-permute-start.9 = (f32[16,512]{1,0:T(8,128)S(1)}, f32[16,512]{1,0:T(8,128)S(1)}, u32[]{:S(2)}, u32[]{:S(2)}) collective-permute-start(f32[16,512]{1,0:T(8,128)S(1)} %get-tuple-element.37), channel_id=1, source_target_pairs={{2,0},{4,2},{6,4},{8,6},{10,8},{12,10},{14,12},{3,1},{5,3},{7,5},{... | collective-permute-start | bytes 98312 | tf_op jit(solution)/shard_map/ppermute | solution.py:350
  112.7 5.6 %collective-permute-start.10 = (f32[3,16,512]{2,1,0:T(8,128)S(1)}, f32[3,16,512]{2,1,0:T(8,128)S(1)}, u32[]{:S(2)}, u32[]{:S(2)}) collective-permute-start(f32[3,16,512]{2,1,0:T(8,128)S(1)} %stats.1), channel_id=1, source_target_pairs={{0,2},{2,0},{4,6},{6,4},{8,10},{10,8},{12,14},{14,12},{1,3},{3,1},... | collective-permute-start | bytes 294920 | tf_op jit(solution)/shard_map/ppermute | solution.py:361
  118.3 4.7 %collective-permute-start.11 = (f32[3,16,512]{2,1,0:T(8,128)S(1)}, f32[3,16,512]{2,1,0:T(8,128)S(1)}, u32[]{:S(2)}, u32[]{:S(2)}) collective-permute-start(f32[3,16,512]{2,1,0:T(8,128)S(1)} %pad_maximum_fusion.1), channel_id=1, source_target_pairs={{0,4},{2,6},{4,0},{6,2},{8,12},{10,14},{12,8},{14,10},{1,5},{3,7},... | collective-permute-start | bytes 294920 | tf_op jit(solution)/shard_map/ppermute | solution.py:361
  123.1 5.6 %collective-permute-start.12 = (f32[3,16,512]{2,1,0:T(8,128)S(1)}, f32[3,16,512]{2,1,0:T(8,128)S(1)}, u32[]{:S(2)}, u32[]{:S(2)}) collective-permute-start(f32[3,16,512]{2,1,0:T(8,128)S(1)} %pad_maximum_fusion.2), channel_id=1, source_target_pairs={{0,8},{2,10},{4,12},{6,14},{8,0},{10,2},{12,4},{14,6},{1,9},{3,11}... | collective-permute-start | bytes 294920 | tf_op jit(solution)/shard_map/ppermute | solution.py:361

commit v2 on v1

v2 whole, which is shorter than its diff:
```python
import functools

import jax
import jax.numpy as jnp
import numpy as np
from jax import lax
from jax.experimental import pallas as pl
from jax.experimental.pallas import tpu as pltpu
from jax.sharding import PartitionSpec as P

BF16 = jnp.bfloat16
F32 = jnp.float32
LANES = 256
VMEM = pl.BlockSpec(memory_space=pltpu.VMEM)
SMEM = pl.BlockSpec(memory_space=pltpu.SMEM)
ROOM = pltpu.CompilerParams(vmem_limit_bytes=48 << 20)

SINGLE = (
    (((0, 0, 0, 3), (1, 0, 0, 3), (2, 0, 0, 2)), (0,)),
    (((0, 3, 0, 3), (1, 3, 0, 3), (2, 3, 0, 2)), (1,)),
    (((0, 1, 0, 3), (0, 2, 0, 3), (1, 1, 0, 2)), (0, 1)),
    (((1, 1, 2, 3), (1, 2, 0, 3), (2, 1, 0, 3), (2, 2, 0, 1)), (0, 1)),
    (((2, 2, 1, 3), (2, 0, 2, 3), (2, 3, 2, 3)), (0, 1)),
)


def tap(a, b, c):
    return 9 * a + 3 * b + c if 0 <= a < 3 and 0 <= b < 3 else None


def single_table():
    table = []
    for blocks, outs in SINGLE:
        for ho in outs:
            row = [tap(dd, hh - ho, c) for dd, hh, c0, c1 in blocks for c in range(c0, c1)]
            table.append(row + [None] * (8 - len(row)))
    return table


def spread_table():
    return [
        [tap(2 - do, hi - ho + 2, c) for hi in range(2) for c in range(3)]
        for ho in range(4) for do in range(3)
    ]


def halo_table(b):
    return [[tap(p - q + 2, b, c) for p in range(2) for c in range(3)] for q in range(4)]


def pack_kernel(tables, conv_ref, *out_refs):
    ch = conv_ref.shape[1]
    for table, out_ref in zip(tables, out_refs):
        for m, row in enumerate(table):
            for k, t in enumerate(row):
                block = jnp.zeros((ch, ch), BF16) if t is None else conv_ref[t]
                out_ref[m * ch : (m + 1) * ch, k * ch : (k + 1) * ch] = block


def packed(conv_weight):
    ch = conv_weight.shape[1]
    tables = [spread_table(), halo_table(0), halo_table(2), single_table()]
    outs = [jax.ShapeDtypeStruct((len(t) * ch, len(t[0]) * ch), BF16) for t in tables]
    return pl.pallas_call(
        functools.partial(pack_kernel, tables),
        name="pack",
        out_shape=outs,
        in_specs=[VMEM],
        out_specs=[VMEM] * len(outs),
        compiler_params=ROOM,
    )(conv_weight)


def regression_rows(reg_weight, rows, inputs, first):
    ch = reg_weight.shape[1]
    taps = reg_weight.reshape(3, 3, 3, ch)
    total = None
    for b in range(3):
        hit = np.arange(inputs)[None, :] + first == np.arange(rows)[:, None] + b - 1
        hit = jnp.asarray(hit, BF16)
        term = taps[:, b][:, :, None, None, :] * hit[None, None, :, :, None]
        total = term if total is None else total + term
    return total.reshape(9 * rows, inputs * ch)


def regression_edges(reg_weight, rows):
    ch = reg_weight.shape[1]
    pick = np.zeros((4, 24, 2, 2, 27))
    for q in range(4):
        for p in range(2):
            for c in range(3):
                for k, out in enumerate((-1, 0, 1, rows - 2, rows - 1, rows)):
                    for e, row in enumerate((0, rows - 1)):
                        t = tap(p - q + 2, row - out + 1, c)
                        if t is not None:
                            pick[q, c * 6 + k, p, e, t] = 1
    pick = jnp.asarray(pick.reshape(96, 4, 27), BF16)
    out = jnp.einsum("mkt,ti->mki", pick, reg_weight, preferred_element_type=F32)
    return out.astype(BF16).reshape(96, 4 * ch)


def shifted(x, by):
    width = x.shape[-1]
    moved = pltpu.roll(x, by % width, x.ndim - 1)
    lane = lax.broadcasted_iota(jnp.int32, x.shape[:-1] + (128,), x.ndim - 1)
    zero = jnp.zeros(x.shape[:-1] + (128,), x.dtype)
    if by == 1:
        edge = jnp.where(lane == 0, zero, moved[..., :128])
        return jnp.concatenate([edge, moved[..., 128:]], axis=-1)
    edge = jnp.where(lane == 127, zero, moved[..., width - 128 :])
    return jnp.concatenate([moved[..., : width - 128], edge], axis=-1)


def put(taps_ref, slot, row, at, x):
    count, size, width = x.shape
    ch = taps_ref.shape[2] // 3
    flat = x.reshape(count * size, width)
    for c, y in ((0, shifted(flat, 1)), (1, flat), (2, shifted(flat, -1))):
        taps_ref[slot, pl.ds(row, count), pl.ds(c * ch + at, size), :] = y.reshape(x.shape)


def edges_kernel(side_ref, vol_ref, near_ref, first_ref, last_ref):
    s = pl.program_id(0)
    steps = pl.num_programs(0)
    rows = vol_ref.shape[2]
    planes = 2 * steps
    top = side_ref[0] == 0
    for p in range(2):
        row = jnp.where(top, vol_ref[:, p, rows - 1, :], vol_ref[:, p, 0, :])
        near_ref[2 * s + p] = row

    @pl.when((s == 0) | (s == steps - 1))
    def _():
        for p in range(2):
            row = jnp.where(top, vol_ref[:, p, rows - 2, :], vol_ref[:, p, 1, :])
            near_ref[planes + p + jnp.where(s == 0, 0, 2)] = row

    @pl.when(s == 0)
    def _():
        first_ref[...] = jnp.swapaxes(vol_ref[:, 0], 0, 1)

    @pl.when(s == steps - 1)
    def _():
        last_ref[...] = jnp.swapaxes(vol_ref[:, 1], 0, 1)


def edges(side, volume):
    ch, planes, rows, width = volume.shape
    near = jax.ShapeDtypeStruct((planes + 4, ch, width), BF16)
    plane = jax.ShapeDtypeStruct((rows, ch, width), BF16)
    zero = lambda s: (0, 0, 0)
    return pl.pallas_call(
        edges_kernel,
        name="edges",
        grid=(planes // 2,),
        out_shape=(near, plane, plane),
        in_specs=[SMEM, pl.BlockSpec((ch, 2, rows, width), lambda s: (0, s, 0, 0))],
        out_specs=[pl.BlockSpec(x.shape, zero) for x in (near, plane, plane)],
        compiler_params=ROOM,
    )(side, volume)


def inner_kernel(
    vol_ref, weight_ref, bias_ref, reg_ref, cost_ref, pre_ref,
    taps_ref, acc_ref, hidden_ref, sums_ref,
):
    s = pl.program_id(0)
    last = pl.num_programs(0) - 1
    ch, _, rows, width = vol_ref.shape
    planes = cost_ref.shape[0]
    half = ch // 2
    new = (s % 2) * 2
    old = ((s + 1) % 2) * 2

    def stage(part):
        p, h = part // 2, part % 2
        block = vol_ref[h * half : (h + 1) * half, p]
        put(taps_ref, new + p, 0, h * half, jnp.swapaxes(block, 0, 1))

    @pl.when(s == 0)
    def _():
        for part in range(4):
            stage(part)
        sums_ref[...] = jnp.zeros_like(sums_ref)
        hidden_ref[...] = jnp.zeros_like(hidden_ref)

    @pl.when(s >= 1)
    def _():
        base = 2 * (s - 1) + 3
        tiles = rows // 2
        for p in range(2):
            slots = [(base + p + do) % 4 for do in range(3)]
            for j in range(tiles):
                ho0 = 1 if j == 0 else 0
                ho1 = 3 if j == tiles - 1 else 4
                w = weight_ref[ho0 * 3 * ch : ho1 * 3 * ch]
                for n in range(0, width, LANES):
                    lanes = slice(n, n + LANES)
                    x = taps_ref[old + p, 2 * j : 2 * j + 2, :, lanes].reshape(6 * ch, LANES)
                    y = jnp.dot(w, x, preferred_element_type=F32)
                    for ho in range(ho0, ho1):
                        for do in range(3):
                            at = ((ho - ho0) * 3 + do) * ch
                            part = y[at : at + ch]
                            fresh = do == 2 and (ho >= 2 or j == 0)
                            if not fresh:
                                part = part + acc_ref[slots[do], 2 * j + ho, :, lanes]
                            acc_ref[slots[do], 2 * j + ho, :, lanes] = part
                if j % (tiles // 2) == tiles // 2 - 1:
                    stage(2 * p + j // (tiles // 2))

    @pl.when(s >= 2)
    def _():
        first = 2 * (s - 1) - 1
        for q in range(2):
            slot = (first + q) % 4
            pre_ref[q, 0] = acc_ref[slot, 1]
            pre_ref[q, 1] = acc_ref[slot, rows]
            for r in range(1, rows - 1):
                y = jnp.maximum(acc_ref[slot, r + 1] + bias_ref[...], 0.0)
                hidden_ref[q, r * ch : (r + 1) * ch, :] = y.astype(BF16)
            for n in range(0, width, LANES):
                lanes = slice(n, n + LANES)
                y = jnp.dot(reg_ref[...], hidden_ref[q, :, lanes], preferred_element_type=F32)
                for a in range(3):
                    for c in range(3):
                        at = (a * 3 + c) * rows
                        sums_ref[c, first + q + 1 - a, :, lanes] += y[at : at + rows]

    @pl.when(s == last)
    def _():
        def finish(d, carry):
            cost_ref[d] = shifted(sums_ref[0, d], 1) + sums_ref[1, d] + shifted(sums_ref[2, d], -1)
            return carry

        lax.fori_loop(0, planes, finish, 0)


def inner(volume, weights, bias, reg):
    ch, planes, rows, width = volume.shape
    blocks = planes // 2
    whole = lambda x: pl.BlockSpec(x.shape, lambda s: (0,) * x.ndim)
    cost = jax.ShapeDtypeStruct((planes, rows, width), F32)
    pre = jax.ShapeDtypeStruct((planes - 2, 2, ch, width), F32)
    work = 2 * 27 * ch * ch * planes * rows * width
    return pl.pallas_call(
        inner_kernel,
        name="inner",
        grid=(blocks + 1,),
        out_shape=(cost, pre),
        in_specs=[
            pl.BlockSpec((ch, 2, rows, width), lambda s: (0, jnp.minimum(s, blocks - 1), 0, 0)),
            whole(weights), whole(bias), whole(reg),
        ],
        out_specs=(
            pl.BlockSpec(cost.shape, lambda s: (0, 0, 0)),
            pl.BlockSpec((2, 2, ch, width), lambda s: (jnp.maximum(s - 2, 0), 0, 0, 0)),
        ),
        scratch_shapes=[
            pltpu.VMEM((4, rows, 3 * ch, width), BF16),
            pltpu.VMEM((4, rows + 2, ch, width), F32),
            pltpu.VMEM((2, rows * ch, width), BF16),
            pltpu.VMEM((3, planes, rows, width), F32),
        ],
        compiler_params=ROOM,
        cost_estimate=pl.CostEstimate(
            flops=2 * work, bytes_accessed=volume.size * 2, transcendentals=0
        ),
    )(volume, weights, bias, reg)


def sides_kernel(
    side_ref, near_ref, pre_ref, above_ref, below_ref, bias_ref, reg_ref, out_ref, send_ref,
    taps_ref, acc_ref, hidden_ref, sums_ref,
):
    planes, _, width = out_ref.shape
    ch = near_ref.shape[1]
    side = side_ref[0]
    w = jnp.where(side == 0, below_ref[...], above_ref[...])
    e = 1 - side
    acc_ref[...] = jnp.zeros_like(acc_ref)
    sums_ref[...] = jnp.zeros_like(sums_ref)
    for d in range(planes):
        put(taps_ref, d // 2, d % 2, 0, near_ref[d][None])
    for k in range(planes // 2):
        for n in range(0, width, LANES):
            lanes = slice(n, n + LANES)
            x = taps_ref[k, :, :, lanes].reshape(6 * ch, LANES)
            y = jnp.dot(w, x, preferred_element_type=F32)
            for q in range(4):
                acc_ref[2 * k + q, :, lanes] += y[q * ch : (q + 1) * ch]
    for k in range(planes // 2 - 1):
        for p in range(2):
            d = 2 * k + 1 + p
            for row in range(2):
                y = pre_ref[d - 1, row] + jnp.where(e == row, acc_ref[d + 1], 0.0)
                y = jnp.maximum(y + bias_ref[...], 0.0).astype(BF16)
                hidden_ref[k, (2 * p + row) * ch : (2 * p + row + 1) * ch, :] = y
        for n in range(0, width, LANES):
            lanes = slice(n, n + LANES)
            y = jnp.dot(reg_ref[...], hidden_ref[k, :, lanes], preferred_element_type=F32)
            for q in range(4):
                sums_ref[2 * k + q, :, lanes] += y[q * 24 : (q + 1) * 24]
    for d in range(planes):
        y = sums_ref[d]
        right, left = shifted(y, 1), shifted(y, -1)
        total = right[0:6] + y[6:12] + left[12:18]
        out_ref[d, 0:6] = total
        send_ref[d : d + 1] = jnp.where(side == 0, total[5:6], total[0:1])


def sides(side, near, pre, above, below, bias, reg):
    ch, width = near.shape[1:]
    planes = near.shape[0] - 4
    return pl.pallas_call(
        sides_kernel,
        name="sides",
        out_shape=(
            jax.ShapeDtypeStruct((planes, 8, width), F32),
            jax.ShapeDtypeStruct((planes, width), F32),
        ),
        in_specs=[SMEM] + [VMEM] * 6,
        out_specs=(VMEM, VMEM),
        scratch_shapes=[
            pltpu.VMEM((planes // 2, 2, 3 * ch, width), BF16),
            pltpu.VMEM((planes + 2, ch, width), F32),
            pltpu.VMEM((planes // 2 - 1, 4 * ch, width), BF16),
            pltpu.VMEM((planes, 24, width), F32),
        ],
        compiler_params=ROOM,
        cost_estimate=pl.CostEstimate(flops=1 << 31, bytes_accessed=1 << 22, transcendentals=0),
    )(side, near, pre, above, below, bias, reg)


def outer_kernel(
    side_ref, vol_ref, near_ref, lo_ref, hi_ref, weight_ref, bias_ref, reg_ref, out_ref,
    taps_ref, hidden_ref,
):
    s = pl.program_id(0)
    ch, _, rows, width = vol_ref.shape
    planes = near_ref.shape[0] - 4
    half = ch // 2
    above = side_ref[0] == 1

    def stage_rows(slot, near, far):
        zero = jnp.zeros_like(near)
        put(taps_ref, slot, 0, 0, jnp.where(above, far, zero)[None])
        put(taps_ref, slot, 1, 0, jnp.where(above, near, zero)[None])
        put(taps_ref, slot, rows + 2, 0, jnp.where(above, zero, near)[None])
        put(taps_ref, slot, rows + 3, 0, jnp.where(above, zero, far)[None])

    low = s == 0
    for p in range(2):
        slot = 1 + p - s
        stage_rows(slot, near_ref[s * (planes - 2) + p], near_ref[planes + 2 * s + p])
        for h in range(2):
            block = vol_ref[h * half : (h + 1) * half, p]
            put(taps_ref, slot, 2, h * half, jnp.swapaxes(block, 0, 1))
    pick = lambda r: jnp.where(low, lo_ref[r], hi_ref[r])
    stage_rows(2 * s, pick(rows), pick(rows + 1))
    for r in range(0, rows, 4):
        put(taps_ref, 2 * s, 2 + r, 0, pick(slice(r, r + 4)))

    for j in range(rows // 2 + 1):
        for n in range(0, width, LANES):
            lanes = slice(n, n + LANES)
            sums = {}
            at = 0
            for blocks, outs in SINGLE:
                pieces = [
                    taps_ref[dd, 2 * j + hh, c0 * ch : c1 * ch, lanes] for dd, hh, c0, c1 in blocks
                ]
                x = jnp.concatenate(pieces, axis=0)
                w = weight_ref[at : at + len(outs) * ch, : x.shape[0]]
                y = jnp.dot(w, x, preferred_element_type=F32)
                for k, ho in enumerate(outs):
                    part = y[k * ch : (k + 1) * ch]
                    sums[ho] = sums[ho] + part if ho in sums else part
                at += len(outs) * ch
            for ho, y in sums.items():
                y = jnp.maximum(y + bias_ref[:, lanes], 0.0)
                r = 2 * j + ho
                if r == 0:
                    y = jnp.where(above, y, 0.0)
                if r == rows + 1:
                    y = jnp.where(above, 0.0, y)
                hidden_ref[r * ch : (r + 1) * ch, lanes] = y.astype(BF16)
    y = jnp.dot(reg_ref[...], hidden_ref[...], preferred_element_type=F32)
    for a in range(3):
        r = [y[(a * 3 + c) * rows : (a * 3 + c + 1) * rows] for c in range(3)]
        out_ref[0, 2 - a] = shifted(r[0], 1) + r[1] + shifted(r[2], -1)


def outer(side, volume, near, lo, hi, weights, bias, reg):
    ch, planes, rows, width = volume.shape
    whole = lambda x: pl.BlockSpec(x.shape, lambda s: (0,) * x.ndim)
    out = jax.ShapeDtypeStruct((2, 3, rows, width), F32)
    work = 2 * 27 * ch * ch * 2 * rows * width
    return pl.pallas_call(
        outer_kernel,
        name="outer",
        grid=(2,),
        out_shape=out,
        in_specs=[
            SMEM,
            pl.BlockSpec((ch, 2, rows, width), lambda s: (0, s * (planes // 2 - 1), 0, 0)),
            whole(near), whole(lo), whole(hi), whole(weights), whole(bias), whole(reg),
        ],
        out_specs=pl.BlockSpec((1, 3, rows, width), lambda s: (s, 0, 0, 0)),
        scratch_shapes=[
            pltpu.VMEM((3, rows + 4, 3 * ch, width), BF16),
            pltpu.VMEM(((rows + 2) * ch, width), BF16),
        ],
        compiler_params=ROOM,
        cost_estimate=pl.CostEstimate(flops=2 * work, bytes_accessed=1 << 22, transcendentals=0),
    )(side, volume, near, lo, hi, weights, bias, reg)


def stats_kernel(
    first_ref, side_ref, cost_ref, sides_ref, row_ref, outer_ref, out_ref, score_ref
):
    planes, rows, width = cost_ref.shape
    row = lax.broadcasted_iota(jnp.int32, (rows, width), 0)
    mine = jnp.where(side_ref[0] == 1, 0, rows - 1)

    def cost_of(d):
        cost = cost_ref[d]
        for k, r in ((1, 0), (2, 1), (3, rows - 2), (4, rows - 1)):
            cost = cost + jnp.where(row == r, sides_ref[d, k : k + 1], 0.0)
        return cost + jnp.where(row == mine, row_ref[d : d + 1], 0.0)

    extra = {0: outer_ref[0, 1], 1: outer_ref[0, 2]}
    for d, x in ((planes - 2, outer_ref[1, 0]), (planes - 1, outer_ref[1, 1])):
        extra[d] = x if d not in extra else extra[d] + x
    peak = None
    for d in range(1, planes - 1):
        cost = cost_of(d)
        if d in extra:
            cost = cost + extra[d]
        score = -cost
        score_ref[d] = score
        peak = score if peak is None else jnp.maximum(peak, score)
    total = jnp.zeros((rows, width), F32)
    moment = jnp.zeros((rows, width), F32)
    first = first_ref[0].astype(F32)
    for d in range(1, planes - 1):
        expo = jnp.exp(score_ref[d] - peak)
        total = total + expo
        moment = moment + (first + float(d)) * expo
    values = (
        peak, total, moment, cost_of(0) + extra[0], cost_of(planes - 1) + extra[planes - 1],
        outer_ref[0, 0], outer_ref[1, 2], jnp.zeros((rows, width), F32),
    )
    for k, value in enumerate(values):
        for t in range(rows // 8):
            for u in range(width // 128):
                tile = value[t * 8 : (t + 1) * 8, u * 128 : (u + 1) * 128]
                out_ref[t * (width // 128) + u, k] = tile


def stats(first, side, cost, sides_cost, row, outer_cost):
    planes, rows, width = cost.shape
    return pl.pallas_call(
        stats_kernel,
        name="stats",
        out_shape=jax.ShapeDtypeStruct((rows * width // 1024, 8, 8, 128), F32),
        in_specs=[SMEM, SMEM] + [VMEM] * 4,
        out_specs=VMEM,
        scratch_shapes=[pltpu.VMEM((planes, rows, width), F32)],
        compiler_params=ROOM,
    )(first, side, cost, sides_cost, row, outer_cost)


def join_kernel(planes, in_ref, out_ref):
    count = in_ref.shape[0]
    scores = []
    peak = None
    for j in range(count):
        low, high = in_ref[j, 3], in_ref[j, 4]
        if j > 0:
            low = low + in_ref[j - 1, 6]
        if j < count - 1:
            high = high + in_ref[j + 1, 5]
        scores.append((-low, -high))
        here = jnp.maximum(in_ref[j, 0], jnp.maximum(-low, -high))
        peak = here if peak is None else jnp.maximum(peak, here)
    total = jnp.zeros_like(peak)
    moment = jnp.zeros_like(peak)
    for j in range(count):
        scale = jnp.exp(in_ref[j, 0] - peak)
        low, high = (jnp.exp(score - peak) for score in scores[j])
        total = total + in_ref[j, 1] * scale + low + high
        ends = float(j * planes) * low + float((j + 1) * planes - 1) * high
        moment = moment + in_ref[j, 2] * scale + ends
    result = moment / total
    for j in range(count):
        out_ref[j] = result


def join(pieces, planes):
    count, _, rows, width = pieces.shape
    return pl.pallas_call(
        functools.partial(join_kernel, planes),
        name="join",
        out_shape=jax.ShapeDtypeStruct((count, rows, width), F32),
        in_specs=[VMEM],
        out_specs=VMEM,
        compiler_params=ROOM,
    )(pieces)


def joined(values, planes, rows, width):
    count = lax.axis_size("disp")
    tiles = values.shape[0]
    if count > tiles:
        parts = count // tiles
        values = values.reshape(tiles, 8, parts, 8 // parts, 128)
        values = jnp.swapaxes(values, 1, 2).reshape(count, 8, 8 // parts, 128)
    elif count < tiles:
        parts = tiles // count
        values = values.reshape(count, parts, 8, 8, 128)
        values = jnp.swapaxes(values, 1, 2).reshape(count, 8, parts * 8, 128)
    pieces = lax.all_to_all(values, "disp", 0, 0)
    result = lax.all_to_all(join(pieces, planes), "disp", 0, 0)
    result = result.reshape(rows // 8, width // 128, 8, 128)
    return jnp.swapaxes(result, 1, 2).reshape(rows, width)


def exchange(x, axis):
    return lax.ppermute(x, axis, [(0, 1), (1, 0)] if lax.axis_size(axis) == 2 else [])


def up(x, axis):
    count = lax.axis_size(axis)
    return lax.ppermute(x, axis, [(i, i + 1) for i in range(count - 1)])


def down(x, axis):
    count = lax.axis_size(axis)
    return lax.ppermute(x, axis, [(i + 1, i) for i in range(count - 1)])


def body(volume, conv_weight, conv_bias, reg_weight):
    ch, planes, rows, width = volume.shape
    bias = jnp.broadcast_to(conv_bias[:, None], (ch, width))
    side = lax.axis_index("rows").astype(jnp.int32).reshape(1)
    first = (lax.axis_index("disp") * planes).astype(jnp.int32).reshape(1)

    near, first_plane, last_plane = edges(side, volume)
    near = exchange(near, "rows")
    spread, above, below, single = packed(conv_weight)
    reg_inner = regression_rows(reg_weight, rows, rows, 0)
    reg_outer = regression_rows(reg_weight, rows, rows + 2, -1)
    reg_edges = regression_edges(reg_weight, rows)
    ends = [near[planes - 1], near[planes + 3]], [near[0], near[planes]]
    lo = up(jnp.concatenate([last_plane, jnp.stack(ends[0])]), "disp")
    hi = down(jnp.concatenate([first_plane, jnp.stack(ends[1])]), "disp")

    cost, pre = inner(volume, spread, bias, reg_inner)
    sides_cost, send = sides(side, near, pre, above, below, bias, reg_edges)
    row = exchange(send, "rows")
    outer_cost = outer(side, volume, near, lo, hi, single, bias, reg_outer)
    values = stats(first, side, cost, sides_cost, row, outer_cost)
    return joined(values, planes, rows, width)


def solution(mesh):
    in_specs = (P(None, "disp", ("tiles", "rows"), None), P(), P(), P())
    out_specs = P(("tiles", "rows"), None)
    return jax.shard_map(body, mesh=mesh, in_specs=in_specs, out_specs=out_specs, check_vma=False)
```

time: 130 us -> 125 us (0.962)
  blocking collectives: 0 us -> 25.6 us
  starting transfers between devices: 31.5 us -> 6.47 us
  local copies, waits for them, and re-layouts: 28.5 us -> 7.25 us
  Pallas kernels: 51.4 us -> 64.4 us
  other arithmetic: 1.41 us -> 3.86 us
  matrix products: 2.52 us -> 0.95 us
  waiting for transfers between devices: 13.7 us -> 15.1 us
    all_to_all x0 -> x2, blocking collectives: none -> 25.6 us  [the longest x1 15.5 us: joined(): pieces = lax.all_to_all(values, 'disp', 0, 0)]
    ppermute x5 -> x1, waiting for transfers between devices: 0.29 us -> 15.1 us  [up(): return lax.ppermute(x, axis, [(i, i + 1) for i in range(count - 1)])]
    ppermute x5 -> x1, starting transfers between devices: 17.8 us -> 4.45 us  [up(): return lax.ppermute(x, axis, [(i, i + 1) for i in range(count - 1)])]
    pallas_call x0 -> x4, Pallas kernels: none -> 12.5 us  [the longest x1 10.7 us: edges(): pl.pallas_call(edges_kernel, name='edges', grid=(planes // 2,), out_shape...]
    slice x2 -> x1, local copies, waits for them, and re-layouts: 9.57 us -> 0.01 us  [body(): ends = ([near[planes - 1], near[planes + 3]], [near[0], near[planes]])]
    ppermute x3 -> x2, waiting for transfers between devices: 8.93 us -> 0.01 us  [exchange(): lax.ppermute(x, axis, [(0, 1), (1, 0)] if lax.axis_size(axis) == 2 else [])]
    ppermute x3 -> x2, starting transfers between devices: 6.9 us -> 0.74 us  [exchange(): lax.ppermute(x, axis, [(0, 1), (1, 0)] if lax.axis_size(axis) == 2 else [])]
    ppermute x5 -> x1, starting transfers between devices: 6.75 us -> 1.28 us  [down(): return lax.ppermute(x, axis, [(i + 1, i) for i in range(count - 1)])]
  transfers between devices with their start and end apart: 13 -> 4, of which waited for: 5 -> 1; matrix products, arithmetic and copies ran while one was open for 21% -> 5% of each run, Pallas kernels for 39% -> 43%
where the time goes in v2:
time: 125 us; the launch traced here: 124 us
  Pallas kernels  64.4 us (52%)
  blocking collectives  25.6 us (20%)
  waiting for transfers between devices  15.1 us (12%)
  local copies, waits for them, and re-layouts  7.25 us (6%)
  starting transfers between devices  6.47 us (5%)
  other arithmetic  3.86 us (3%)
    pallas_call x1, Pallas kernels, inner(): pl.pallas_call(inner_kernel, name='inner', grid=(blocks + 1,), out_shape=...  43.5 us
    all_to_all x1, blocking collectives, joined(): pieces = lax.all_to_all(values, 'disp', 0, 0)  15.5 us
    ppermute x1, waiting for transfers between devices, up(): return lax.ppermute(x, axis, [(i, i + 1) for i in range(count - 1)])  15.1 us
    pallas_call x1, Pallas kernels, edges(): pl.pallas_call(edges_kernel, name='edges', grid=(planes // 2,), out_shape...  10.7 us
    all_to_all x1, blocking collectives, joined(): result = lax.all_to_all(join(pieces, planes), 'disp', 0, 0)  10.1 us
    pallas_call x1, Pallas kernels, outer(): pl.pallas_call(outer_kernel, name='outer', grid=(2,), out_shape=out, in_s...  7.99 us
    unnamed x25, local copies, waits for them, and re-layouts  4.87 us
    ppermute x1, starting transfers between devices, up(): return lax.ppermute(x, axis, [(i, i + 1) for i in range(count - 1)])  4.45 us
  transfers between devices with their start and end apart: 4, of which 1 were waited for; matrix products, arithmetic and copies ran while one was open for 5% of the time, Pallas kernels for 43%

profile of v2, /device:TPU:0, one launch (start us, length us, event | category | flops | bytes accessed | tf_op | source)
XLA Modules:
  0.0 123.8 jit_solution(3186147566780437276)
XLA Ops:
  0.0 10.7 %edges.1 = (bf16[28,32,512]{2,1,0:T(8,128)(2,1)}, bf16[16,32,512]{2,1,0:T(8,128)(2,1)S(1)}, bf16[16,32,512]{2,1,0:T(8,128)(2,1)S(1)}) custom-call(s32[1]{0:T(128)} %bitcast.1.side_ref, bf16[32,24,16,512]{3,2,1,0:T(8,128)(2,1)} %vol_ref.5), custom_call_target="tpu_custom_call" | custom-call | tf_op jit(solution)/shard_map/edges/pallas_call | solution.py:152
  10.7 0.5 collective-permute-start
  11.2 0.5 pack.1
  11.8 0.2 multiply_add_fusion.1
  11.9 0.5 add.26.reg_ref
  12.5 43.5 %inner.1 = (f32[24,16,512]{2,1,0:T(8,128)S(1)}, f32[22,2,32,512]{3,2,1,0:T(8,128)S(1)}) custom-call(bf16[32,24,16,512]{3,2,1,0:T(8,128)(2,1)} %vol_ref.5, bf16[384,192]{1,0:T(8,128)(2,1)S(1)} %get-tuple-element.16.weight_ref, f32[32,512]{1,0:T(8,128)S(1)} %broadcast_in_dim.2.bias_ref, bf16[144,512]{1,0:T(8,128)(2,1)S(1)} %add.26.reg_ref), custom_call_target="tpu_custom_call" | custom-call | flops 21743271936 | bytes 12582912 | tf_op jit(solution)/shard_map/inner/pallas_call | solution.py:246
  56.0 1.6 %copy-done.3 = f32[22,2,32,512]{3,2,1,0:T(8,128)} copy-done((f32[22,2,32,512]{3,2,1,0:T(8,128)}, f32[22,2,32,512]{3,2,1,0:T(8,128)S(1)}, u32[]{:S(2)}) %copy-start.3) | copy-done | bytes 2883608
  57.6 0.9 pad_maximum_fusion
  58.5 4.4 %collective-permute-start.2 = (bf16[18,32,512]{2,1,0:T(8,128)(2,1)}, bf16[18,32,512]{2,1,0:T(8,128)(2,1)S(1)}, u32[]{:S(2)}, u32[]{:S(2)}) collective-permute-start(bf16[18,32,512]{2,1,0:T(8,128)(2,1)} %pad_maximum_fusion), channel_id=1, source_target_pairs={{0,2},{2,4},{4,6},{6,8},{8,10},{10,12},{12,14},{1,3},{3,5},{5,7},{... | collective-permute-start | bytes 1769480 | tf_op jit(solution)/shard_map/ppermute | solution.py:535
  63.0 0.9 pad_maximum_fusion.1
  63.9 1.3 %collective-permute-start.3 = (bf16[18,32,512]{2,1,0:T(8,128)(2,1)}, bf16[18,32,512]{2,1,0:T(8,128)(2,1)S(1)}, u32[]{:S(2)}, u32[]{:S(2)}) collective-permute-start(bf16[18,32,512]{2,1,0:T(8,128)(2,1)} %pad_maximum_fusion.1), channel_id=1, source_target_pairs={{2,0},{4,2},{6,4},{8,6},{10,8},{12,10},{14,12},{3,1},{5,3},{7,5},{... | collective-permute-start | bytes 1769480 | tf_op jit(solution)/shard_map/ppermute | solution.py:540
  65.2 0.9 convolution_convert_fusion
  66.2 1.9 %multiply_add_fusion = bf16[3,3,16,18,32]{4,3,2,1,0:T(8,128)(2,1)} fusion(bf16[16,18]{1,0:T(8,128)(2,1)S(1)} %copy-done.6, bf16[3,3,32]{2,1,0:T(4,128)(2,1)S(1)} %get-tuple-element.32, bf16[16,18]{1,0:T(8,128)(2,1)S(1)} %copy-done.7, bf16[3,3,32]{2,1,0:T(4,128)(2,1)S(1)} %get-tuple-element.33, bf16[16,18]{1,0:T(8,128)(2,1)} %constant.27.clone, ...), kind=kLoop, calls=%fused_computation.1 | loop fusion | flops 414720 | bytes 169344 | tf_op jit(solution)/shard_map/add | solution.py:82
  68.1 1.7 %add.29.reg_ref = bf16[144,576]{1,0:T(8,128)(2,1)S(1)} reshape(bf16[3,3,16,18,32]{4,3,2,1,0:T(8,128)(2,1)} %multiply_add_fusion) | data formatting | bytes 331776 | tf_op jit(solution)/shard_map/add | solution.py:82
  69.8 0.8 copy-done.2
  70.6 1.8 %copy-done.4 = f32[22,2,32,512]{3,2,1,0:T(8,128)S(1)} copy-done((f32[22,2,32,512]{3,2,1,0:T(8,128)S(1)}, f32[22,2,32,512]{3,2,1,0:T(8,128)}, u32[]{:S(2)}) %copy-start.4) | copy-done | bytes 2883608
  72.4 1.3 %sides.1 = (f32[24,8,512]{2,1,0:T(8,128)S(1)}, f32[24,512]{1,0:T(8,128)S(1)}) custom-call(s32[1]{0:T(128)} %bitcast.1.side_ref, bf16[28,32,512]{2,1,0:T(8,128)(2,1)S(1)} %collective-permute-done.near_ref, f32[22,2,32,512]{3,2,1,0:T(8,128)S(1)} %copy-done.4, bf16[128,192]{1,0:T(8,128)(2,1)S(1)} %get-tuple-element.20.above_ref, ...), custom_call_target="tpu_custom_call" | custom-call | flops 2147483648 | bytes 4194304 | tf_op jit(solution)/shard_map/sides/pallas_call | solution.py:315
  73.7 0.3 collective-permute-start.1
  74.0 15.1 %collective-permute-done.2.lo_ref = bf16[18,32,512]{2,1,0:T(8,128)(2,1)S(1)} collective-permute-done((bf16[18,32,512]{2,1,0:T(8,128)(2,1)}, bf16[18,32,512]{2,1,0:T(8,128)(2,1)S(1)}, u32[]{:S(2)}, u32[]{:S(2)}) %collective-permute-start.2) | collective-permute-done | bytes 589856 | tf_op jit(solution)/shard_map/ppermute | solution.py:535
  89.1 8.0 %outer.1.outer_ref = f32[2,3,16,512]{3,2,1,0:T(8,128)S(1)} custom-call(s32[1]{0:T(128)} %bitcast.1.side_ref, bf16[32,24,16,512]{3,2,1,0:T(8,128)(2,1)} %vol_ref.5, bf16[28,32,512]{2,1,0:T(8,128)(2,1)S(1)} %collective-permute-done.near_ref, bf16[18,32,512]{2,1,0:T(8,128)(2,1)S(1)} %collective-permute-done.2.lo_ref, ...), custom_call_target="tpu_custom_call" | custom-call | flops 1811939328 | bytes 4194304 | tf_op jit(solution)/shard_map/outer/pallas_call | solution.py:399
  97.1 0.4 stats.1
  97.6 15.5 %all_to_all.10.in_ref = f32[8,8,8,128]{3,2,1,0:T(8,128)S(1)} all-to-all(f32[8,8,8,128]{3,2,1,0:T(8,128)S(1)} %stats.1), channel_id=1, replica_groups=mesh['tiles'=2,'disp'=8,'rows'=2] {'disp'}, dimensions={0} | all-to-all | bytes 524288 | tf_op jit(solution)/shard_map/all_to_all | solution.py:523
  113.2 10.1 %all_to_all.11 = f32[8,8,128]{2,1,0:T(8,128)S(1)} all-to-all(f32[8,8,128]{2,1,0:T(8,128)S(1)} %join.1), channel_id=1, replica_groups=mesh['tiles'=2,'disp'=8,'rows'=2] {'disp'}, dimensions={0} | all-to-all | bytes 65536 | tf_op jit(solution)/shard_map/all_to_all | solution.py:524
  123.2 0.6 copy.19
  (30 shorter events, 0.3 us)
Async XLA Ops:
  0.0 11.7 %copy-start.8 = (bf16[16,16]{1,0:T(8,128)(2,1)S(1)}, bf16[16,16]{1,0:T(8,128)(2,1)}, u32[]{:S(2)}) copy-start(bf16[16,16]{1,0:T(8,128)(2,1)} %constant.26.clone) | copy-start | bytes 1540
  0.0 11.7 %copy-start.9 = (bf16[16,16]{1,0:T(8,128)(2,1)S(1)}, bf16[16,16]{1,0:T(8,128)(2,1)}, u32[]{:S(2)}) copy-start(bf16[16,16]{1,0:T(8,128)(2,1)} %constant.25.clone) | copy-start | bytes 1540
  0.0 11.7 %copy-start.10 = (bf16[16,16]{1,0:T(8,128)(2,1)S(1)}, bf16[16,16]{1,0:T(8,128)(2,1)}, u32[]{:S(2)}) copy-start(bf16[16,16]{1,0:T(8,128)(2,1)} %constant.24.clone) | copy-start | bytes 1540
  0.0 11.2 %copy-start.5 = (bf16[27,32]{1,0:T(8,128)(2,1)S(1)}, bf16[27,32]{1,0:T(8,128)(2,1)}, u32[]{:S(2)}) copy-start(bf16[27,32]{1,0:T(8,128)(2,1)} %param.14) | copy-start | bytes 5188
  0.0 11.2 %copy-start = (bf16[27,32,32]{2,1,0:T(8,128)(2,1)S(1)}, bf16[27,32,32]{2,1,0:T(8,128)(2,1)}, u32[]{:S(2)}) copy-start(bf16[27,32,32]{2,1,0:T(8,128)(2,1)} %conv_ref.1) | copy-start | bytes 165892
  0.0 12.4 %copy-start.11 = (f32[32]{0:T(128)S(1)}, f32[32]{0:T(128)}, u32[]{:S(2)}) copy-start(f32[32]{0:T(128)} %param.13) | copy-start | bytes 388
  10.7 46.9 %collective-permute-start = (bf16[28,32,512]{2,1,0:T(8,128)(2,1)}, bf16[28,32,512]{2,1,0:T(8,128)(2,1)S(1)}, u32[]{:S(2)}, u32[]{:S(2)}) collective-permute-start(bf16[28,32,512]{2,1,0:T(8,128)(2,1)} %get-tuple-element.18), channel_id=1, source_target_pairs={{0,1},{1,0},{2,3},{3,2},{4,5},{5,4},{6,7},{7,6},{8,9},{9,8},{10,11... | collective-permute-start | bytes 2752520 | tf_op jit(solution)/shard_map/ppermute | solution.py:530
  11.7 44.3 %copy-start.1 = (bf16[128,192]{1,0:T(8,128)(2,1)}, bf16[128,192]{1,0:T(8,128)(2,1)S(1)}, u32[]{:S(2)}) copy-start(bf16[128,192]{1,0:T(8,128)(2,1)S(1)} %get-tuple-element.21.below_ref) | copy-start | bytes 147460
  12.5 53.7 %copy-start.6 = (bf16[16,18]{1,0:T(8,128)(2,1)S(1)}, bf16[16,18]{1,0:T(8,128)(2,1)}, u32[]{:S(2)}) copy-start(bf16[16,18]{1,0:T(8,128)(2,1)} %constant.29.clone) | copy-start | bytes 1732
  12.5 53.7 %copy-start.7 = (bf16[16,18]{1,0:T(8,128)(2,1)S(1)}, bf16[16,18]{1,0:T(8,128)(2,1)}, u32[]{:S(2)}) copy-start(bf16[16,18]{1,0:T(8,128)(2,1)} %constant.28.clone) | copy-start | bytes 1732
  56.0 1.6 %copy-start.3 = (f32[22,2,32,512]{3,2,1,0:T(8,128)}, f32[22,2,32,512]{3,2,1,0:T(8,128)S(1)}, u32[]{:S(2)}) copy-start(f32[22,2,32,512]{3,2,1,0:T(8,128)S(1)} %get-tuple-element.19.pre_ref) | copy-start | bytes 8650756
  58.5 30.6 %collective-permute-start.2 = (bf16[18,32,512]{2,1,0:T(8,128)(2,1)}, bf16[18,32,512]{2,1,0:T(8,128)(2,1)S(1)}, u32[]{:S(2)}, u32[]{:S(2)}) collective-permute-start(bf16[18,32,512]{2,1,0:T(8,128)(2,1)} %pad_maximum_fusion), channel_id=1, source_target_pairs={{0,2},{2,4},{4,6},{6,8},{8,10},{10,12},{12,14},{1,3},{3,5},{5,7},{... | collective-permute-start | bytes 1769480 | tf_op jit(solution)/shard_map/ppermute | solution.py:535
  63.9 25.2 %collective-permute-start.3 = (bf16[18,32,512]{2,1,0:T(8,128)(2,1)}, bf16[18,32,512]{2,1,0:T(8,128)(2,1)S(1)}, u32[]{:S(2)}, u32[]{:S(2)}) collective-permute-start(bf16[18,32,512]{2,1,0:T(8,128)(2,1)} %pad_maximum_fusion.1), channel_id=1, source_target_pairs={{2,0},{4,2},{6,4},{8,6},{10,8},{12,10},{14,12},{3,1},{5,3},{7,5},{... | collective-permute-start | bytes 1769480 | tf_op jit(solution)/shard_map/ppermute | solution.py:540
  69.8 0.8 copy-start.2
  70.6 1.8 %copy-start.4 = (f32[22,2,32,512]{3,2,1,0:T(8,128)S(1)}, f32[22,2,32,512]{3,2,1,0:T(8,128)}, u32[]{:S(2)}) copy-start(f32[22,2,32,512]{3,2,1,0:T(8,128)} %copy-done.3) | copy-start | bytes 8650756
  73.7 23.4 %collective-permute-start.1 = (f32[24,512]{1,0:T(8,128)S(1)}, f32[24,512]{1,0:T(8,128)S(1)}, u32[]{:S(2)}, u32[]{:S(2)}) collective-permute-start(f32[24,512]{1,0:T(8,128)S(1)} %get-tuple-element.23), channel_id=1, source_target_pairs={{0,1},{1,0},{2,3},{3,2},{4,5},{5,4},{6,7},{7,6},{8,9},{9,8},{10,11... | collective-permute-start | bytes 147464 | tf_op jit(solution)/shard_map/ppermute | solution.py:530

commit v3 on v2

--- a/solution.py
+++ b/solution.py
@@ -48,55 +48,71 @@
     return [[tap(p - q + 2, b, c) for p in range(2) for c in range(3)] for q in range(4)]
 
 
-def pack_kernel(tables, conv_ref, *out_refs):
+def pack_kernel(tables, rows, conv_ref, bias_ref, reg_ref, *refs):
     ch = conv_ref.shape[1]
-    for table, out_ref in zip(tables, out_refs):
+    weight_refs = refs[: len(tables)]
+    wide_ref, inner_ref, outer_ref, edges_ref, turn_ref, line_ref, sparse_ref = refs[len(tables) :]
+    for table, out_ref in zip(tables, weight_refs):
         for m, row in enumerate(table):
             for k, t in enumerate(row):
                 block = jnp.zeros((ch, ch), BF16) if t is None else conv_ref[t]
                 out_ref[m * ch : (m + 1) * ch, k * ch : (k + 1) * ch] = block
-
-
-def packed(conv_weight):
+    wide_ref[...] = jnp.broadcast_to(bias_ref[...], wide_ref.shape)
+    size = turn_ref.shape[0]
+    r = lax.broadcasted_iota(jnp.int32, (size, size), 0)
+    k = lax.broadcasted_iota(jnp.int32, (size, size), 1)
+    half = size // rows
+    hit = k == (r % half) * rows + r // half
+    turn_ref[...] = jnp.where(hit, 1.0, 0.0).astype(BF16)
+
+    reg = reg_ref[...].astype(F32)
+    line_ref[...] = jnp.zeros_like(line_ref)
+    sparse_ref[...] = jnp.zeros_like(sparse_ref)
+    for a in range(3):
+        for b in range(3):
+            for c in range(3):
+                t = tap(a, b, c)
+                one = reg[t : t + 1]
+                line_ref[a * 3 + c : a * 3 + c + 1, b * ch : (b + 1) * ch] = one
+                for p in range(2):
+                    q = p + 2 - a
+                    for e in range(2):
+                        at = q * 24 + c * 6 + (2 - b) + 3 * e
+                        col = (2 * p + e) * ch
+                        sparse_ref[at : at + 1, col : col + ch] = one
+    edges_ref[...] = sparse_ref[...].astype(BF16)
+    width = line_ref.shape[1]
+    row = lax.broadcasted_iota(jnp.int32, (rows, width), 0)
+    for k in range(9):
+        x = jnp.broadcast_to(line_ref[k : k + 1], (rows, width))
+        step = 1
+        while step < rows:
+            x = jnp.where((row & step) != 0, pltpu.roll(x, step * ch, 1), x)
+            step *= 2
+        at = slice(k * rows, (k + 1) * rows)
+        outer_ref[at] = x[:, : (rows + 2) * ch].astype(BF16)
+        inner_ref[at] = pltpu.roll(x, width - ch, 1)[:, : rows * ch].astype(BF16)
+
+
+def packed(conv_weight, conv_bias, reg_weight, rows, width):
     ch = conv_weight.shape[1]
     tables = [spread_table(), halo_table(0), halo_table(2), single_table()]
-    outs = [jax.ShapeDtypeStruct((len(t) * ch, len(t[0]) * ch), BF16) for t in tables]
+    shapes = [((len(t) * ch, len(t[0]) * ch), BF16) for t in tables]
+    shapes += [
+        ((ch, width), F32), ((9 * rows, rows * ch), BF16), ((9 * rows, (rows + 2) * ch), BF16),
+        ((96, 4 * ch), BF16), ((rows * ch // 2, rows * ch // 2), BF16),
+    ]
+    outs = [jax.ShapeDtypeStruct(*x) for x in shapes]
+    line = -(-(rows + 3) * ch // 128) * 128
     return pl.pallas_call(
-        functools.partial(pack_kernel, tables),
+        functools.partial(pack_kernel, tables, rows),
         name="pack",
         out_shape=outs,
-        in_specs=[VMEM],
+        in_specs=[VMEM] * 3,
         out_specs=[VMEM] * len(outs),
+        scratch_shapes=[pltpu.VMEM((16, line), F32), pltpu.VMEM((96, 4 * ch), F32)],
         compiler_params=ROOM,
-    )(conv_weight)
-
-
-def regression_rows(reg_weight, rows, inputs, first):
-    ch = reg_weight.shape[1]
-    taps = reg_weight.reshape(3, 3, 3, ch)
-    total = None
-    for b in range(3):
-        hit = np.arange(inputs)[None, :] + first == np.arange(rows)[:, None] + b - 1
-        hit = jnp.asarray(hit, BF16)
-        term = taps[:, b][:, :, None, None, :] * hit[None, None, :, :, None]
-        total = term if total is None else total + term
-    return total.reshape(9 * rows, inputs * ch)
-
-
-def regression_edges(reg_weight, rows):
-    ch = reg_weight.shape[1]
-    pick = np.zeros((4, 24, 2, 2, 27))
-    for q in range(4):
-        for p in range(2):
-            for c in range(3):
-                for k, out in enumerate((-1, 0, 1, rows - 2, rows - 1, rows)):
-                    for e, row in enumerate((0, rows - 1)):
-                        t = tap(p - q + 2, row - out + 1, c)
-                        if t is not None:
-                            pick[q, c * 6 + k, p, e, t] = 1
-    pick = jnp.asarray(pick.reshape(96, 4, 27), BF16)
-    out = jnp.einsum("mkt,ti->mki", pick, reg_weight, preferred_element_type=F32)
-    return out.astype(BF16).reshape(96, 4 * ch)
+    )(conv_weight, conv_bias[:, None], reg_weight)
 
 
 def shifted(x, by):
@@ -119,49 +135,83 @@
         taps_ref[slot, pl.ds(row, count), pl.ds(c * ch + at, size), :] = y.reshape(x.shape)
 
 
-def edges_kernel(side_ref, vol_ref, near_ref, first_ref, last_ref):
+def turn(taps_ref, slot, row, at, block, turn_ref):
+    size, rows, width = block.shape
+    ch = taps_ref.shape[2] // 3
+    y = jnp.dot(turn_ref[...], block.reshape(size * rows, width), preferred_element_type=F32)
+    taps_ref[slot, pl.ds(row, rows), ch + at : ch + at + size, :] = (
+        y.astype(BF16).reshape(rows, size, width)
+    )
+
+
+def spread(taps_ref, slot, row, count):
+    width = taps_ref.shape[3]
+    ch = taps_ref.shape[2] // 3
+    x = taps_ref[slot, pl.ds(row, count), ch : 2 * ch, :].reshape(count * ch, width)
+    taps_ref[slot, pl.ds(row, count), :ch, :] = shifted(x, 1).reshape(count, ch, width)
+    taps_ref[slot, pl.ds(row, count), 2 * ch :, :] = shifted(x, -1).reshape(count, ch, width)
+
+
+def edges_kernel(side_ref, vol_ref, near_ref, first_ref, last_ref, pick_ref):
     s = pl.program_id(0)
     steps = pl.num_programs(0)
-    rows = vol_ref.shape[2]
+    ch, _, rows, width = vol_ref.shape
     planes = 2 * steps
-    top = side_ref[0] == 0
+
+    @pl.when(s == 0)
+    def _():
+        r = lax.broadcasted_iota(jnp.int32, pick_ref.shape, 0)
+        k = lax.broadcasted_iota(jnp.int32, pick_ref.shape, 1)
+        far = jnp.where(r >= ch, 1, 0)
+        row = jnp.where(side_ref[0] == 0, rows - 1 - far, far)
+        pick_ref[...] = jnp.where(k == (r - ch * far) * rows + row, 1.0, 0.0).astype(BF16)
+
+    def rows_of(p, part):
+        x = vol_ref[:, p].reshape(ch * rows, width)
+        w = pick_ref[part * ch : (part + 1) * ch]
+        return jnp.dot(w, x, preferred_element_type=F32).astype(BF16)
+
     for p in range(2):
-        row = jnp.where(top, vol_ref[:, p, rows - 1, :], vol_ref[:, p, 0, :])
-        near_ref[2 * s + p] = row
+        near_ref[2 * s + p] = rows_of(p, 0)
 
     @pl.when((s == 0) | (s == steps - 1))
     def _():
         for p in range(2):
-            row = jnp.where(top, vol_ref[:, p, rows - 2, :], vol_ref[:, p, 1, :])
-            near_ref[planes + p + jnp.where(s == 0, 0, 2)] = row
+            near_ref[planes + p + jnp.where(s == 0, 0, 2)] = rows_of(p, 1)
 
     @pl.when(s == 0)
     def _():
-        first_ref[...] = jnp.swapaxes(vol_ref[:, 0], 0, 1)
+        first_ref[0] = near_ref[0]
+        first_ref[1] = near_ref[planes]
 
     @pl.when(s == steps - 1)
     def _():
-        last_ref[...] = jnp.swapaxes(vol_ref[:, 1], 0, 1)
+        last_ref[0] = near_ref[planes - 1]
+        last_ref[1] = near_ref[planes + 3]
 
 
 def edges(side, volume):
     ch, planes, rows, width = volume.shape
     near = jax.ShapeDtypeStruct((planes + 4, ch, width), BF16)
-    plane = jax.ShapeDtypeStruct((rows, ch, width), BF16)
+    corner = jax.ShapeDtypeStruct((2, ch, width), BF16)
     zero = lambda s: (0, 0, 0)
     return pl.pallas_call(
         edges_kernel,
         name="edges",
         grid=(planes // 2,),
-        out_shape=(near, plane, plane),
+        out_shape=(near, corner, corner),
         in_specs=[SMEM, pl.BlockSpec((ch, 2, rows, width), lambda s: (0, s, 0, 0))],
-        out_specs=[pl.BlockSpec(x.shape, zero) for x in (near, plane, plane)],
+        out_specs=[pl.BlockSpec(x.shape, zero) for x in (near, corner, corner)],
+        scratch_shapes=[pltpu.VMEM((2 * ch, ch * rows), BF16)],
         compiler_params=ROOM,
+        cost_estimate=pl.CostEstimate(
+            flops=1 << 30, bytes_accessed=volume.size * 2, transcendentals=0
+        ),
     )(side, volume)
 
 
 def inner_kernel(
-    vol_ref, weight_ref, bias_ref, reg_ref, cost_ref, pre_ref,
+    vol_ref, weight_ref, bias_ref, reg_ref, turn_ref, cost_ref, pre_ref,
     taps_ref, acc_ref, hidden_ref, sums_ref,
 ):
     s = pl.program_id(0)
@@ -173,13 +223,16 @@
     old = ((s + 1) % 2) * 2
 
     def stage(part):
-        p, h = part // 2, part % 2
-        block = vol_ref[h * half : (h + 1) * half, p]
-        put(taps_ref, new + p, 0, h * half, jnp.swapaxes(block, 0, 1))
+        p, h = part // 4, part % 4
+        if h < 2:
+            block = vol_ref[h * half : (h + 1) * half, p]
+            turn(taps_ref, new + p, 0, h * half, block, turn_ref)
+        else:
+            spread(taps_ref, new + p, (h - 2) * (rows // 2), rows // 2)
 
     @pl.when(s == 0)
     def _():
-        for part in range(4):
+        for part in range(8):
             stage(part)
         sums_ref[...] = jnp.zeros_like(sums_ref)
         hidden_ref[...] = jnp.zeros_like(hidden_ref)
@@ -206,8 +259,8 @@
                             if not fresh:
                                 part = part + acc_ref[slots[do], 2 * j + ho, :, lanes]
                             acc_ref[slots[do], 2 * j + ho, :, lanes] = part
-                if j % (tiles // 2) == tiles // 2 - 1:
-                    stage(2 * p + j // (tiles // 2))
+                if (j + 1) * 4 // tiles > j * 4 // tiles:
+                    stage(4 * p + j * 4 // tiles)
 
     @pl.when(s >= 2)
     def _():
@@ -236,7 +289,7 @@
         lax.fori_loop(0, planes, finish, 0)
 
 
-def inner(volume, weights, bias, reg):
+def inner(volume, weights, bias, reg, turning):
     ch, planes, rows, width = volume.shape
     blocks = planes // 2
     whole = lambda x: pl.BlockSpec(x.shape, lambda s: (0,) * x.ndim)
@@ -250,7 +303,7 @@
         out_shape=(cost, pre),
         in_specs=[
             pl.BlockSpec((ch, 2, rows, width), lambda s: (0, jnp.minimum(s, blocks - 1), 0, 0)),
-            whole(weights), whole(bias), whole(reg),
+            whole(weights), whole(bias), whole(reg), whole(turning),
         ],
         out_specs=(
             pl.BlockSpec(cost.shape, lambda s: (0, 0, 0)),
@@ -266,7 +319,7 @@
         cost_estimate=pl.CostEstimate(
             flops=2 * work, bytes_accessed=volume.size * 2, transcendentals=0
         ),
-    )(volume, weights, bias, reg)
+    )(volume, weights, bias, reg, turning)
 
 
 def sides_kernel(
@@ -333,8 +386,8 @@
 
 
 def outer_kernel(
-    side_ref, vol_ref, near_ref, lo_ref, hi_ref, weight_ref, bias_ref, reg_ref, out_ref,
-    taps_ref, hidden_ref,
+    side_ref, vol_ref, near_ref, lo_ref, hi_ref, lo_rows_ref, hi_rows_ref, weight_ref, bias_ref,
+    reg_ref, turn_ref, out_ref, taps_ref, hidden_ref,
 ):
     s = pl.program_id(0)
     ch, _, rows, width = vol_ref.shape
@@ -351,15 +404,18 @@
 
     low = s == 0
     for p in range(2):
-        slot = 1 + p - s
-        stage_rows(slot, near_ref[s * (planes - 2) + p], near_ref[planes + 2 * s + p])
-        for h in range(2):
-            block = vol_ref[h * half : (h + 1) * half, p]
-            put(taps_ref, slot, 2, h * half, jnp.swapaxes(block, 0, 1))
-    pick = lambda r: jnp.where(low, lo_ref[r], hi_ref[r])
-    stage_rows(2 * s, pick(rows), pick(rows + 1))
-    for r in range(0, rows, 4):
-        put(taps_ref, 2 * s, 2 + r, 0, pick(slice(r, r + 4)))
+        stage_rows(1 + p - s, near_ref[s * (planes - 2) + p], near_ref[planes + 2 * s + p])
+    corner = jnp.where(low, lo_rows_ref[...], hi_rows_ref[...])
+    stage_rows(2 * s, corner[0], corner[1])
+    for h in range(2):
+        part = slice(h * half, (h + 1) * half)
+        for p in range(2):
+            turn(taps_ref, 1 + p - s, 2, h * half, vol_ref[part, p], turn_ref)
+        far_block = jnp.where(low, lo_ref[part], hi_ref[part])
+        turn(taps_ref, 2 * s, 2, h * half, far_block, turn_ref)
+    for slot in range(3):
+        for r in range(0, rows, rows // 2):
+            spread(taps_ref, slot, 2 + r, rows // 2)
 
     for j in range(rows // 2 + 1):
         for n in range(0, width, LANES):
@@ -391,7 +447,7 @@
         out_ref[0, 2 - a] = shifted(r[0], 1) + r[1] + shifted(r[2], -1)
 
 
-def outer(side, volume, near, lo, hi, weights, bias, reg):
+def outer(side, volume, near, halos, weights, bias, reg, turning):
     ch, planes, rows, width = volume.shape
     whole = lambda x: pl.BlockSpec(x.shape, lambda s: (0,) * x.ndim)
     out = jax.ShapeDtypeStruct((2, 3, rows, width), F32)
@@ -404,7 +460,8 @@
         in_specs=[
             SMEM,
             pl.BlockSpec((ch, 2, rows, width), lambda s: (0, s * (planes // 2 - 1), 0, 0)),
-            whole(near), whole(lo), whole(hi), whole(weights), whole(bias), whole(reg),
+            whole(near), *map(whole, halos), whole(weights), whole(bias), whole(reg),
+            whole(turning),
         ],
         out_specs=pl.BlockSpec((1, 3, rows, width), lambda s: (s, 0, 0, 0)),
         scratch_shapes=[
@@ -413,7 +470,7 @@
         ],
         compiler_params=ROOM,
         cost_estimate=pl.CostEstimate(flops=2 * work, bytes_accessed=1 << 22, transcendentals=0),
-    )(side, volume, near, lo, hi, weights, bias, reg)
+    )(side, volume, near, *halos, weights, bias, reg, turning)
 
 
 def stats_kernel(
@@ -540,26 +597,39 @@
     return lax.ppermute(x, axis, [(i + 1, i) for i in range(count - 1)])
 
 
+def across(x, step):
+    count = lax.axis_size("disp")
+    sides = lax.axis_size("rows")
+    pairs = [
+        (i * sides + r, (i + step) * sides + 1 - r)
+        for i in range(count) for r in range(sides)
+        if 0 <= i + step < count and sides == 2
+    ]
+    return lax.ppermute(x, ("disp", "rows"), pairs)
+
+
 def body(volume, conv_weight, conv_bias, reg_weight):
     ch, planes, rows, width = volume.shape
-    bias = jnp.broadcast_to(conv_bias[:, None], (ch, width))
     side = lax.axis_index("rows").astype(jnp.int32).reshape(1)
     first = (lax.axis_index("disp") * planes).astype(jnp.int32).reshape(1)
 
-    near, first_plane, last_plane = edges(side, volume)
+    ends = volume[:, planes - 1], volume[:, 0]
+    volume, ends = lax.optimization_barrier((volume, ends))
+    lo = up(ends[0], "disp")
+    hi = down(ends[1], "disp")
+    near, first_rows, last_rows = edges(side, volume)
     near = exchange(near, "rows")
-    spread, above, below, single = packed(conv_weight)
-    reg_inner = regression_rows(reg_weight, rows, rows, 0)
-    reg_outer = regression_rows(reg_weight, rows, rows + 2, -1)
-    reg_edges = regression_edges(reg_weight, rows)
-    ends = [near[planes - 1], near[planes + 3]], [near[0], near[planes]]
-    lo = up(jnp.concatenate([last_plane, jnp.stack(ends[0])]), "disp")
-    hi = down(jnp.concatenate([first_plane, jnp.stack(ends[1])]), "disp")
-
-    cost, pre = inner(volume, spread, bias, reg_inner)
+    lo_rows = across(last_rows, 1)
+    hi_rows = across(first_rows, -1)
+    spread_w, above, below, single, bias, reg_inner, reg_outer, reg_edges, turning = packed(
+        conv_weight, conv_bias, reg_weight, rows, width
+    )
+
+    cost, pre = inner(volume, spread_w, bias, reg_inner, turning)
     sides_cost, send = sides(side, near, pre, above, below, bias, reg_edges)
     row = exchange(send, "rows")
-    outer_cost = outer(side, volume, near, lo, hi, single, bias, reg_outer)
+    halos = (lo, hi, lo_rows, hi_rows)
+    outer_cost = outer(side, volume, near, halos, single, bias, reg_outer, turning)
     values = stats(first, side, cost, sides_cost, row, outer_cost)
     return joined(values, planes, rows, width)
 

time: 125 us -> 115 us (0.920)
  waiting for transfers between devices: 15.1 us -> 0.02 us
  starting transfers between devices: 6.47 us -> 12.3 us
  other arithmetic: 3.86 us -> 0 us
  local copies, waits for them, and re-layouts: 7.25 us -> 9.27 us
  Pallas kernels: 64.4 us -> 66.3 us
    ppermute x1, waiting for transfers between devices: 15.1 us -> 0.01 us  [up(): return lax.ppermute(x, axis, [(i, i + 1) for i in range(count - 1)])]
    ppermute x0 -> x2, starting transfers between devices: none -> 4.71 us  [across(): return lax.ppermute(x, ('disp', 'rows'), pairs)]
    squeeze x0 -> x1, local copies, waits for them, and re-layouts: none -> 2.28 us  [body(): ends = (volume[:, planes - 1], volume[:, 0])]
    add x2 -> x0, local copies, waits for them, and re-layouts: 2.18 us -> none  [regression_rows(): total = term if total is None else total + term]
    add x2 -> x0, other arithmetic: 2.05 us -> none  [regression_rows(): total = term if total is None else total + term]
    unnamed x25 -> x19, local copies, waits for them, and re-layouts: 4.87 us -> 6.91 us
    concatenate x2 -> x0, other arithmetic: 1.8 us -> none  [the longest x1 0.91 us: body(): hi = down(jnp.concatenate([first_plane, jnp.stack(ends[1])]), 'disp')]
  transfers between devices with their start and end apart: 4 -> 6, of which waited for: 1 -> 0; matrix products, arithmetic and copies ran while one was open for 5% -> 0% of each run, Pallas kernels for 43% -> 57%
where the time goes in v3:
time: 115 us
  Pallas kernels  66.3 us (58%)
  blocking collectives  26.8 us (23%)
  starting transfers between devices  12.3 us (11%)
  local copies, waits for them, and re-layouts  9.27 us (8%)
    pallas_call x1, Pallas kernels, inner(): pl.pallas_call(inner_kernel, name='inner', grid=(blocks + 1,), out_shape=...  44.4 us
    all_to_all x1, blocking collectives, joined(): pieces = lax.all_to_all(values, 'disp', 0, 0)  16.8 us
    pallas_call x1, Pallas kernels, edges(): pl.pallas_call(edges_kernel, name='edges', grid=(planes // 2,), out_shape...  11.3 us
    all_to_all x1, blocking collectives, joined(): result = lax.all_to_all(join(pieces, planes), 'disp', 0, 0)  10.1 us
    pallas_call x1, Pallas kernels, outer(): pl.pallas_call(outer_kernel, name='outer', grid=(2,), out_shape=out, in_s...  7.17 us
    unnamed x19, local copies, waits for them, and re-layouts  6.91 us
    ppermute x1, starting transfers between devices, up(): return lax.ppermute(x, axis, [(i, i + 1) for i in range(count - 1)])  4.9 us
    ppermute x2, starting transfers between devices, across(): return lax.ppermute(x, ('disp', 'rows'), pairs)  4.71 us
  transfers between devices with their start and end apart: 6, of which 0 were waited for; matrix products, arithmetic and copies ran while one was open for 0% of the time, Pallas kernels for 57%

profile of v3, /device:TPU:0, one launch (start us, length us, event | category | flops | bytes accessed | tf_op | source)
XLA Modules:
  0.0 114.8 jit_solution(15210357842629047619)
XLA Ops:
  0.0 2.3 %slice_bitcast_fusion = (bf16[32,16,512]{2,1,0:T(8,128)(2,1)}, bf16[32,16,512]{2,1,0:T(8,128)(2,1)}) fusion(bf16[32,24,16,512]{3,2,1,0:T(8,128)(2,1)} %vol_ref.2), kind=kLoop, calls=%fused_computation | loop fusion | bytes 2097152 | tf_op jit(solution)/shard_map/squeeze | solution.py:616
  2.3 4.9 %collective-permute-start.2 = (bf16[32,16,512]{2,1,0:T(8,128)(2,1)}, bf16[32,16,512]{2,1,0:T(8,128)(2,1)S(1)}, u32[]{:S(2)}, u32[]{:S(2)}) collective-permute-start(bf16[32,16,512]{2,1,0:T(8,128)(2,1)} %get-tuple-element.37), channel_id=1, source_target_pairs={{0,2},{2,4},{4,6},{6,8},{8,10},{10,12},{12,14},{1,3},{3,5},{5,7},{... | collective-permute-start | bytes 1572872 | tf_op jit(solution)/shard_map/ppermute | solution.py:592
  7.2 1.3 %collective-permute-start.3 = (bf16[32,16,512]{2,1,0:T(8,128)(2,1)}, bf16[32,16,512]{2,1,0:T(8,128)(2,1)S(1)}, u32[]{:S(2)}, u32[]{:S(2)}) collective-permute-start(bf16[32,16,512]{2,1,0:T(8,128)(2,1)} %get-tuple-element.38), channel_id=1, source_target_pairs={{2,0},{4,2},{6,4},{8,6},{10,8},{12,10},{14,12},{3,1},{5,3},{7,5},{... | collective-permute-start | bytes 1572872 | tf_op jit(solution)/shard_map/ppermute | solution.py:597
  8.5 11.3 %edges.1 = (bf16[28,32,512]{2,1,0:T(8,128)(2,1)}, bf16[2,32,512]{2,1,0:T(8,128)(2,1)S(1)}, bf16[2,32,512]{2,1,0:T(8,128)(2,1)S(1)}) custom-call(s32[1]{0:T(128)} %bitcast.1.side_ref, bf16[32,24,16,512]{3,2,1,0:T(8,128)(2,1)} %vol_ref.2), custom_call_target="tpu_custom_call" | custom-call | flops 1073741824 | bytes 12582912 | tf_op jit(solution)/shard_map/edges/pallas_call | solution.py:198
  19.8 3.4 %collective-permute-start.4 = (bf16[2,32,512]{2,1,0:T(8,128)(2,1)S(1)}, bf16[2,32,512]{2,1,0:T(8,128)(2,1)S(1)}, u32[]{:S(2)}, u32[]{:S(2)}) collective-permute-start(bf16[2,32,512]{2,1,0:T(8,128)(2,1)S(1)} %get-tuple-element.39), channel_id=1, source_target_pairs={{0,3},{1,2},{2,5},{3,4},{4,7},{5,6},{6,9},{7,8},{8,11},{9,10},{10,... | collective-permute-start | bytes 196616 | tf_op jit(solution)/shard_map/ppermute | solution.py:608
  23.2 1.3 %collective-permute-start.5 = (bf16[2,32,512]{2,1,0:T(8,128)(2,1)S(1)}, bf16[2,32,512]{2,1,0:T(8,128)(2,1)S(1)}, u32[]{:S(2)}, u32[]{:S(2)}) collective-permute-start(bf16[2,32,512]{2,1,0:T(8,128)(2,1)S(1)} %get-tuple-element.40), channel_id=1, source_target_pairs={{2,1},{3,0},{4,3},{5,2},{6,5},{7,4},{8,7},{9,6},{10,9},{11,8},{12,... | collective-permute-start | bytes 196616 | tf_op jit(solution)/shard_map/ppermute | solution.py:608
  24.5 1.3 %collective-permute-start = (bf16[28,32,512]{2,1,0:T(8,128)(2,1)}, bf16[28,32,512]{2,1,0:T(8,128)(2,1)S(1)}, u32[]{:S(2)}, u32[]{:S(2)}) collective-permute-start(bf16[28,32,512]{2,1,0:T(8,128)(2,1)} %get-tuple-element.30), channel_id=1, source_target_pairs={{0,1},{1,0},{2,3},{3,2},{4,5},{5,4},{6,7},{7,6},{8,9},{9,8},{10,11... | collective-permute-start | bytes 2752520 | tf_op jit(solution)/shard_map/ppermute | solution.py:587
  25.8 0.1 copy.7.bias_ref
  25.9 1.6 %pack.1 = (bf16[384,192]{1,0:T(8,128)(2,1)S(1)}, bf16[128,192]{1,0:T(8,128)(2,1)S(1)}, bf16[128,192]{1,0:T(8,128)(2,1)S(1)}, bf16[256,256]{1,0:T(8,128)(2,1)S(1)...) custom-call(bf16[27,32,32]{2,1,0:T(8,128)(2,1)S(1)} %copy-done, ...), custom_call_target="tpu_custom_call" | custom-call | tf_op jit(solution)/shard_map/pack/pallas_call | solution.py:107
  27.5 0.6 copy-done.2
  28.2 0.6 copy-done.4
  28.8 44.4 %inner.1 = (f32[24,16,512]{2,1,0:T(8,128)S(1)}, f32[22,2,32,512]{3,2,1,0:T(8,128)S(1)}) custom-call(bf16[32,24,16,512]{3,2,1,0:T(8,128)(2,1)} %vol_ref.2, bf16[384,192]{1,0:T(8,128)(2,1)S(1)} %get-tuple-element.25.weight_ref, f32[32,512]{1,0:T(8,128)S(1)} %get-tuple-element.26.bias_ref, bf16[144,512]{1,0:T(8,128)(2,1)S(1)} %get-tuple-element.27.reg_ref, ...), custom_call_target="tpu_custom_call" | custom-call | flops 21743271936 | bytes 12582912 | tf_op jit(solution)/shard_map/inner/pallas_call | solution.py:299
  73.2 1.6 %copy-done.6 = f32[22,2,32,512]{3,2,1,0:T(8,128)} copy-done((f32[22,2,32,512]{3,2,1,0:T(8,128)}, f32[22,2,32,512]{3,2,1,0:T(8,128)S(1)}, u32[]{:S(2)}) %copy-start.6) | copy-done | bytes 2883608
  74.8 0.8 copy-done.3
  75.6 0.8 copy-done.5
  76.5 1.8 %copy-done.7 = f32[22,2,32,512]{3,2,1,0:T(8,128)S(1)} copy-done((f32[22,2,32,512]{3,2,1,0:T(8,128)S(1)}, f32[22,2,32,512]{3,2,1,0:T(8,128)}, u32[]{:S(2)}) %copy-start.7) | copy-done | bytes 2883608
  78.3 1.3 %sides.1 = (f32[24,8,512]{2,1,0:T(8,128)S(1)}, f32[24,512]{1,0:T(8,128)S(1)}) custom-call(s32[1]{0:T(128)} %bitcast.1.side_ref, bf16[28,32,512]{2,1,0:T(8,128)(2,1)S(1)} %collective-permute-done.near_ref, f32[22,2,32,512]{3,2,1,0:T(8,128)S(1)} %copy-done.7, bf16[128,192]{1,0:T(8,128)(2,1)S(1)} %copy-done.3, bf16[128,192]{1,0:T(8,128)(2,1)S(1)} %copy-done.5, ...), custom_call_target="tpu_custom_call" | custom-call | flops 2147483648 | bytes 4194304 | tf_op jit(solution)/shard_map/sides/pallas_call | solution.py:368
  79.6 0.1 collective-permute-start.1
  79.7 7.2 %outer.1.outer_ref = f32[2,3,16,512]{3,2,1,0:T(8,128)S(1)} custom-call(s32[1]{0:T(128)} %bitcast.1.side_ref, bf16[32,24,16,512]{3,2,1,0:T(8,128)(2,1)} %vol_ref.2, bf16[28,32,512]{2,1,0:T(8,128)(2,1)S(1)} %collective-permute-done.near_ref, bf16[32,16,512]{2,1,0:T(8,128)(2,1)S(1)} %collective-permute-done.2.lo_ref, ...), custom_call_target="tpu_custom_call" | custom-call | flops 1811939328 | bytes 4194304 | tf_op jit(solution)/shard_map/outer/pallas_call | solution.py:455
  86.9 0.4 stats.1
  87.3 16.8 %all_to_all.10.in_ref = f32[8,8,8,128]{3,2,1,0:T(8,128)S(1)} all-to-all(f32[8,8,8,128]{3,2,1,0:T(8,128)S(1)} %stats.1), channel_id=1, replica_groups=mesh['tiles'=2,'disp'=8,'rows'=2] {'disp'}, dimensions={0} | all-to-all | bytes 524288 | tf_op jit(solution)/shard_map/all_to_all | solution.py:580
  104.1 0.1 join.1
  104.1 10.1 %all_to_all.11 = f32[8,8,128]{2,1,0:T(8,128)S(1)} all-to-all(f32[8,8,128]{2,1,0:T(8,128)S(1)} %join.1), channel_id=1, replica_groups=mesh['tiles'=2,'disp'=8,'rows'=2] {'disp'}, dimensions={0} | all-to-all | bytes 65536 | tf_op jit(solution)/shard_map/all_to_all | solution.py:581
  114.2 0.6 copy.11
  (18 shorter events, 0.0 us)
Async XLA Ops:
  0.0 25.8 %copy-start.8 = (f32[32]{0:T(128)S(1)}, f32[32]{0:T(128)}, u32[]{:S(2)}) copy-start(f32[32]{0:T(128)} %param.6) | copy-start | bytes 388
  0.0 25.9 %copy-start.1 = (bf16[27,32]{1,0:T(8,128)(2,1)S(1)}, bf16[27,32]{1,0:T(8,128)(2,1)}, u32[]{:S(2)}) copy-start(bf16[27,32]{1,0:T(8,128)(2,1)} %reg_ref.1) | copy-start | bytes 5188
  0.0 25.9 %copy-start = (bf16[27,32,32]{2,1,0:T(8,128)(2,1)S(1)}, bf16[27,32,32]{2,1,0:T(8,128)(2,1)}, u32[]{:S(2)}) copy-start(bf16[27,32,32]{2,1,0:T(8,128)(2,1)} %conv_ref.1) | copy-start | bytes 165892
  2.3 77.4 %collective-permute-start.2 = (bf16[32,16,512]{2,1,0:T(8,128)(2,1)}, bf16[32,16,512]{2,1,0:T(8,128)(2,1)S(1)}, u32[]{:S(2)}, u32[]{:S(2)}) collective-permute-start(bf16[32,16,512]{2,1,0:T(8,128)(2,1)} %get-tuple-element.37), channel_id=1, source_target_pairs={{0,2},{2,4},{4,6},{6,8},{8,10},{10,12},{12,14},{1,3},{3,5},{5,7},{... | collective-permute-start | bytes 1572872 | tf_op jit(solution)/shard_map/ppermute | solution.py:592
  7.2 72.5 %collective-permute-start.3 = (bf16[32,16,512]{2,1,0:T(8,128)(2,1)}, bf16[32,16,512]{2,1,0:T(8,128)(2,1)S(1)}, u32[]{:S(2)}, u32[]{:S(2)}) collective-permute-start(bf16[32,16,512]{2,1,0:T(8,128)(2,1)} %get-tuple-element.38), channel_id=1, source_target_pairs={{2,0},{4,2},{6,4},{8,6},{10,8},{12,10},{14,12},{3,1},{5,3},{7,5},{... | collective-permute-start | bytes 1572872 | tf_op jit(solution)/shard_map/ppermute | solution.py:597
  19.8 59.8 %collective-permute-start.4 = (bf16[2,32,512]{2,1,0:T(8,128)(2,1)S(1)}, bf16[2,32,512]{2,1,0:T(8,128)(2,1)S(1)}, u32[]{:S(2)}, u32[]{:S(2)}) collective-permute-start(bf16[2,32,512]{2,1,0:T(8,128)(2,1)S(1)} %get-tuple-element.39), channel_id=1, source_target_pairs={{0,3},{1,2},{2,5},{3,4},{4,7},{5,6},{6,9},{7,8},{8,11},{9,10},{10,... | collective-permute-start | bytes 196616 | tf_op jit(solution)/shard_map/ppermute | solution.py:608
  23.2 56.4 %collective-permute-start.5 = (bf16[2,32,512]{2,1,0:T(8,128)(2,1)S(1)}, bf16[2,32,512]{2,1,0:T(8,128)(2,1)S(1)}, u32[]{:S(2)}, u32[]{:S(2)}) collective-permute-start(bf16[2,32,512]{2,1,0:T(8,128)(2,1)S(1)} %get-tuple-element.40), channel_id=1, source_target_pairs={{2,1},{3,0},{4,3},{5,2},{6,5},{7,4},{8,7},{9,6},{10,9},{11,8},{12,... | collective-permute-start | bytes 196616 | tf_op jit(solution)/shard_map/ppermute | solution.py:608
  24.5 50.3 %collective-permute-start = (bf16[28,32,512]{2,1,0:T(8,128)(2,1)}, bf16[28,32,512]{2,1,0:T(8,128)(2,1)S(1)}, u32[]{:S(2)}, u32[]{:S(2)}) collective-permute-start(bf16[28,32,512]{2,1,0:T(8,128)(2,1)} %get-tuple-element.30), channel_id=1, source_target_pairs={{0,1},{1,0},{2,3},{3,2},{4,5},{5,4},{6,7},{7,6},{8,9},{9,8},{10,11... | collective-permute-start | bytes 2752520 | tf_op jit(solution)/shard_map/ppermute | solution.py:587
  27.5 0.6 copy-start.2
  28.2 0.6 copy-start.4
  73.2 1.6 %copy-start.6 = (f32[22,2,32,512]{3,2,1,0:T(8,128)}, f32[22,2,32,512]{3,2,1,0:T(8,128)S(1)}, u32[]{:S(2)}) copy-start(f32[22,2,32,512]{3,2,1,0:T(8,128)S(1)} %get-tuple-element.31.pre_ref) | copy-start | bytes 8650756
  74.8 0.8 copy-start.3
  75.6 0.8 copy-start.5
  76.5 1.8 %copy-start.7 = (f32[22,2,32,512]{3,2,1,0:T(8,128)S(1)}, f32[22,2,32,512]{3,2,1,0:T(8,128)}, u32[]{:S(2)}) copy-start(f32[22,2,32,512]{3,2,1,0:T(8,128)} %copy-done.6) | copy-start | bytes 8650756
  79.6 7.3 %collective-permute-start.1 = (f32[24,512]{1,0:T(8,128)S(1)}, f32[24,512]{1,0:T(8,128)S(1)}, u32[]{:S(2)}, u32[]{:S(2)}) collective-permute-start(f32[24,512]{1,0:T(8,128)S(1)} %get-tuple-element.36), channel_id=1, source_target_pairs={{0,1},{1,0},{2,3},{3,2},{4,5},{5,4},{6,7},{7,6},{8,9},{9,8},{10,11... | collective-permute-start | bytes 147464 | tf_op jit(solution)/shard_map/ppermute | solution.py:587

commit v4 on v3

--- a/solution.py
+++ b/solution.py
@@ -10,10 +10,12 @@
 
 BF16 = jnp.bfloat16
 F32 = jnp.float32
-LANES = 256
-VMEM = pl.BlockSpec(memory_space=pltpu.VMEM)
 SMEM = pl.BlockSpec(memory_space=pltpu.SMEM)
-ROOM = pltpu.CompilerParams(vmem_limit_bytes=48 << 20)
+ROOM = pltpu.CompilerParams(vmem_limit_bytes=32 << 20)
+
+
+def whole(x):
+    return pl.BlockSpec(x.shape, lambda s: (0,) * x.ndim)
 
 SINGLE = (
     (((0, 0, 0, 3), (1, 0, 0, 3), (2, 0, 0, 2)), (0,)),
@@ -48,10 +50,27 @@
     return [[tap(p - q + 2, b, c) for p in range(2) for c in range(3)] for q in range(4)]
 
 
-def pack_kernel(tables, rows, conv_ref, bias_ref, reg_ref, *refs):
+def pick_rows(side, width, rows):
+    ch = width // rows
+    r = lax.broadcasted_iota(jnp.int32, (2 * ch, width), 0)
+    k = lax.broadcasted_iota(jnp.int32, (2 * ch, width), 1)
+    far = jnp.where(r >= ch, 1, 0)
+    row = jnp.where(side == 0, rows - 1 - far, far)
+    return jnp.where(k == (r - ch * far) * rows + row, 1.0, 0.0).astype(BF16)
+
+
+def pack_kernel(tables, rows, side_ref, conv_ref, bias_ref, reg_ref, first_ref, last_ref, *refs):
     ch = conv_ref.shape[1]
     weight_refs = refs[: len(tables)]
-    wide_ref, inner_ref, outer_ref, edges_ref, turn_ref, line_ref, sparse_ref = refs[len(tables) :]
+    (
+        wide_ref, inner_ref, outer_ref, edges_ref, turn_ref, first_rows_ref, last_rows_ref,
+        line_ref, sparse_ref,
+    ) = refs[len(tables) :]
+    pick = pick_rows(side_ref[0], ch * rows, rows)
+    for plane_ref, rows_ref in ((first_ref, first_rows_ref), (last_ref, last_rows_ref)):
+        x = plane_ref[...].reshape(ch * rows, plane_ref.shape[2])
+        y = jnp.dot(pick, x, preferred_element_type=F32)
+        rows_ref[...] = y.astype(BF16).reshape(rows_ref.shape)
     for table, out_ref in zip(tables, weight_refs):
         for m, row in enumerate(table):
             for k, t in enumerate(row):
@@ -94,25 +113,29 @@
         inner_ref[at] = pltpu.roll(x, width - ch, 1)[:, : rows * ch].astype(BF16)
 
 
-def packed(conv_weight, conv_bias, reg_weight, rows, width):
+def packed(side, conv_weight, conv_bias, reg_weight, first, last):
+    rows, width = first.shape[1:]
     ch = conv_weight.shape[1]
     tables = [spread_table(), halo_table(0), halo_table(2), single_table()]
     shapes = [((len(t) * ch, len(t[0]) * ch), BF16) for t in tables]
     shapes += [
         ((ch, width), F32), ((9 * rows, rows * ch), BF16), ((9 * rows, (rows + 2) * ch), BF16),
         ((96, 4 * ch), BF16), ((rows * ch // 2, rows * ch // 2), BF16),
+        ((2, ch, width), BF16), ((2, ch, width), BF16),
     ]
     outs = [jax.ShapeDtypeStruct(*x) for x in shapes]
     line = -(-(rows + 3) * ch // 128) * 128
+    args = conv_weight, conv_bias[:, None], reg_weight, first, last
     return pl.pallas_call(
         functools.partial(pack_kernel, tables, rows),
         name="pack",
+        grid=(1,),
         out_shape=outs,
-        in_specs=[VMEM] * 3,
-        out_specs=[VMEM] * len(outs),
+        in_specs=[SMEM, *map(whole, args)],
+        out_specs=[whole(x) for x in outs],
         scratch_shapes=[pltpu.VMEM((16, line), F32), pltpu.VMEM((96, 4 * ch), F32)],
         compiler_params=ROOM,
-    )(conv_weight, conv_bias[:, None], reg_weight)
+    )(side, *args)
 
 
 def shifted(x, by):
@@ -152,66 +175,8 @@
     taps_ref[slot, pl.ds(row, count), 2 * ch :, :] = shifted(x, -1).reshape(count, ch, width)
 
 
-def edges_kernel(side_ref, vol_ref, near_ref, first_ref, last_ref, pick_ref):
-    s = pl.program_id(0)
-    steps = pl.num_programs(0)
-    ch, _, rows, width = vol_ref.shape
-    planes = 2 * steps
-
-    @pl.when(s == 0)
-    def _():
-        r = lax.broadcasted_iota(jnp.int32, pick_ref.shape, 0)
-        k = lax.broadcasted_iota(jnp.int32, pick_ref.shape, 1)
-        far = jnp.where(r >= ch, 1, 0)
-        row = jnp.where(side_ref[0] == 0, rows - 1 - far, far)
-        pick_ref[...] = jnp.where(k == (r - ch * far) * rows + row, 1.0, 0.0).astype(BF16)
-
-    def rows_of(p, part):
-        x = vol_ref[:, p].reshape(ch * rows, width)
-        w = pick_ref[part * ch : (part + 1) * ch]
-        return jnp.dot(w, x, preferred_element_type=F32).astype(BF16)
-
-    for p in range(2):
-        near_ref[2 * s + p] = rows_of(p, 0)
-
-    @pl.when((s == 0) | (s == steps - 1))
-    def _():
-        for p in range(2):
-            near_ref[planes + p + jnp.where(s == 0, 0, 2)] = rows_of(p, 1)
-
-    @pl.when(s == 0)
-    def _():
-        first_ref[0] = near_ref[0]
-        first_ref[1] = near_ref[planes]
-
-    @pl.when(s == steps - 1)
-    def _():
-        last_ref[0] = near_ref[planes - 1]
-        last_ref[1] = near_ref[planes + 3]
-
-
-def edges(side, volume):
-    ch, planes, rows, width = volume.shape
-    near = jax.ShapeDtypeStruct((planes + 4, ch, width), BF16)
-    corner = jax.ShapeDtypeStruct((2, ch, width), BF16)
-    zero = lambda s: (0, 0, 0)
-    return pl.pallas_call(
-        edges_kernel,
-        name="edges",
-        grid=(planes // 2,),
-        out_shape=(near, corner, corner),
-        in_specs=[SMEM, pl.BlockSpec((ch, 2, rows, width), lambda s: (0, s, 0, 0))],
-        out_specs=[pl.BlockSpec(x.shape, zero) for x in (near, corner, corner)],
-        scratch_shapes=[pltpu.VMEM((2 * ch, ch * rows), BF16)],
-        compiler_params=ROOM,
-        cost_estimate=pl.CostEstimate(
-            flops=1 << 30, bytes_accessed=volume.size * 2, transcendentals=0
-        ),
-    )(side, volume)
-
-
 def inner_kernel(
-    vol_ref, weight_ref, bias_ref, reg_ref, turn_ref, cost_ref, pre_ref,
+    side_ref, vol_ref, weight_ref, bias_ref, reg_ref, turn_ref, cost_ref, pre_ref, near_ref,
     taps_ref, acc_ref, hidden_ref, sums_ref,
 ):
     s = pl.program_id(0)
@@ -229,6 +194,16 @@
             turn(taps_ref, new + p, 0, h * half, block, turn_ref)
         else:
             spread(taps_ref, new + p, (h - 2) * (rows // 2), rows // 2)
+        if h == 2:
+            block = jnp.minimum(s, last - 1)
+            near = jnp.where(side_ref[0] == 0, rows - 1, 0)
+            near_ref[2 * block + p] = taps_ref[new + p, near, ch : 2 * ch, :]
+
+            @pl.when((block == 0) | (block == last - 1))
+            def _():
+                far = jnp.where(side_ref[0] == 0, rows - 2, 1)
+                at = planes + p + jnp.where(block == 0, 0, 2)
+                near_ref[at] = taps_ref[new + p, far, ch : 2 * ch, :]
 
     @pl.when(s == 0)
     def _():
@@ -247,18 +222,16 @@
                 ho0 = 1 if j == 0 else 0
                 ho1 = 3 if j == tiles - 1 else 4
                 w = weight_ref[ho0 * 3 * ch : ho1 * 3 * ch]
-                for n in range(0, width, LANES):
-                    lanes = slice(n, n + LANES)
-                    x = taps_ref[old + p, 2 * j : 2 * j + 2, :, lanes].reshape(6 * ch, LANES)
-                    y = jnp.dot(w, x, preferred_element_type=F32)
-                    for ho in range(ho0, ho1):
-                        for do in range(3):
-                            at = ((ho - ho0) * 3 + do) * ch
-                            part = y[at : at + ch]
-                            fresh = do == 2 and (ho >= 2 or j == 0)
-                            if not fresh:
-                                part = part + acc_ref[slots[do], 2 * j + ho, :, lanes]
-                            acc_ref[slots[do], 2 * j + ho, :, lanes] = part
+                x = taps_ref[old + p, 2 * j : 2 * j + 2].reshape(6 * ch, width)
+                y = jnp.dot(w, x, preferred_element_type=F32)
+                for ho in range(ho0, ho1):
+                    for do in range(3):
+                        at = ((ho - ho0) * 3 + do) * ch
+                        part = y[at : at + ch]
+                        fresh = do == 2 and (ho >= 2 or j == 0)
+                        if not fresh:
+                            part = part + acc_ref[slots[do], 2 * j + ho]
+                        acc_ref[slots[do], 2 * j + ho] = part
                 if (j + 1) * 4 // tiles > j * 4 // tiles:
                     stage(4 * p + j * 4 // tiles)
 
@@ -272,13 +245,11 @@
             for r in range(1, rows - 1):
                 y = jnp.maximum(acc_ref[slot, r + 1] + bias_ref[...], 0.0)
                 hidden_ref[q, r * ch : (r + 1) * ch, :] = y.astype(BF16)
-            for n in range(0, width, LANES):
-                lanes = slice(n, n + LANES)
-                y = jnp.dot(reg_ref[...], hidden_ref[q, :, lanes], preferred_element_type=F32)
-                for a in range(3):
-                    for c in range(3):
-                        at = (a * 3 + c) * rows
-                        sums_ref[c, first + q + 1 - a, :, lanes] += y[at : at + rows]
+            y = jnp.dot(reg_ref[...], hidden_ref[q], preferred_element_type=F32)
+            for a in range(3):
+                for c in range(3):
+                    at = (a * 3 + c) * rows
+                    sums_ref[c, first + q + 1 - a] += y[at : at + rows]
 
     @pl.when(s == last)
     def _():
@@ -289,25 +260,27 @@
         lax.fori_loop(0, planes, finish, 0)
 
 
-def inner(volume, weights, bias, reg, turning):
+def inner(side, volume, weights, bias, reg, turning):
     ch, planes, rows, width = volume.shape
     blocks = planes // 2
-    whole = lambda x: pl.BlockSpec(x.shape, lambda s: (0,) * x.ndim)
     cost = jax.ShapeDtypeStruct((planes, rows, width), F32)
     pre = jax.ShapeDtypeStruct((planes - 2, 2, ch, width), F32)
+    near = jax.ShapeDtypeStruct((planes + 4, ch, width), BF16)
     work = 2 * 27 * ch * ch * planes * rows * width
     return pl.pallas_call(
         inner_kernel,
         name="inner",
         grid=(blocks + 1,),
-        out_shape=(cost, pre),
+        out_shape=(cost, pre, near),
         in_specs=[
+            SMEM,
             pl.BlockSpec((ch, 2, rows, width), lambda s: (0, jnp.minimum(s, blocks - 1), 0, 0)),
             whole(weights), whole(bias), whole(reg), whole(turning),
         ],
         out_specs=(
-            pl.BlockSpec(cost.shape, lambda s: (0, 0, 0)),
+            whole(cost),
             pl.BlockSpec((2, 2, ch, width), lambda s: (jnp.maximum(s - 2, 0), 0, 0, 0)),
+            whole(near),
         ),
         scratch_shapes=[
             pltpu.VMEM((4, rows, 3 * ch, width), BF16),
@@ -319,7 +292,7 @@
         cost_estimate=pl.CostEstimate(
             flops=2 * work, bytes_accessed=volume.size * 2, transcendentals=0
         ),
-    )(volume, weights, bias, reg, turning)
+    )(side, volume, weights, bias, reg, turning)
 
 
 def sides_kernel(
@@ -336,12 +309,10 @@
     for d in range(planes):
         put(taps_ref, d // 2, d % 2, 0, near_ref[d][None])
     for k in range(planes // 2):
-        for n in range(0, width, LANES):
-            lanes = slice(n, n + LANES)
-            x = taps_ref[k, :, :, lanes].reshape(6 * ch, LANES)
-            y = jnp.dot(w, x, preferred_element_type=F32)
-            for q in range(4):
-                acc_ref[2 * k + q, :, lanes] += y[q * ch : (q + 1) * ch]
+        x = taps_ref[k].reshape(6 * ch, width)
+        y = jnp.dot(w, x, preferred_element_type=F32)
+        for q in range(4):
+            acc_ref[2 * k + q] += y[q * ch : (q + 1) * ch]
     for k in range(planes // 2 - 1):
         for p in range(2):
             d = 2 * k + 1 + p
@@ -349,11 +320,9 @@
                 y = pre_ref[d - 1, row] + jnp.where(e == row, acc_ref[d + 1], 0.0)
                 y = jnp.maximum(y + bias_ref[...], 0.0).astype(BF16)
                 hidden_ref[k, (2 * p + row) * ch : (2 * p + row + 1) * ch, :] = y
-        for n in range(0, width, LANES):
-            lanes = slice(n, n + LANES)
-            y = jnp.dot(reg_ref[...], hidden_ref[k, :, lanes], preferred_element_type=F32)
-            for q in range(4):
-                sums_ref[2 * k + q, :, lanes] += y[q * 24 : (q + 1) * 24]
+        y = jnp.dot(reg_ref[...], hidden_ref[k], preferred_element_type=F32)
+        for q in range(4):
+            sums_ref[2 * k + q] += y[q * 24 : (q + 1) * 24]
     for d in range(planes):
         y = sums_ref[d]
         right, left = shifted(y, 1), shifted(y, -1)
@@ -365,15 +334,18 @@
 def sides(side, near, pre, above, below, bias, reg):
     ch, width = near.shape[1:]
     planes = near.shape[0] - 4
+    args = near, pre, above, below, bias, reg
+    outs = (
+        jax.ShapeDtypeStruct((planes, 8, width), F32),
+        jax.ShapeDtypeStruct((planes, width), F32),
+    )
     return pl.pallas_call(
         sides_kernel,
         name="sides",
-        out_shape=(
-            jax.ShapeDtypeStruct((planes, 8, width), F32),
-            jax.ShapeDtypeStruct((planes, width), F32),
-        ),
-        in_specs=[SMEM] + [VMEM] * 6,
-        out_specs=(VMEM, VMEM),
+        grid=(1,),
+        out_shape=outs,
+        in_specs=[SMEM, *map(whole, args)],
+        out_specs=[whole(x) for x in outs],
         scratch_shapes=[
             pltpu.VMEM((planes // 2, 2, 3 * ch, width), BF16),
             pltpu.VMEM((planes + 2, ch, width), F32),
@@ -382,7 +354,7 @@
         ],
         compiler_params=ROOM,
         cost_estimate=pl.CostEstimate(flops=1 << 31, bytes_accessed=1 << 22, transcendentals=0),
-    )(side, near, pre, above, below, bias, reg)
+    )(side, *args)
 
 
 def outer_kernel(
@@ -418,29 +390,25 @@
             spread(taps_ref, slot, 2 + r, rows // 2)
 
     for j in range(rows // 2 + 1):
-        for n in range(0, width, LANES):
-            lanes = slice(n, n + LANES)
-            sums = {}
-            at = 0
-            for blocks, outs in SINGLE:
-                pieces = [
-                    taps_ref[dd, 2 * j + hh, c0 * ch : c1 * ch, lanes] for dd, hh, c0, c1 in blocks
-                ]
-                x = jnp.concatenate(pieces, axis=0)
-                w = weight_ref[at : at + len(outs) * ch, : x.shape[0]]
-                y = jnp.dot(w, x, preferred_element_type=F32)
-                for k, ho in enumerate(outs):
-                    part = y[k * ch : (k + 1) * ch]
-                    sums[ho] = sums[ho] + part if ho in sums else part
-                at += len(outs) * ch
-            for ho, y in sums.items():
-                y = jnp.maximum(y + bias_ref[:, lanes], 0.0)
-                r = 2 * j + ho
-                if r == 0:
-                    y = jnp.where(above, y, 0.0)
-                if r == rows + 1:
-                    y = jnp.where(above, 0.0, y)
-                hidden_ref[r * ch : (r + 1) * ch, lanes] = y.astype(BF16)
+        sums = {}
+        at = 0
+        for blocks, outs in SINGLE:
+            pieces = [taps_ref[dd, 2 * j + hh, c0 * ch : c1 * ch] for dd, hh, c0, c1 in blocks]
+            x = jnp.concatenate(pieces, axis=0)
+            w = weight_ref[at : at + len(outs) * ch, : x.shape[0]]
+            y = jnp.dot(w, x, preferred_element_type=F32)
+            for k, ho in enumerate(outs):
+                part = y[k * ch : (k + 1) * ch]
+                sums[ho] = sums[ho] + part if ho in sums else part
+            at += len(outs) * ch
+        for ho, y in sums.items():
+            y = jnp.maximum(y + bias_ref[...], 0.0)
+            r = 2 * j + ho
+            if r == 0:
+                y = jnp.where(above, y, 0.0)
+            if r == rows + 1:
+                y = jnp.where(above, 0.0, y)
+            hidden_ref[r * ch : (r + 1) * ch] = y.astype(BF16)
     y = jnp.dot(reg_ref[...], hidden_ref[...], preferred_element_type=F32)
     for a in range(3):
         r = [y[(a * 3 + c) * rows : (a * 3 + c + 1) * rows] for c in range(3)]
@@ -449,7 +417,6 @@
 
 def outer(side, volume, near, halos, weights, bias, reg, turning):
     ch, planes, rows, width = volume.shape
-    whole = lambda x: pl.BlockSpec(x.shape, lambda s: (0,) * x.ndim)
     out = jax.ShapeDtypeStruct((2, 3, rows, width), F32)
     work = 2 * 27 * ch * ch * 2 * rows * width
     return pl.pallas_call(
@@ -517,15 +484,18 @@
 
 def stats(first, side, cost, sides_cost, row, outer_cost):
     planes, rows, width = cost.shape
+    args = cost, sides_cost, row, outer_cost
+    out = jax.ShapeDtypeStruct((rows * width // 1024, 8, 8, 128), F32)
     return pl.pallas_call(
         stats_kernel,
         name="stats",
-        out_shape=jax.ShapeDtypeStruct((rows * width // 1024, 8, 8, 128), F32),
-        in_specs=[SMEM, SMEM] + [VMEM] * 4,
-        out_specs=VMEM,
+        grid=(1,),
+        out_shape=out,
+        in_specs=[SMEM, SMEM, *map(whole, args)],
+        out_specs=whole(out),
         scratch_shapes=[pltpu.VMEM((planes, rows, width), F32)],
         compiler_params=ROOM,
-    )(first, side, cost, sides_cost, row, outer_cost)
+    )(first, side, *args)
 
 
 def join_kernel(planes, in_ref, out_ref):
@@ -556,12 +526,14 @@
 
 def join(pieces, planes):
     count, _, rows, width = pieces.shape
+    out = jax.ShapeDtypeStruct((count, rows, width), F32)
     return pl.pallas_call(
         functools.partial(join_kernel, planes),
         name="join",
-        out_shape=jax.ShapeDtypeStruct((count, rows, width), F32),
-        in_specs=[VMEM],
-        out_specs=VMEM,
+        grid=(1,),
+        out_shape=out,
+        in_specs=[whole(pieces)],
+        out_specs=whole(out),
         compiler_params=ROOM,
     )(pieces)
 
@@ -617,15 +589,16 @@
     volume, ends = lax.optimization_barrier((volume, ends))
     lo = up(ends[0], "disp")
     hi = down(ends[1], "disp")
-    near, first_rows, last_rows = edges(side, volume)
-    near = exchange(near, "rows")
+    (
+        spread_w, above, below, single, bias, reg_inner, reg_outer, reg_edges, turning,
+        first_rows, last_rows,
+    ) = packed(side, conv_weight, conv_bias, reg_weight, ends[1], ends[0])
     lo_rows = across(last_rows, 1)
     hi_rows = across(first_rows, -1)
-    spread_w, above, below, single, bias, reg_inner, reg_outer, reg_edges, turning = packed(
-        conv_weight, conv_bias, reg_weight, rows, width
-    )
-
-    cost, pre = inner(volume, spread_w, bias, reg_inner, turning)
+
+    cost, pre, near = inner(side, volume, spread_w, bias, reg_inner, turning)
+    near, lo, hi, lo_rows, hi_rows = lax.optimization_barrier((near, lo, hi, lo_rows, hi_rows))
+    near = exchange(near, "rows")
     sides_cost, send = sides(side, near, pre, above, below, bias, reg_edges)
     row = exchange(send, "rows")
     halos = (lo, hi, lo_rows, hi_rows)

time: 115 us -> 116 us (level)
  Pallas kernels: 66.3 us -> 54.6 us
  local copies, waits for them, and re-layouts: 9.27 us -> 19.7 us
  waiting for transfers between devices: 0.02 us -> 2.32 us
  blocking collectives: 26.8 us -> 25.1 us
  starting transfers between devices: 12.3 us -> 13.5 us
    pallas_call x4 -> x3, Pallas kernels: 13.1 us -> 1.82 us  [the longest x1 1.35 us: sides(): pl.pallas_call(sides_kernel, name='sides', grid=(1,), out_shape=outs, in_...]
    unnamed x19 -> x21, local copies, waits for them, and re-layouts: 6.91 us -> 17.7 us
    ppermute x2, waiting for transfers between devices: 0.01 us -> 2.31 us  [exchange(): lax.ppermute(x, axis, [(0, 1), (1, 0)] if lax.axis_size(axis) == 2 else [])]
    all_to_all x1, blocking collectives: 16.8 us -> 15 us  [joined(): pieces = lax.all_to_all(values, 'disp', 0, 0)]
  transfers between devices with their start and end apart: 6 -> 6, of which waited for: 0 -> 1; matrix products, arithmetic and copies ran while one was open for 0% -> 1% of each run, Pallas kernels for 57% -> 46%
where the time goes in v4:
time: 116 us; the launch traced here: 115 us
  Pallas kernels  54.6 us (47%)
  blocking collectives  25.1 us (22%)
  local copies, waits for them, and re-layouts  19.7 us (17%)
  starting transfers between devices  13.5 us (12%)
  waiting for transfers between devices  2.32 us (2%)
    pallas_call x1, Pallas kernels, inner(): pl.pallas_call(inner_kernel, name='inner', grid=(blocks + 1,), out_shape=...  45.1 us
    unnamed x21, local copies, waits for them, and re-layouts  17.7 us
    all_to_all x1, blocking collectives, joined(): pieces = lax.all_to_all(values, 'disp', 0, 0)  15 us
    all_to_all x1, blocking collectives, joined(): result = lax.all_to_all(join(pieces, planes), 'disp', 0, 0)  10.1 us
    pallas_call x1, Pallas kernels, outer(): pl.pallas_call(outer_kernel, name='outer', grid=(2,), out_shape=out, in_s...  6.04 us
    ppermute x1, starting transfers between devices, up(): return lax.ppermute(x, axis, [(i, i + 1) for i in range(count - 1)])  5.53 us
    ppermute x2, starting transfers between devices, across(): return lax.ppermute(x, ('disp', 'rows'), pairs)  4.95 us
  transfers between devices with their start and end apart: 6, of which 1 were waited for; matrix products, arithmetic and copies ran while one was open for 1% of the time, Pallas kernels for 46%

profile of v4, /device:TPU:0, one launch (start us, length us, event | category | flops | bytes accessed | tf_op | source)
XLA Modules:
  0.0 115.3 jit_solution(4007266787954055837)
XLA Ops:
  0.0 1.3 %slice_bitcast_fusion = (bf16[32,16,512]{2,1,0:T(8,128)(2,1)S(1)}, bf16[32,16,512]{2,1,0:T(8,128)(2,1)S(1)}) fusion(bf16[32,24,16,512]{3,2,1,0:T(8,128)(2,1)} %vol_ref.1), kind=kLoop, calls=%fused_computation | loop fusion | bytes 2097152 | tf_op jit(solution)/shard_map/squeeze | solution.py:588
  1.3 1.3 %collective-permute-start.1 = (bf16[32,16,512]{2,1,0:T(8,128)(2,1)S(1)}, bf16[32,16,512]{2,1,0:T(8,128)(2,1)S(1)}, u32[]{:S(2)}, u32[]{:S(2)}) collective-permute-start(bf16[32,16,512]{2,1,0:T(8,128)(2,1)S(1)} %get-tuple-element.30.first_ref), channel_id=1, source_target_pairs={{2,0},{4,2},{6,4},{8,6},{10,8},{12,10},{14,12},{3,1},{5,3},{7,5},{... | collective-permute-start | bytes 1572872 | tf_op jit(solution)/shard_map/ppermute | solution.py:569
  2.6 5.5 %collective-permute-start = (bf16[32,16,512]{2,1,0:T(8,128)(2,1)S(1)}, bf16[32,16,512]{2,1,0:T(8,128)(2,1)S(1)}, u32[]{:S(2)}, u32[]{:S(2)}) collective-permute-start(bf16[32,16,512]{2,1,0:T(8,128)(2,1)S(1)} %get-tuple-element.31.last_ref), channel_id=1, source_target_pairs={{0,2},{2,4},{4,6},{6,8},{8,10},{10,12},{12,14},{1,3},{3,5},{5,7},{... | collective-permute-start | bytes 1572872 | tf_op jit(solution)/shard_map/ppermute | solution.py:564
  8.1 0.7 copy.7.bias_ref
  8.9 0.9 copy-done.2
  9.8 0.7 copy-done.3
  10.5 1.6 %pack.1 = (bf16[384,192]{1,0:T(8,128)(2,1)S(1)}, bf16[128,192]{1,0:T(8,128)(2,1)S(1)}, bf16[128,192]{1,0:T(8,128)(2,1)S(1)}, bf16[256,256]{1,0:T(8,128)(2,1)S(1)...) custom-call(s32[1]{0:T(128)} %bitcast.1.side_ref, ...), custom_call_target="tpu_custom_call" | custom-call | tf_op jit(solution)/shard_map/pack/pallas_call | solution.py:129
  12.8 0.6 copy-done.6
  13.4 3.7 %collective-permute-start.2 = (bf16[2,32,512]{2,1,0:T(8,128)(2,1)S(1)}, bf16[2,32,512]{2,1,0:T(8,128)(2,1)S(1)}, u32[]{:S(2)}, u32[]{:S(2)}) collective-permute-start(bf16[2,32,512]{2,1,0:T(8,128)(2,1)S(1)} %get-tuple-element.38), channel_id=1, source_target_pairs={{0,3},{1,2},{2,5},{3,4},{4,7},{5,6},{6,9},{7,8},{8,11},{9,10},{10,... | collective-permute-start | bytes 196616 | tf_op jit(solution)/shard_map/ppermute | solution.py:580
  17.1 1.3 %collective-permute-start.3 = (bf16[2,32,512]{2,1,0:T(8,128)(2,1)S(1)}, bf16[2,32,512]{2,1,0:T(8,128)(2,1)S(1)}, u32[]{:S(2)}, u32[]{:S(2)}) collective-permute-start(bf16[2,32,512]{2,1,0:T(8,128)(2,1)S(1)} %get-tuple-element.39), channel_id=1, source_target_pairs={{2,1},{3,0},{4,3},{5,2},{6,5},{7,4},{8,7},{9,6},{10,9},{11,8},{12,... | collective-permute-start | bytes 196616 | tf_op jit(solution)/shard_map/ppermute | solution.py:580
  18.4 4.6 %copy-done = bf16[32,24,16,512]{3,2,1,0:T(8,128)(2,1)S(1)} copy-done((bf16[32,24,16,512]{3,2,1,0:T(8,128)(2,1)S(1)}, bf16[32,24,16,512]{3,2,1,0:T(8,128)(2,1)}, u32[]{:S(2)}) %copy-start) | copy-done | bytes 12582936
  22.9 45.1 %inner.1 = (f32[24,16,512]{2,1,0:T(8,128)S(1)}, f32[22,2,32,512]{3,2,1,0:T(8,128)S(1)}, bf16[28,32,512]{2,1,0:T(8,128)(2,1)}) custom-call(s32[1]{0:T(128)} %bitcast.1.side_ref, bf16[32,24,16,512]{3,2,1,0:T(8,128)(2,1)S(1)} %copy-done, bf16[384,192]{1,0:T(8,128)(2,1)S(1)} %get-tuple-element.32.weight_ref, f32[32,512]{1,0:T(8,128)S(1)} %get-tuple-element.33.bias_ref, ...), custom_call_target="tpu_custom_call" | custom-call | flops 21743271936 | bytes 12582912 | tf_op jit(solution)/shard_map/inner/pallas_call | solution.py:270
  68.0 1.6 %copy-done.8 = f32[22,2,32,512]{3,2,1,0:T(8,128)} copy-done((f32[22,2,32,512]{3,2,1,0:T(8,128)}, f32[22,2,32,512]{3,2,1,0:T(8,128)S(1)}, u32[]{:S(2)}) %copy-start.8) | copy-done | bytes 2883608
  69.6 1.3 %collective-permute-start.4 = (bf16[28,32,512]{2,1,0:T(8,128)(2,1)}, bf16[28,32,512]{2,1,0:T(8,128)(2,1)S(1)}, u32[]{:S(2)}, u32[]{:S(2)}) collective-permute-start(bf16[28,32,512]{2,1,0:T(8,128)(2,1)} %get-tuple-element.40), channel_id=1, source_target_pairs={{0,1},{1,0},{2,3},{3,2},{4,5},{5,4},{6,7},{7,6},{8,9},{9,8},{10,11... | collective-permute-start | bytes 2752520 | tf_op jit(solution)/shard_map/ppermute | solution.py:559
  70.9 2.3 %collective-permute-done.4.near_ref = bf16[28,32,512]{2,1,0:T(8,128)(2,1)S(1)} collective-permute-done((bf16[28,32,512]{2,1,0:T(8,128)(2,1)}, bf16[28,32,512]{2,1,0:T(8,128)(2,1)S(1)}, u32[]{:S(2)}, u32[]{:S(2)}) %collective-permute-start.4) | collective-permute-done | bytes 917536 | tf_op jit(solution)/shard_map/ppermute | solution.py:559
  73.2 0.8 copy-done.5
  74.0 0.8 copy-done.7
  74.9 1.8 %copy-done.9 = f32[22,2,32,512]{3,2,1,0:T(8,128)S(1)} copy-done((f32[22,2,32,512]{3,2,1,0:T(8,128)S(1)}, f32[22,2,32,512]{3,2,1,0:T(8,128)}, u32[]{:S(2)}) %copy-start.9) | copy-done | bytes 2883608
  76.7 1.3 %sides.1 = (f32[24,8,512]{2,1,0:T(8,128)S(1)}, f32[24,512]{1,0:T(8,128)S(1)}) custom-call(s32[1]{0:T(128)} %bitcast.1.side_ref, bf16[28,32,512]{2,1,0:T(8,128)(2,1)S(1)} %collective-permute-done.4.near_ref, f32[22,2,32,512]{3,2,1,0:T(8,128)S(1)} %copy-done.9, bf16[128,192]{1,0:T(8,128)(2,1)S(1)} %copy-done.5, bf16[128,192]{1,0:T(8,128)(2,1)S(1)} %copy-done.7, ...), custom_call_target="tpu_custom_call" | custom-call | flops 2147483648 | bytes 4194304 | tf_op jit(solution)/shard_map/sides/pallas_call | solution.py:342
  78.5 4.6 %copy-done.1 = bf16[32,24,16,512]{3,2,1,0:T(8,128)(2,1)S(1)} copy-done((bf16[32,24,16,512]{3,2,1,0:T(8,128)(2,1)S(1)}, bf16[32,24,16,512]{3,2,1,0:T(8,128)(2,1)}, u32[]{:S(2)}) %copy-start.1) | copy-done | bytes 12582936
  83.1 6.0 %outer.1.outer_ref = f32[2,3,16,512]{3,2,1,0:T(8,128)S(1)} custom-call(s32[1]{0:T(128)} %bitcast.1.side_ref, bf16[32,24,16,512]{3,2,1,0:T(8,128)(2,1)S(1)} %copy-done.1, bf16[28,32,512]{2,1,0:T(8,128)(2,1)S(1)} %collective-permute-done.4.near_ref, bf16[32,16,512]{2,1,0:T(8,128)(2,1)S(1)} %collective-permute-done.lo_ref, ...), custom_call_target="tpu_custom_call" | custom-call | flops 1811939328 | bytes 4194304 | tf_op jit(solution)/shard_map/outer/pallas_call | solution.py:422
  89.6 15.0 %all_to_all.10.in_ref = f32[8,8,8,128]{3,2,1,0:T(8,128)S(1)} all-to-all(f32[8,8,8,128]{3,2,1,0:T(8,128)S(1)} %stats.1), channel_id=1, replica_groups=mesh['tiles'=2,'disp'=8,'rows'=2] {'disp'}, dimensions={0} | all-to-all | bytes 524288 | tf_op jit(solution)/shard_map/all_to_all | solution.py:552
  104.6 10.1 %all_to_all.11 = f32[8,8,128]{2,1,0:T(8,128)S(1)} all-to-all(f32[8,8,128]{2,1,0:T(8,128)S(1)} %join.1), channel_id=1, replica_groups=mesh['tiles'=2,'disp'=8,'rows'=2] {'disp'}, dimensions={0} | all-to-all | bytes 65536 | tf_op jit(solution)/shard_map/all_to_all | solution.py:553
  114.7 0.6 copy.11
  (19 shorter events, 1.6 us)
Async XLA Ops:
  1.3 68.3 %collective-permute-start.1 = (bf16[32,16,512]{2,1,0:T(8,128)(2,1)S(1)}, bf16[32,16,512]{2,1,0:T(8,128)(2,1)S(1)}, u32[]{:S(2)}, u32[]{:S(2)}) collective-permute-start(bf16[32,16,512]{2,1,0:T(8,128)(2,1)S(1)} %get-tuple-element.30.first_ref), channel_id=1, source_target_pairs={{2,0},{4,2},{6,4},{8,6},{10,8},{12,10},{14,12},{3,1},{5,3},{7,5},{... | collective-permute-start | bytes 1572872 | tf_op jit(solution)/shard_map/ppermute | solution.py:569
  2.6 67.0 %collective-permute-start = (bf16[32,16,512]{2,1,0:T(8,128)(2,1)S(1)}, bf16[32,16,512]{2,1,0:T(8,128)(2,1)S(1)}, u32[]{:S(2)}, u32[]{:S(2)}) collective-permute-start(bf16[32,16,512]{2,1,0:T(8,128)(2,1)S(1)} %get-tuple-element.31.last_ref), channel_id=1, source_target_pairs={{0,2},{2,4},{4,6},{6,8},{8,10},{10,12},{12,14},{1,3},{3,5},{5,7},{... | collective-permute-start | bytes 1572872 | tf_op jit(solution)/shard_map/ppermute | solution.py:564
  8.9 0.9 copy-start.2
  9.8 0.7 copy-start.3
  12.1 0.6 copy-start.4
  12.8 0.6 copy-start.6
  13.4 56.2 %collective-permute-start.2 = (bf16[2,32,512]{2,1,0:T(8,128)(2,1)S(1)}, bf16[2,32,512]{2,1,0:T(8,128)(2,1)S(1)}, u32[]{:S(2)}, u32[]{:S(2)}) collective-permute-start(bf16[2,32,512]{2,1,0:T(8,128)(2,1)S(1)} %get-tuple-element.38), channel_id=1, source_target_pairs={{0,3},{1,2},{2,5},{3,4},{4,7},{5,6},{6,9},{7,8},{8,11},{9,10},{10,... | collective-permute-start | bytes 196616 | tf_op jit(solution)/shard_map/ppermute | solution.py:580
  17.1 52.5 %collective-permute-start.3 = (bf16[2,32,512]{2,1,0:T(8,128)(2,1)S(1)}, bf16[2,32,512]{2,1,0:T(8,128)(2,1)S(1)}, u32[]{:S(2)}, u32[]{:S(2)}) collective-permute-start(bf16[2,32,512]{2,1,0:T(8,128)(2,1)S(1)} %get-tuple-element.39), channel_id=1, source_target_pairs={{2,1},{3,0},{4,3},{5,2},{6,5},{7,4},{8,7},{9,6},{10,9},{11,8},{12,... | collective-permute-start | bytes 196616 | tf_op jit(solution)/shard_map/ppermute | solution.py:580
  18.4 4.6 %copy-start = (bf16[32,24,16,512]{3,2,1,0:T(8,128)(2,1)S(1)}, bf16[32,24,16,512]{3,2,1,0:T(8,128)(2,1)}, u32[]{:S(2)}) copy-start(bf16[32,24,16,512]{3,2,1,0:T(8,128)(2,1)} %vol_ref.1) | copy-start | bytes 37748740
  68.0 1.6 %copy-start.8 = (f32[22,2,32,512]{3,2,1,0:T(8,128)}, f32[22,2,32,512]{3,2,1,0:T(8,128)S(1)}, u32[]{:S(2)}) copy-start(f32[22,2,32,512]{3,2,1,0:T(8,128)S(1)} %get-tuple-element.41.pre_ref) | copy-start | bytes 8650756
  69.6 3.6 %collective-permute-start.4 = (bf16[28,32,512]{2,1,0:T(8,128)(2,1)}, bf16[28,32,512]{2,1,0:T(8,128)(2,1)S(1)}, u32[]{:S(2)}, u32[]{:S(2)}) collective-permute-start(bf16[28,32,512]{2,1,0:T(8,128)(2,1)} %get-tuple-element.40), channel_id=1, source_target_pairs={{0,1},{1,0},{2,3},{3,2},{4,5},{5,4},{6,7},{7,6},{8,9},{9,8},{10,11... | collective-permute-start | bytes 2752520 | tf_op jit(solution)/shard_map/ppermute | solution.py:559
  73.2 0.8 copy-start.5
  74.0 0.8 copy-start.7
  74.9 1.8 %copy-start.9 = (f32[22,2,32,512]{3,2,1,0:T(8,128)S(1)}, f32[22,2,32,512]{3,2,1,0:T(8,128)}, u32[]{:S(2)}) copy-start(f32[22,2,32,512]{3,2,1,0:T(8,128)} %copy-done.8) | copy-start | bytes 8650756
  78.0 11.1 %collective-permute-start.5 = (f32[24,512]{1,0:T(8,128)S(1)}, f32[24,512]{1,0:T(8,128)S(1)}, u32[]{:S(2)}, u32[]{:S(2)}) collective-permute-start(f32[24,512]{1,0:T(8,128)S(1)} %get-tuple-element.46), channel_id=1, source_target_pairs={{0,1},{1,0},{2,3},{3,2},{4,5},{5,4},{6,7},{7,6},{8,9},{9,8},{10,11... | collective-permute-start | bytes 147464 | tf_op jit(solution)/shard_map/ppermute | solution.py:559
  78.5 4.6 %copy-start.1 = (bf16[32,24,16,512]{3,2,1,0:T(8,128)(2,1)S(1)}, bf16[32,24,16,512]{3,2,1,0:T(8,128)(2,1)}, u32[]{:S(2)}) copy-start(bf16[32,24,16,512]{3,2,1,0:T(8,128)(2,1)} %vol_ref.1) | copy-start | bytes 37748740

commit v5 on v4

--- a/solution.py
+++ b/solution.py
@@ -11,7 +11,7 @@
 BF16 = jnp.bfloat16
 F32 = jnp.float32
 SMEM = pl.BlockSpec(memory_space=pltpu.SMEM)
-ROOM = pltpu.CompilerParams(vmem_limit_bytes=32 << 20)
+ROOM = pltpu.CompilerParams(vmem_limit_bytes=56 << 20)
 
 
 def whole(x):
@@ -39,11 +39,41 @@
     return table
 
 
-def spread_table():
-    return [
-        [tap(2 - do, hi - ho + 2, c) for hi in range(2) for c in range(3)]
-        for ho in range(4) for do in range(3)
-    ]
+def table_of(tiles):
+    table = []
+    for blocks, outs in tiles:
+        for do, ho in outs:
+            table.append(
+                [tap(dd - do, hh - ho, c) for dd, hh, c0, c1 in blocks for c in range(c0, c1)]
+            )
+    return table
+
+
+CENTER = (
+    (
+        ((1, 1, 0, 3), (1, 2, 0, 3), (0, 0, 2, 3), (0, 3, 2, 3))
+        + ((2, 1, 0, 3), (2, 2, 0, 3), (3, 3, 2, 3), (3, 0, 2, 3)),
+        ((0, 0), (0, 1), (1, 0), (1, 1)),
+    ),
+)
+RIM = (
+    (((0, 1, 0, 3), (0, 2, 0, 3), (0, 0, 0, 2)), ((0, 0), (0, 1))),
+    (((3, 1, 0, 3), (3, 2, 0, 3), (3, 3, 0, 2)), ((1, 0), (1, 1))),
+    (((1, 0, 0, 3), (2, 0, 0, 3), (3, 0, 0, 2)), ((0, 0), (1, 0))),
+    (((1, 3, 0, 3), (2, 3, 0, 3), (0, 3, 0, 2)), ((0, 1), (1, 1))),
+)
+
+
+def side_tiles(out):
+    first, second = (0, out), (1, out)
+    return (
+        (
+            ((1, 0, 0, 3), (1, 1, 0, 3), (0, 0, 0, 2))
+            + ((2, 0, 0, 3), (2, 1, 0, 3), (3, 0, 0, 2))
+            + ((0, 0, 2, 3), (0, 1, 0, 3), (3, 0, 2, 3), (3, 1, 0, 3)),
+            (first, second),
+        ),
+    )
 
 
 def halo_table(b):
@@ -116,7 +146,8 @@
 def packed(side, conv_weight, conv_bias, reg_weight, first, last):
     rows, width = first.shape[1:]
     ch = conv_weight.shape[1]
-    tables = [spread_table(), halo_table(0), halo_table(2), single_table()]
+    tables = [table_of(CENTER), table_of(RIM), table_of(side_tiles(-1)), table_of(side_tiles(0))]
+    tables += [halo_table(0), halo_table(2), single_table()]
     shapes = [((len(t) * ch, len(t[0]) * ch), BF16) for t in tables]
     shapes += [
         ((ch, width), F32), ((9 * rows, rows * ch), BF16), ((9 * rows, (rows + 2) * ch), BF16),
@@ -176,91 +207,110 @@
 
 
 def inner_kernel(
-    side_ref, vol_ref, weight_ref, bias_ref, reg_ref, turn_ref, cost_ref, pre_ref, near_ref,
-    taps_ref, acc_ref, hidden_ref, sums_ref,
+    side_ref, vol_ref, center_ref, rim_ref, top_ref, bottom_ref, bias_ref, reg_ref, turn_ref,
+    cost_ref, pre_ref, near_ref, taps0, taps1, taps2, hidden0, hidden1, hidden2, sums_ref,
 ):
+    taps = taps0, taps1, taps2
+    hidden = hidden0, hidden1, hidden2
     s = pl.program_id(0)
-    last = pl.num_programs(0) - 1
     ch, _, rows, width = vol_ref.shape
     planes = cost_ref.shape[0]
+    blocks = planes // 2
     half = ch // 2
-    new = (s % 2) * 2
-    old = ((s + 1) % 2) * 2
-
-    def stage(part):
+
+    def stage(new, part):
         p, h = part // 4, part % 4
         if h < 2:
-            block = vol_ref[h * half : (h + 1) * half, p]
-            turn(taps_ref, new + p, 0, h * half, block, turn_ref)
+            turn(new, p, 0, h * half, vol_ref[h * half : (h + 1) * half, p], turn_ref)
         else:
-            spread(taps_ref, new + p, (h - 2) * (rows // 2), rows // 2)
+            spread(new, p, (h - 2) * (rows // 2), rows // 2)
         if h == 2:
-            block = jnp.minimum(s, last - 1)
+            block = jnp.minimum(s, blocks - 1)
             near = jnp.where(side_ref[0] == 0, rows - 1, 0)
-            near_ref[2 * block + p] = taps_ref[new + p, near, ch : 2 * ch, :]
-
-            @pl.when((block == 0) | (block == last - 1))
+            near_ref[2 * block + p] = new[p, near, ch : 2 * ch, :]
+
+            @pl.when((block == 0) | (block == blocks - 1))
             def _():
                 far = jnp.where(side_ref[0] == 0, rows - 2, 1)
                 at = planes + p + jnp.where(block == 0, 0, 2)
-                near_ref[at] = taps_ref[new + p, far, ch : 2 * ch, :]
+                near_ref[at] = new[p, far, ch : 2 * ch, :]
+
+    def patch(old, mid, row, groups):
+        sums = {}
+        four = (old, 0), (old, 1), (mid, 0), (mid, 1)
+        for tiles, w_ref in groups:
+            at = 0
+            for parts, outs in tiles:
+                pieces = []
+                for dd, hh, c0, c1 in parts:
+                    ref, p = four[dd]
+                    pieces.append(ref[p, row + hh, c0 * ch : c1 * ch, :])
+                x = jnp.concatenate(pieces, axis=0)
+                w = w_ref[at : at + len(outs) * ch]
+                y = jnp.dot(w, x, preferred_element_type=F32)
+                for k, out in enumerate(outs):
+                    part = y[k * ch : (k + 1) * ch]
+                    sums[out] = sums[out] + part if out in sums else part
+                at += len(outs) * ch
+        return sums
+
+    def regress(old, q):
+        first = 2 * (s - 3) + 1
+        y = jnp.dot(reg_ref[...], old[q], preferred_element_type=F32)
+        for a in range(3):
+            for c in range(3):
+                at = (a * 3 + c) * rows
+                sums_ref[c, first + q + 3 - a] += y[at : at + rows]
 
     @pl.when(s == 0)
     def _():
         for part in range(8):
-            stage(part)
+            stage(taps0, part)
         sums_ref[...] = jnp.zeros_like(sums_ref)
-        hidden_ref[...] = jnp.zeros_like(hidden_ref)
-
-    @pl.when(s >= 1)
+        for ref in hidden:
+            ref[...] = jnp.zeros_like(ref)
+
+    @pl.when(s == 1)
     def _():
-        base = 2 * (s - 1) + 3
-        tiles = rows // 2
-        for p in range(2):
-            slots = [(base + p + do) % 4 for do in range(3)]
-            for j in range(tiles):
-                ho0 = 1 if j == 0 else 0
-                ho1 = 3 if j == tiles - 1 else 4
-                w = weight_ref[ho0 * 3 * ch : ho1 * 3 * ch]
-                x = taps_ref[old + p, 2 * j : 2 * j + 2].reshape(6 * ch, width)
-                y = jnp.dot(w, x, preferred_element_type=F32)
-                for ho in range(ho0, ho1):
-                    for do in range(3):
-                        at = ((ho - ho0) * 3 + do) * ch
-                        part = y[at : at + ch]
-                        fresh = do == 2 and (ho >= 2 or j == 0)
-                        if not fresh:
-                            part = part + acc_ref[slots[do], 2 * j + ho]
-                        acc_ref[slots[do], 2 * j + ho] = part
-                if (j + 1) * 4 // tiles > j * 4 // tiles:
-                    stage(4 * p + j * 4 // tiles)
-
-    @pl.when(s >= 2)
+        for part in range(8):
+            stage(taps1, part)
+
+    for r in range(3):
+        @pl.when((s >= 2) & (s <= blocks) & (s % 3 == r))
+        def _(r=r):
+            new, mid, old = taps[r], taps[(r + 2) % 3], taps[(r + 1) % 3]
+            hidden_new, hidden_old = hidden[r], hidden[(r + 2) % 3]
+            patches = rows // 2 - 1
+            part = 0
+            for j in range(patches):
+                sums = patch(old, mid, 2 * j, ((CENTER, center_ref), (RIM, rim_ref)))
+                for (do, ho), y in sums.items():
+                    at = (2 * j + 1 + ho) * ch
+                    y = jnp.maximum(y + bias_ref[...], 0.0).astype(BF16)
+                    hidden_new[do, at : at + ch, :] = y
+                while part * patches < 8 * (j + 1) and part < 8:
+                    stage(new, part)
+                    part += 1
+                if j in (1, 2):
+                    regress(hidden_old, j - 1)
+            for e, (row, w_ref) in enumerate(((0, top_ref), (rows - 2, bottom_ref))):
+                for (do, _), y in patch(old, mid, row, ((side_tiles(e - 1), w_ref),)).items():
+                    pre_ref[do, e] = y
+
+    @pl.when(s == blocks + 1)
     def _():
-        first = 2 * (s - 1) - 1
         for q in range(2):
-            slot = (first + q) % 4
-            pre_ref[q, 0] = acc_ref[slot, 1]
-            pre_ref[q, 1] = acc_ref[slot, rows]
-            for r in range(1, rows - 1):
-                y = jnp.maximum(acc_ref[slot, r + 1] + bias_ref[...], 0.0)
-                hidden_ref[q, r * ch : (r + 1) * ch, :] = y.astype(BF16)
-            y = jnp.dot(reg_ref[...], hidden_ref[q], preferred_element_type=F32)
-            for a in range(3):
-                for c in range(3):
-                    at = (a * 3 + c) * rows
-                    sums_ref[c, first + q + 1 - a] += y[at : at + rows]
-
-    @pl.when(s == last)
-    def _():
+            regress(hidden[blocks % 3], q)
+
         def finish(d, carry):
-            cost_ref[d] = shifted(sums_ref[0, d], 1) + sums_ref[1, d] + shifted(sums_ref[2, d], -1)
+            right, left = shifted(sums_ref[0, d + 2], 1), shifted(sums_ref[2, d + 2], -1)
+            cost_ref[d] = right + sums_ref[1, d + 2] + left
             return carry
 
         lax.fori_loop(0, planes, finish, 0)
 
 
-def inner(side, volume, weights, bias, reg, turning):
+def inner(side, volume, *rest):
     ch, planes, rows, width = volume.shape
     blocks = planes // 2
     cost = jax.ShapeDtypeStruct((planes, rows, width), F32)
@@ -270,29 +320,28 @@
     return pl.pallas_call(
         inner_kernel,
         name="inner",
-        grid=(blocks + 1,),
+        grid=(blocks + 2,),
         out_shape=(cost, pre, near),
         in_specs=[
             SMEM,
             pl.BlockSpec((ch, 2, rows, width), lambda s: (0, jnp.minimum(s, blocks - 1), 0, 0)),
-            whole(weights), whole(bias), whole(reg), whole(turning),
+            *map(whole, rest),
         ],
         out_specs=(
             whole(cost),
-            pl.BlockSpec((2, 2, ch, width), lambda s: (jnp.maximum(s - 2, 0), 0, 0, 0)),
+            pl.BlockSpec(
+                (2, 2, ch, width), lambda s: (jnp.clip(s - 2, 0, blocks - 2), 0, 0, 0)
+            ),
             whole(near),
         ),
-        scratch_shapes=[
-            pltpu.VMEM((4, rows, 3 * ch, width), BF16),
-            pltpu.VMEM((4, rows + 2, ch, width), F32),
-            pltpu.VMEM((2, rows * ch, width), BF16),
-            pltpu.VMEM((3, planes, rows, width), F32),
-        ],
+        scratch_shapes=[pltpu.VMEM((2, rows, 3 * ch, width), BF16)] * 3
+        + [pltpu.VMEM((2, rows * ch, width), BF16)] * 3
+        + [pltpu.VMEM((3, planes + 4, rows, width), F32)],
         compiler_params=ROOM,
         cost_estimate=pl.CostEstimate(
             flops=2 * work, bytes_accessed=volume.size * 2, transcendentals=0
         ),
-    )(side, volume, weights, bias, reg, turning)
+    )(side, volume, *rest)
 
 
 def sides_kernel(
@@ -590,13 +639,15 @@
     lo = up(ends[0], "disp")
     hi = down(ends[1], "disp")
     (
-        spread_w, above, below, single, bias, reg_inner, reg_outer, reg_edges, turning,
+        center, rim, top, bottom, above, below, single, bias, reg_inner, reg_outer, reg_edges, turning,
         first_rows, last_rows,
     ) = packed(side, conv_weight, conv_bias, reg_weight, ends[1], ends[0])
     lo_rows = across(last_rows, 1)
     hi_rows = across(first_rows, -1)
 
-    cost, pre, near = inner(side, volume, spread_w, bias, reg_inner, turning)
+    cost, pre, near = inner(
+        side, volume, center, rim, top, bottom, bias, reg_inner, turning
+    )
     near, lo, hi, lo_rows, hi_rows = lax.optimization_barrier((near, lo, hi, lo_rows, hi_rows))
     near = exchange(near, "rows")
     sides_cost, send = sides(side, near, pre, above, below, bias, reg_edges)

time: 116 us -> 109 us (0.940)
  local copies, waits for them, and re-layouts: 19.7 us -> 4.79 us
  Pallas kernels: 54.6 us -> 62.4 us
    unnamed x21 -> x17, local copies, waits for them, and re-layouts: 17.7 us -> 2.18 us
    pallas_call x1, Pallas kernels: 45.1 us -> 41.5 us  [inner(): pl.pallas_call(inner_kernel, name='inner', grid=(blocks + 2,), out_shape=...]
    pallas_call x1, Pallas kernels: 1.35 us -> 4.05 us  [sides(): pl.pallas_call(sides_kernel, name='sides', grid=(1,), out_shape=outs, in_...]
    pallas_call x1, Pallas kernels: 6.04 us -> 8.69 us  [outer(): pl.pallas_call(outer_kernel, name='outer', grid=(2,), out_shape=out, in_s...]
    pallas_call x1, Pallas kernels: 1.64 us -> 4.21 us  [packed(): pl.pallas_call(functools.partial(pack_kernel, tables, rows), name='pack',...]
    pallas_call x1, Pallas kernels: 0.42 us -> 2.41 us  [stats(): pl.pallas_call(stats_kernel, name='stats', grid=(1,), out_shape=out, in_s...]
    pallas_call x1, Pallas kernels: 0.05 us -> 1.62 us  [join(): pl.pallas_call(functools.partial(join_kernel, planes), name='join', grid=...]
  transfers between devices with their start and end apart: 6 -> 6, of which waited for: 1 -> 1; matrix products, arithmetic and copies ran while one was open for 1% -> 1% of each run, Pallas kernels for 46% -> 50%
where the time goes in v5:
time: 109 us
  Pallas kernels  62.4 us (57%)
  blocking collectives  25.7 us (24%)
  starting transfers between devices  13.4 us (12%)
  local copies, waits for them, and re-layouts  4.79 us (4%)
  waiting for transfers between devices  2.32 us (2%)
    pallas_call x1, Pallas kernels, inner(): pl.pallas_call(inner_kernel, name='inner', grid=(blocks + 2,), out_shape=...  41.5 us
    all_to_all x1, blocking collectives, joined(): pieces = lax.all_to_all(values, 'disp', 0, 0)  15.4 us
    all_to_all x1, blocking collectives, joined(): result = lax.all_to_all(join(pieces, planes), 'disp', 0, 0)  10.3 us
    pallas_call x1, Pallas kernels, outer(): pl.pallas_call(outer_kernel, name='outer', grid=(2,), out_shape=out, in_s...  8.69 us
    ppermute x1, starting transfers between devices, up(): return lax.ppermute(x, axis, [(i, i + 1) for i in range(count - 1)])  5.53 us
    ppermute x2, starting transfers between devices, across(): return lax.ppermute(x, ('disp', 'rows'), pairs)  4.97 us
    pallas_call x1, Pallas kernels, packed(): pl.pallas_call(functools.partial(pack_kernel, tables, rows), name='pack',...  4.21 us
    pallas_call x1, Pallas kernels, sides(): pl.pallas_call(sides_kernel, name='sides', grid=(1,), out_shape=outs, in_...  4.05 us
  transfers between devices with their start and end apart: 6, of which 1 were waited for; matrix products, arithmetic and copies ran while one was open for 1% of the time, Pallas kernels for 50%

profile of v5, /device:TPU:0, one launch (start us, length us, event | category | flops | bytes accessed | tf_op | source)
XLA Modules:
  0.0 108.7 jit_solution(12593462011337942753)
XLA Ops:
  0.0 1.3 %slice_bitcast_fusion = (bf16[32,16,512]{2,1,0:T(8,128)(2,1)S(1)}, bf16[32,16,512]{2,1,0:T(8,128)(2,1)S(1)}) fusion(bf16[32,24,16,512]{3,2,1,0:T(8,128)(2,1)} %vol_ref.1), kind=kLoop, calls=%fused_computation | loop fusion | bytes 2097152 | tf_op jit(solution)/shard_map/squeeze | solution.py:637
  1.3 1.3 %collective-permute-start.1 = (bf16[32,16,512]{2,1,0:T(8,128)(2,1)S(1)}, bf16[32,16,512]{2,1,0:T(8,128)(2,1)S(1)}, u32[]{:S(2)}, u32[]{:S(2)}) collective-permute-start(bf16[32,16,512]{2,1,0:T(8,128)(2,1)S(1)} %get-tuple-element.33.first_ref), channel_id=1, source_target_pairs={{2,0},{4,2},{6,4},{8,6},{10,8},{12,10},{14,12},{3,1},{5,3},{7,5},{... | collective-permute-start | bytes 1572872 | tf_op jit(solution)/shard_map/ppermute | solution.py:618
  2.6 5.5 %collective-permute-start = (bf16[32,16,512]{2,1,0:T(8,128)(2,1)S(1)}, bf16[32,16,512]{2,1,0:T(8,128)(2,1)S(1)}, u32[]{:S(2)}, u32[]{:S(2)}) collective-permute-start(bf16[32,16,512]{2,1,0:T(8,128)(2,1)S(1)} %get-tuple-element.34.last_ref), channel_id=1, source_target_pairs={{0,2},{2,4},{4,6},{6,8},{8,10},{10,12},{12,14},{1,3},{3,5},{5,7},{... | collective-permute-start | bytes 1572872 | tf_op jit(solution)/shard_map/ppermute | solution.py:613
  8.1 1.3 %copy.7.bias_ref = f32[32,1]{1,0:T(8,128)} copy(f32[32,1]{0,1:T(1,128)} %bitcast.17) | data formatting | bytes 256 | tf_op jit(solution)/shard_map/broadcast_in_dim | solution.py:159
  9.5 4.2 %pack.1 = (bf16[128,512]{1,0:T(8,128)(2,1)}, bf16[256,256]{1,0:T(8,128)(2,1)}, bf16[64,768]{1,0:T(8,128)(2,1)}, bf16[64,768]{1,0:T(8,128)(2,1)}, bf16[128,192]{1...) custom-call(s32[1]{0:T(128)} %bitcast.1.side_ref, ...), custom_call_target="tpu_custom_call" | custom-call | tf_op jit(solution)/shard_map/pack/pallas_call | solution.py:160
  13.7 3.7 %collective-permute-start.2 = (bf16[2,32,512]{2,1,0:T(8,128)(2,1)}, bf16[2,32,512]{2,1,0:T(8,128)(2,1)S(1)}, u32[]{:S(2)}, u32[]{:S(2)}) collective-permute-start(bf16[2,32,512]{2,1,0:T(8,128)(2,1)} %get-tuple-element.44), channel_id=1, source_target_pairs={{0,3},{1,2},{2,5},{3,4},{4,7},{5,6},{6,9},{7,8},{8,11},{9,10},{10,... | collective-permute-start | bytes 196616 | tf_op jit(solution)/shard_map/ppermute | solution.py:629
  17.4 1.3 %collective-permute-start.3 = (bf16[2,32,512]{2,1,0:T(8,128)(2,1)}, bf16[2,32,512]{2,1,0:T(8,128)(2,1)S(1)}, u32[]{:S(2)}, u32[]{:S(2)}) collective-permute-start(bf16[2,32,512]{2,1,0:T(8,128)(2,1)} %get-tuple-element.45), channel_id=1, source_target_pairs={{2,1},{3,0},{4,3},{5,2},{6,5},{7,4},{8,7},{9,6},{10,9},{11,8},{12,... | collective-permute-start | bytes 196616 | tf_op jit(solution)/shard_map/ppermute | solution.py:629
  18.7 41.5 %inner.1 = (f32[24,16,512]{2,1,0:T(8,128)}, f32[22,2,32,512]{3,2,1,0:T(8,128)}, bf16[28,32,512]{2,1,0:T(8,128)(2,1)}) custom-call(s32[1]{0:T(128)} %bitcast.1.side_ref, bf16[32,24,16,512]{3,2,1,0:T(8,128)(2,1)} %vol_ref.1, bf16[128,512]{1,0:T(8,128)(2,1)} %get-tuple-element.35.center_ref, bf16[256,256]{1,0:T(8,128)(2,1)} %get-tuple-element.36.rim_ref, ...), custom_call_target="tpu_custom_call" | custom-call | flops 21743271936 | bytes 12582912 | tf_op jit(solution)/shard_map/inner/pallas_call | solution.py:320
  60.1 0.0 collective-permute-done.2.lo_rows_ref
  60.2 0.0 collective-permute-done.3.hi_rows_ref
  60.2 0.0 collective-permute-done.1.hi_ref
  60.2 1.2 %collective-permute-start.4 = (bf16[28,32,512]{2,1,0:T(8,128)(2,1)}, bf16[28,32,512]{2,1,0:T(8,128)(2,1)S(1)}, u32[]{:S(2)}, u32[]{:S(2)}) collective-permute-start(bf16[28,32,512]{2,1,0:T(8,128)(2,1)} %get-tuple-element.46), channel_id=1, source_target_pairs={{0,1},{1,0},{2,3},{3,2},{4,5},{5,4},{6,7},{7,6},{8,9},{9,8},{10,11... | collective-permute-start | bytes 2752520 | tf_op jit(solution)/shard_map/ppermute | solution.py:608
  61.4 2.3 %collective-permute-done.4.near_ref = bf16[28,32,512]{2,1,0:T(8,128)(2,1)S(1)} collective-permute-done((bf16[28,32,512]{2,1,0:T(8,128)(2,1)}, bf16[28,32,512]{2,1,0:T(8,128)(2,1)S(1)}, u32[]{:S(2)}, u32[]{:S(2)}) %collective-permute-start.4) | collective-permute-done | bytes 917536 | tf_op jit(solution)/shard_map/ppermute | solution.py:608
  63.7 0.9 copy-done.2
  64.6 4.1 %sides.1 = (f32[24,8,512]{2,1,0:T(8,128)}, f32[24,512]{1,0:T(8,128)}) custom-call(s32[1]{0:T(128)} %bitcast.1.side_ref, bf16[28,32,512]{2,1,0:T(8,128)(2,1)} %copy-done.2, f32[22,2,32,512]{3,2,1,0:T(8,128)} %get-tuple-element.47.pre_ref, bf16[128,192]{1,0:T(8,128)(2,1)} %get-tuple-element.48.above_ref, bf16[128,192]{1,0:T(8,128)(2,1)} %get-tuple-element.49.below_ref, ...), custom_call_target="tpu_custom_call" | custom-call | flops 2147483648 | bytes 4194304 | tf_op jit(solution)/shard_map/sides/pallas_call | solution.py:391
  68.7 0.4 collective-permute-start.5
  69.1 8.7 %outer.1.outer_ref = f32[2,3,16,512]{3,2,1,0:T(8,128)} custom-call(s32[1]{0:T(128)} %bitcast.1.side_ref, bf16[32,24,16,512]{3,2,1,0:T(8,128)(2,1)} %vol_ref.1, bf16[28,32,512]{2,1,0:T(8,128)(2,1)} %copy-done.2, bf16[32,16,512]{2,1,0:T(8,128)(2,1)} %copy-done.4, bf16[32,16,512]{2,1,0:T(8,128)(2,1)} %copy-done.3, bf16[2,32,512]{2,1,0:T(8,128)(2,1)} %copy-done.5, ...), custom_call_target="tpu_custom_call" | custom-call | flops 1811939328 | bytes 4194304 | tf_op jit(solution)/shard_map/outer/pallas_call | solution.py:471
  77.8 0.0 collective-permute-done.5.row_ref
  77.8 0.6 copy-done.7
  78.4 2.4 %stats.1 = f32[8,8,8,128]{3,2,1,0:T(8,128)} custom-call(s32[1]{0:T(128)} %bitcast.first_ref, s32[1]{0:T(128)} %bitcast.1.side_ref, f32[24,16,512]{2,1,0:T(8,128)} %get-tuple-element.42.cost_ref, f32[24,8,512]{2,1,0:T(8,128)} %get-tuple-element.51.sides_ref, f32[24,512]{1,0:T(8,128)} %copy-done.7, f32[2,3,16,512]{3,2,1,0:T(8,128)} %outer.1.outer_ref), custom_call_target="tpu_custom_call" | custom-call | tf_op jit(solution)/shard_map/stats/pallas_call | solution.py:538
  80.8 15.4 %all_to_all.10.in_ref = f32[8,8,8,128]{3,2,1,0:T(8,128)} all-to-all(f32[8,8,8,128]{3,2,1,0:T(8,128)} %stats.1), channel_id=1, replica_groups=mesh['tiles'=2,'disp'=8,'rows'=2] {'disp'}, dimensions={0} | all-to-all | bytes 524288 | tf_op jit(solution)/shard_map/all_to_all | solution.py:601
  96.2 1.6 %join.1 = f32[8,8,128]{2,1,0:T(8,128)} custom-call(f32[8,8,8,128]{3,2,1,0:T(8,128)} %all_to_all.10.in_ref), custom_call_target="tpu_custom_call" | custom-call | tf_op jit(solution)/shard_map/join/pallas_call | solution.py:579
  97.9 10.3 %all_to_all.11 = f32[8,8,128]{2,1,0:T(8,128)S(1)} all-to-all(f32[8,8,128]{2,1,0:T(8,128)} %join.1), channel_id=1, replica_groups=mesh['tiles'=2,'disp'=8,'rows'=2] {'disp'}, dimensions={0} | all-to-all | bytes 65536 | tf_op jit(solution)/shard_map/all_to_all | solution.py:602
  108.1 0.6 copy.11
  (15 shorter events, 0.0 us)
Async XLA Ops:
  1.3 8.2 %copy-start = (bf16[32,16,512]{2,1,0:T(8,128)(2,1)}, bf16[32,16,512]{2,1,0:T(8,128)(2,1)S(1)}, u32[]{:S(2)}) copy-start(bf16[32,16,512]{2,1,0:T(8,128)(2,1)S(1)} %get-tuple-element.34.last_ref) | copy-start | bytes 1572868
  1.3 8.2 %copy-start.1 = (bf16[32,16,512]{2,1,0:T(8,128)(2,1)}, bf16[32,16,512]{2,1,0:T(8,128)(2,1)S(1)}, u32[]{:S(2)}) copy-start(bf16[32,16,512]{2,1,0:T(8,128)(2,1)S(1)} %get-tuple-element.33.first_ref) | copy-start | bytes 1572868
  1.3 58.9 %collective-permute-start.1 = (bf16[32,16,512]{2,1,0:T(8,128)(2,1)S(1)}, bf16[32,16,512]{2,1,0:T(8,128)(2,1)S(1)}, u32[]{:S(2)}, u32[]{:S(2)}) collective-permute-start(bf16[32,16,512]{2,1,0:T(8,128)(2,1)S(1)} %get-tuple-element.33.first_ref), channel_id=1, source_target_pairs={{2,0},{4,2},{6,4},{8,6},{10,8},{12,10},{14,12},{3,1},{5,3},{7,5},{... | collective-permute-start | bytes 1572872 | tf_op jit(solution)/shard_map/ppermute | solution.py:618
  2.6 57.6 %collective-permute-start = (bf16[32,16,512]{2,1,0:T(8,128)(2,1)S(1)}, bf16[32,16,512]{2,1,0:T(8,128)(2,1)S(1)}, u32[]{:S(2)}, u32[]{:S(2)}) collective-permute-start(bf16[32,16,512]{2,1,0:T(8,128)(2,1)S(1)} %get-tuple-element.34.last_ref), channel_id=1, source_target_pairs={{0,2},{2,4},{4,6},{6,8},{8,10},{10,12},{12,14},{1,3},{3,5},{5,7},{... | collective-permute-start | bytes 1572872 | tf_op jit(solution)/shard_map/ppermute | solution.py:613
  13.7 46.4 %collective-permute-start.2 = (bf16[2,32,512]{2,1,0:T(8,128)(2,1)}, bf16[2,32,512]{2,1,0:T(8,128)(2,1)S(1)}, u32[]{:S(2)}, u32[]{:S(2)}) collective-permute-start(bf16[2,32,512]{2,1,0:T(8,128)(2,1)} %get-tuple-element.44), channel_id=1, source_target_pairs={{0,3},{1,2},{2,5},{3,4},{4,7},{5,6},{6,9},{7,8},{8,11},{9,10},{10,... | collective-permute-start | bytes 196616 | tf_op jit(solution)/shard_map/ppermute | solution.py:629
  17.4 42.8 %collective-permute-start.3 = (bf16[2,32,512]{2,1,0:T(8,128)(2,1)}, bf16[2,32,512]{2,1,0:T(8,128)(2,1)S(1)}, u32[]{:S(2)}, u32[]{:S(2)}) collective-permute-start(bf16[2,32,512]{2,1,0:T(8,128)(2,1)} %get-tuple-element.45), channel_id=1, source_target_pairs={{2,1},{3,0},{4,3},{5,2},{6,5},{7,4},{8,7},{9,6},{10,9},{11,8},{12,... | collective-permute-start | bytes 196616 | tf_op jit(solution)/shard_map/ppermute | solution.py:629
  60.1 8.9 %copy-start.5 = (bf16[2,32,512]{2,1,0:T(8,128)(2,1)}, bf16[2,32,512]{2,1,0:T(8,128)(2,1)S(1)}, u32[]{:S(2)}) copy-start(bf16[2,32,512]{2,1,0:T(8,128)(2,1)S(1)} %collective-permute-done.2.lo_rows_ref) | copy-start | bytes 196612
  60.2 8.9 %copy-start.6 = (bf16[2,32,512]{2,1,0:T(8,128)(2,1)}, bf16[2,32,512]{2,1,0:T(8,128)(2,1)S(1)}, u32[]{:S(2)}) copy-start(bf16[2,32,512]{2,1,0:T(8,128)(2,1)S(1)} %collective-permute-done.3.hi_rows_ref) | copy-start | bytes 196612
  60.2 8.9 %copy-start.3 = (bf16[32,16,512]{2,1,0:T(8,128)(2,1)}, bf16[32,16,512]{2,1,0:T(8,128)(2,1)S(1)}, u32[]{:S(2)}) copy-start(bf16[32,16,512]{2,1,0:T(8,128)(2,1)S(1)} %collective-permute-done.1.hi_ref) | copy-start | bytes 1572868
  60.2 8.9 %copy-start.4 = (bf16[32,16,512]{2,1,0:T(8,128)(2,1)}, bf16[32,16,512]{2,1,0:T(8,128)(2,1)S(1)}, u32[]{:S(2)}) copy-start(bf16[32,16,512]{2,1,0:T(8,128)(2,1)S(1)} %collective-permute-done.lo_ref) | copy-start | bytes 1572868
  60.2 3.5 %collective-permute-start.4 = (bf16[28,32,512]{2,1,0:T(8,128)(2,1)}, bf16[28,32,512]{2,1,0:T(8,128)(2,1)S(1)}, u32[]{:S(2)}, u32[]{:S(2)}) collective-permute-start(bf16[28,32,512]{2,1,0:T(8,128)(2,1)} %get-tuple-element.46), channel_id=1, source_target_pairs={{0,1},{1,0},{2,3},{3,2},{4,5},{5,4},{6,7},{7,6},{8,9},{9,8},{10,11... | collective-permute-start | bytes 2752520 | tf_op jit(solution)/shard_map/ppermute | solution.py:608
  63.7 0.9 copy-start.2
  68.7 9.1 %collective-permute-start.5 = (f32[24,512]{1,0:T(8,128)}, f32[24,512]{1,0:T(8,128)S(1)}, u32[]{:S(2)}, u32[]{:S(2)}) collective-permute-start(f32[24,512]{1,0:T(8,128)} %get-tuple-element.52), channel_id=1, source_target_pairs={{0,1},{1,0},{2,3},{3,2},{4,5},{5,4},{6,7},{7,6},{8,9},{9,8},{10,11... | collective-permute-start | bytes 147464 | tf_op jit(solution)/shard_map/ppermute | solution.py:608
  77.8 0.6 copy-start.7
